TPU v7x, 256 devices: a whole 4x4x8 slice. The times are simulated.
256 devices in a mesh: row: 16 (over y, x), col: 16 (over z, core).
Axes of the slice: x: 4, y: 4, z: 8, core: 2. Of those that a mesh axis runs over, the one named last changes fastest.
Arguments:
- x_panels: bfloat16 [2, 16, 96, 128, 128], P(None, 'row', 'col'), may hold values from -0.5 to 0.5
- square_panels: bfloat16 [2, 16, 192, 128, 128], P(None, 'row', 'col'), may hold values from -6 to 6
- x_blocks: bfloat16 [16, 512, 128, 128], P('row', 'col'), may hold values from -6 to 6
- pair_lists: int32 [16, 16, 2, 3, 128], P('row', 'col'), may hold values from 0 to 191, as said below
- pair_counts: int32 [16, 16, 2], P('row', 'col'), may hold values from 16 to 128, as said below
Outputs:
- new_blocks: bfloat16 [16, 512, 128, 128], P('row', 'col')
Inputs may be any that keep to these rules, and one draw needn't show every extreme that they name: `pair_lists`: entry 0 of every index list is 0 and the largest index is reached at every device. For e < 16 the first index lies in [e * 6, (e + 1) * 6), for e < 16 the second in [e * 12, (e + 1) * 12). `pair_counts`: in each panel some device has a full list.
All inputs are finite; a program needn't handle non-finite values.
Results may differ from a plain program's by a relative error of at most 0.001.
Values may be sent and summed in bfloat16 or wider, within the bound.
No kernel may reach another device: no remote copies, remote signals or barrier semaphores. Data moves between devices by JAX's collectives and lax.ppermute only.
A program may use at most 128 MiB of HBM per device.

v0:
```python
import functools

import jax
import jax.numpy as jnp
import numpy as np
from jax import lax
from jax.experimental import pallas as pl
from jax.experimental.pallas import tpu as pltpu
from jax.sharding import PartitionSpec as P

SIDE = 4
GROUP = 16
STAGES = 3
PARTS = (11, 11, 10)

UNITS = {
    (0, 0): ((0, 0), (0, 1)),
    (3, 0): ((0, 2), (0, 3)),
    (1, 0): ((0, 4), (0, 5)),
    (2, 0): ((0, 6), (0, 7)),
    (0, 3): ((0, 8), (0, 9)),
    (0, 1): ((0, 10), (0, 11)),
    (3, 3): ((0, 12), (0, 13)),
    (1, 1): ((0, 14), (0, 15)),
    (2, 3): ((1, 0), (1, 1)),
    (2, 1): ((1, 2), (1, 3)),
    (3, 2): ((2, 0), (1, 4)),
    (1, 3): ((2, 1), (1, 5)),
    (1, 2): ((2, 2), (1, 6)),
    (3, 1): ((2, 3), (1, 7)),
    (0, 2): ((1, 8), (1, 10)),
    (2, 2): ((1, 9), (1, 11)),
}


def place_right(shard):
    right = np.zeros((2, 2, SIDE, SIDE), np.int32)
    for core in range(2):
        for column in range(2):
            for dx in range(SIDE):
                for dy in range(SIDE):
                    stage, slot = UNITS[(dx, dy) if core == 0 else (dy, dx)][column]
                    right[core, column, dx, dy] = stage << 12 | slot * shard
    return right.reshape(-1)


def sort_kernel(left_shard, shard, depth, pairs, slots, here, right_at, own, got, entries, groups, lengths):
    x, y, z, core = here[0], here[1], here[2], here[3]
    way = 2 * core - 1
    for stage in range(STAGES):
        lengths[stage] = 0
    for column, lists in enumerate((own, got)):
        base = core * 3 * pairs

        def add(e, carry, column=column, lists=lists, base=base):
            first = lists[base + e]
            second = lists[base + pairs + e]
            slot = lists[base + 2 * pairs + e] + column * slots
            owner = (first * (2**16 // left_shard + 1)) >> 16
            steps = (((owner >> 1) - z) * way) & (depth - 1)
            left = first + (2 * steps + ((owner & 1) ^ core) - owner) * left_shard
            owner = (second * (2**16 // shard + 1)) >> 16
            dx = (owner - x) & (SIDE - 1)
            dy = ((owner >> 2) - y) & (SIDE - 1)
            found = right_at[((core * 2 + column) * SIDE + dx) * SIDE + dy]
            stage = found >> 12
            place = (found & 4095) + second - owner * shard
            at = lengths[stage]
            entries[stage, at] = left | place << 8 | slot << 16
            lengths[stage] = at + 1
            return carry

        lax.fori_loop(0, lists[6 * pairs + core], add, 0)
    for stage in range(STAGES):
        length = lengths[stage]
        unused = (2 * slots if stage < 2 else slots) << 16
        for e in range(GROUP - 1):
            entries[stage, length + e] = unused
        groups[stage] = (length + GROUP - 1) // GROUP


def sort_lists(here, own, got, left_shard, shard, depth, pairs, slots):
    smem = pl.BlockSpec(memory_space=pltpu.SMEM)
    return pl.pallas_call(
        functools.partial(sort_kernel, left_shard, shard, depth, pairs, slots),
        out_shape=(
            jax.ShapeDtypeStruct((STAGES, 2 * pairs + GROUP), jnp.int32),
            jax.ShapeDtypeStruct((STAGES,), jnp.int32),
        ),
        in_specs=[smem] * 4,
        out_specs=(smem, smem),
        scratch_shapes=[pltpu.SMEM((STAGES,), jnp.int32)],
        cost_estimate=pl.CostEstimate(flops=0, bytes_accessed=8 * 2**20, transcendentals=0),
        name="sort_lists",
    )(here, jnp.asarray(place_right(shard)), own, got)


def select_kernel(core, own, got, own_left, got_left, unit, pair, sems):
    c = core[0]
    shard, left_shard = own.shape[1], own_left.shape[1]
    copies = [
        pltpu.make_async_copy(own.at[c], unit.at[pl.ds(0, shard)], sems.at[0]),
        pltpu.make_async_copy(got.at[c], unit.at[pl.ds(shard, shard)], sems.at[1]),
        pltpu.make_async_copy(own_left.at[c], pair.at[pl.ds(0, left_shard)], sems.at[2]),
        pltpu.make_async_copy(got_left.at[c], pair.at[pl.ds(left_shard, left_shard)], sems.at[3]),
    ]
    for copy in copies:
        copy.start()
    for copy in copies:
        copy.wait()


def select_panel(core, own, got, own_left, got_left):
    hbm = pl.BlockSpec(memory_space=pl.ANY)
    vmem = pl.BlockSpec(memory_space=pltpu.VMEM)
    block = own.shape[-2:]
    return pl.pallas_call(
        select_kernel,
        out_shape=(
            jax.ShapeDtypeStruct((2 * own.shape[1], *block), own.dtype),
            jax.ShapeDtypeStruct((2 * own_left.shape[1], *block), own.dtype),
        ),
        in_specs=[pl.BlockSpec(memory_space=pltpu.SMEM)] + [hbm] * 4,
        out_specs=(vmem, vmem),
        scratch_shapes=[pltpu.SemaphoreType.DMA((4,))],
        cost_estimate=pl.CostEstimate(flops=0, bytes_accessed=2**20, transcendentals=0),
        name="select_panel",
    )(core.reshape(1), own, got, own_left, got_left)


def products_kernel(stage, groups, entries, left, right, *refs):
    if stage == 0:
        start, acc = refs
        count = start.shape[0]
        acc[:count] = -3.0 * start[...].astype(jnp.float32)
        acc[count:] = jnp.zeros((acc.shape[0] - count, *acc.shape[1:]), jnp.float32)
    elif stage == 1:
        start, acc = refs[0], refs[-1]
        acc[...] = start[...]
    else:
        start, acc, out = refs[0], refs[-1], refs[-2]
        count = start.shape[0]
        at = 0
        for part in refs[1:-2]:
            size = part.shape[0]
            acc[at : at + size] = start[at : at + size] + part[...]
            at += size
        acc[count] = jnp.zeros_like(acc[count])

    def step(g, carry):
        words = [entries[stage, g * GROUP + e] for e in range(GROUP)]
        made = [
            jnp.dot(left[w & 255], right[(w >> 8) & 255], preferred_element_type=jnp.float32)
            for w in words
        ]
        for w, product in zip(words, made):
            slot = w >> 16
            acc[slot] = acc[slot] + product
        return carry

    lax.fori_loop(0, groups[stage], step, 0)
    if stage == 1:
        own = refs[1]
        at = own.shape[0]
        own[...] = acc[:at]
        for part in refs[2:-1]:
            part[...] = acc[at : at + part.shape[0]]
            at += part.shape[0]
    elif stage == 2:
        out[...] = (-0.5 * acc[:count]).astype(out.dtype)


def add_products(stage, groups, entries, left, right, starts, slots):
    smem = pl.BlockSpec(memory_space=pltpu.SMEM)
    vmem = pl.BlockSpec(memory_space=pltpu.VMEM)
    block = left.shape[-1]

    def result(count, dtype=jnp.float32):
        return jax.ShapeDtypeStruct((count, block, block), dtype)

    if stage == 0:
        outs, scratch = [result(2 * slots + 1)], []
    elif stage == 1:
        outs = [result(slots)] + [result(part) for part in PARTS]
        scratch = [pltpu.VMEM((2 * slots + 1, block, block), jnp.float32)]
    else:
        outs = [result(slots, jnp.bfloat16)]
        scratch = [pltpu.VMEM((slots + 1, block, block), jnp.float32)]
    return pl.pallas_call(
        functools.partial(products_kernel, stage),
        out_shape=outs,
        in_specs=[smem, smem] + [vmem] * (2 + len(starts)),
        out_specs=[vmem] * len(outs),
        scratch_shapes=scratch,
        cost_estimate=pl.CostEstimate(flops=2**20, bytes_accessed=2**20, transcendentals=0),
        compiler_params=pltpu.CompilerParams(vmem_limit_bytes=28 * 2**20),
        name="products",
    )(groups, entries, left, right, *starts)


def move(blocks, step):
    depth = lax.axis_size("col") // 2
    pairs = []
    for y in range(SIDE):
        for x in range(SIDE):
            for z in range(depth):
                for core in range(2):
                    tx, ty, tz, tcore = step(x, y, z, core)
                    to = ((ty % SIDE * SIDE + tx % SIDE) * depth + tz % depth) * 2 + tcore
                    pairs.append((((y * SIDE + x) * depth + z) * 2 + core, to))
    return lax.ppermute(blocks, ("row", "col"), pairs)


def sibling(blocks):
    return move(blocks, lambda x, y, z, c: (x, y, z, 1 - c))


def onward(blocks):
    return move(blocks, lambda x, y, z, c: (x, y, z + 1 - 2 * c, c))


def first(forth, back):
    return [
        move(v, lambda x, y, z, c: (x, y + by, z, c) if c else (x + by, y, z, c))
        for v, by in ((forth, 1), (back, -1))
    ]


def second(forth, back):
    return [
        move(v, lambda x, y, z, c: (x + by, y, z, c) if c else (x, y + by, z, c))
        for v, by in ((forth, 1), (back, -1))
    ]


def join(*pieces):
    return jnp.concatenate(pieces)


def on_device(x_panels, square_panels, x_blocks, pair_lists, pair_counts):
    block = x_blocks.shape[-1]
    left_shard, shard = x_panels.shape[2], square_panels.shape[2]
    pairs, slots = pair_lists.shape[-1], x_blocks.shape[1]
    depth = lax.axis_size("col") // 2
    row, col = lax.axis_index("row"), lax.axis_index("col")
    core = (col % 2).astype(jnp.int32)
    here = jnp.stack([row % SIDE, row // SIDE, col // 2, core]).astype(jnp.int32)
    order = lax.optimization_barrier
    scope = jax.named_scope

    own, own_left = square_panels[:, 0], x_panels[:, 0]
    with scope("w0"):
        got = sibling(own)
    with scope("w1"):
        got_left = sibling(own_left)
    lists = join(pair_lists.reshape(-1), pair_counts.reshape(-1))
    with scope("w2"):
        got_lists = sibling(lists)
    unit, pair = select_panel(core, own, got, own_left, got_left)

    with scope("s1"):
        r1, l1 = first(unit, unit)
    with scope("t"):
        t = second(unit, unit)
    entries, groups = sort_lists(here, lists, got_lists, left_shard, shard, depth, pairs, slots)
    passed = [pair]
    for step in range(1, depth):
        with scope(f"z{step}"):
            passed.append(onward(passed[-1]))
    left = join(*passed)
    with scope("s2"):
        s2 = first(r1[:shard], l1[shard:])
    t, ar, al = order((t, r1, l1))
    with scope("a1"):
        a1 = second(ar, al)
    x2 = join(*s2)
    with scope("b"):
        b = second(x2, x2)
    with scope("ga"):
        ga = second(join(a1[0][shard:], l1[shard:]), join(a1[1][shard:], r1[shard:]))
    with scope("gh"):
        gh = second(join(t[0][:shard], b[0][:shard]), join(t[1][shard:], b[1][shard:]))
    near = join(unit, r1, l1, *s2, *t, *a1)
    (total,) = add_products(0, groups, entries, left, near, [x_blocks[0]], slots)
    ga, ar, al, a1 = order((ga, r1, l1, a1))
    with scope("a2"):
        a2 = second(join(a1[0][:shard], al[:shard]), join(a1[1][:shard], ar[:shard]))
    far = join(*b, *ga, *gh)
    total, *theirs = add_products(1, groups, entries, left, far, [total], slots)
    with scope("w3"):
        mine = [sibling(part) for part in theirs]
    return add_products(2, groups, entries, left, join(*a2), [total, *mine], slots)[0][None]


def solution(mesh):
    in_specs = (
        P(None, "row", "col", None, None),
        P(None, "row", "col", None, None),
        P("row", "col", None, None),
        P("row", "col", None, None, None),
        P("row", "col", None),
    )
    out_specs = P("row", "col", None, None)
    return jax.shard_map(
        on_device, mesh=mesh, in_specs=in_specs, out_specs=out_specs, check_vma=False
    )
```

profile of v0, /device:TPU:1, one launch (start us, length us, event | category | flops | bytes accessed | tf_op | source)
XLA Modules:
  0.0 95.6 jit_solution(12319192999207081420)
XLA Ops:
  0.0 3.2 %collective-permute-start.1 = (bf16[2,12,128,128]{3,2,1,0:T(8,128)(2,1)}, bf16[2,12,128,128]{3,2,1,0:T(8,128)(2,1)S(1)}, u32[]{:S(2)}, u32[]{:S(2)}) collective-permute-start(bf16[2,12,128,128]{3,2,1,0:T(8,128)(2,1)} %bitcast.10), channel_id=1, source_target_pairs={{0,1},{1,0},{2,3},{3,2},{4,5},{5,4},{6,7},{7,6},{8,9},{9,8},{10,11... | collective-permute-start | bytes 2359304 | tf_op jit(solution)/shard_map/w0/ppermute | solution.py:211
  3.2 2.7 %collective-permute-done.2.got_left = bf16[2,6,128,128]{3,2,1,0:T(8,128)(2,1)S(1)} collective-permute-done((bf16[2,6,128,128]{3,2,1,0:T(8,128)(2,1)}, bf16[2,6,128,128]{3,2,1,0:T(8,128)(2,1)S(1)}, u32[]{:S(2)}, u32[]{:S(2)}) %collective-permute-start.2) | collective-permute-done | bytes 393248 | tf_op jit(solution)/shard_map/w1/ppermute | solution.py:211
  5.9 0.8 copy-done.6
  6.7 0.2 copy-done.5
  6.9 2.3 %select_panel.1 = (bf16[24,128,128]{2,1,0:T(8,128)(2,1)}, bf16[12,128,128]{2,1,0:T(8,128)(2,1)}) custom-call(s32[1]{0:T(128)} %bitcast.3.core, bf16[2,12,128,128]{3,2,1,0:T(8,128)(2,1)} %bitcast.11, bf16[2,12,128,128]{3,2,1,0:T(8,128)(2,1)} %copy-done.5, bf16[2,6,128,128]{3,2,1,0:T(8,128)(2,1)} %bitcast.13, bf16[2,6,128,128]{3,2,1,0:T(8,128)(2,1)} %copy-done.6), custom_call_target="tpu_custom_call" | custom-call | bytes 1048576 | tf_op jit(solution)/shard_map/select_panel/pallas_call | solution.py:117
  9.2 0.1 collective-permute-start.12
  9.3 0.7 copy.7
  10.0 2.7 %collective-permute-start.13 = (bf16[24,128,128]{2,1,0:T(8,128)(2,1)}, bf16[24,128,128]{2,1,0:T(8,128)(2,1)S(1)}, u32[]{:S(2)}, u32[]{:S(2)}) collective-permute-start(bf16[24,128,128]{2,1,0:T(8,128)(2,1)} %get-tuple-element.26), channel_id=1, source_target_pairs={{0,48},{1,193},{2,50},{3,195},{4,52},{5,197},{6,54},{7,199},{8,56}... | collective-permute-start | bytes 2359304 | tf_op jit(solution)/shard_map/s1/ppermute | solution.py:211
  12.7 2.7 %collective-permute-start.11 = (bf16[24,128,128]{2,1,0:T(8,128)(2,1)}, bf16[24,128,128]{2,1,0:T(8,128)(2,1)S(1)}, u32[]{:S(2)}, u32[]{:S(2)}) collective-permute-start(bf16[24,128,128]{2,1,0:T(8,128)(2,1)} %get-tuple-element.26), channel_id=1, source_target_pairs={{0,192},{1,49},{2,194},{3,51},{4,196},{5,53},{6,198},{7,55},{8,200... | collective-permute-start | bytes 2359304 | tf_op jit(solution)/shard_map/t/ppermute | solution.py:211
  15.4 0.7 pad_add_fusion.own
  16.0 1.5 %collective-permute-start = (s32[770]{0:T(1024)S(1)}, s32[770]{0:T(1024)S(1)}, u32[]{:S(2)}, u32[]{:S(2)}) collective-permute-start(s32[770]{0:T(1024)S(1)} %pad_add_fusion.own), channel_id=1, source_target_pairs={{0,1},{1,0},{2,3},{3,2},{4,5},{5,4},{6,7},{7,6},{8,9},{9,8},{10,11... | collective-permute-start | bytes 9248 | tf_op jit(solution)/shard_map/w2/ppermute | solution.py:211
  17.5 0.8 collective-permute-done.got
  18.4 3.8 %collective-permute-start.3 = (bf16[12,128,128]{2,1,0:T(8,128)(2,1)}, bf16[12,128,128]{2,1,0:T(8,128)(2,1)S(1)}, u32[]{:S(2)}, u32[]{:S(2)}) collective-permute-start(bf16[12,128,128]{2,1,0:T(8,128)(2,1)} %get-tuple-element.25), channel_id=1, source_target_pairs={{0,2},{1,15},{2,4},{3,1},{4,6},{5,3},{6,8},{7,5},{8,10},{9,7},{10,... | collective-permute-start | bytes 1179656 | tf_op jit(solution)/shard_map/z1/ppermute | solution.py:211
  22.2 0.6 pad_add_fusion.1.here
  22.8 3.0 %sort_lists.1 = (s32[3,272]{1,0:T(4,128)}, s32[3]{0:T(128)}) custom-call(s32[4]{0:T(128)} %pad_add_fusion.1.here, s32[64]{0:T(128)} %constant.51.clone.right_at, s32[770]{0:T(1024)} %copy-done.7, s32[770]{0:T(1024)} %copy-done.8), custom_call_target="tpu_custom_call" | custom-call | bytes 8388608 | tf_op jit(solution)/shard_map/sort_lists/pallas_call | solution.py:84
  25.8 1.0 %constant_dynamic-update-slice_fusion.7 = bf16[96,128,128]{2,1,0:T(8,128)(2,1)S(1)} fusion(bf16[12,128,128]{2,1,0:T(8,128)(2,1)} %get-tuple-element.25), kind=kLoop, calls=%fused_computation.14 | loop fusion | bytes 786432
  26.8 1.2 %constant_dynamic-update-slice_fusion.24 = bf16[192,128,128]{2,1,0:T(8,128)(2,1)S(1)} fusion(bf16[24,128,128]{2,1,0:T(8,128)(2,1)} %get-tuple-element.26), kind=kLoop, calls=%fused_computation.31 | loop fusion | bytes 1572864
  28.0 3.1 %collective-permute-start.4 = (bf16[12,128,128]{2,1,0:T(8,128)(2,1)S(1)}, bf16[12,128,128]{2,1,0:T(8,128)(2,1)S(1)}, u32[]{:S(2)}, u32[]{:S(2)}) collective-permute-start(bf16[12,128,128]{2,1,0:T(8,128)(2,1)S(1)} %collective-permute-done.3), channel_id=1, source_target_pairs={{0,2},{1,15},{2,4},{3,1},{4,6},{5,3},{6,8},{7,5},{8,10},{9,7},{10,... | collective-permute-start | bytes 1179656 | tf_op jit(solution)/shard_map/z2/ppermute | solution.py:211
  31.2 2.0 %collective-permute-start.20 = (bf16[12,128,128]{2,1,0:T(8,128)(2,1)S(1)}, bf16[12,128,128]{2,1,0:T(8,128)(2,1)S(1)}, u32[]{:S(2)}, u32[]{:S(2)}) collective-permute-start(bf16[12,128,128]{2,1,0:T(8,128)(2,1)S(1)} %get-tuple-element.41), channel_id=1, source_target_pairs={{0,16},{1,65},{2,18},{3,67},{4,20},{5,69},{6,22},{7,71},{8,24},{9,... | collective-permute-start | bytes 1179656 | tf_op jit(solution)/shard_map/s2/ppermute | solution.py:211
  33.3 0.8 collective-permute-start.21
  34.2 0.9 collective-permute-start.14
  35.1 2.5 %collective-permute-start.16 = (bf16[24,128,128]{2,1,0:T(8,128)(2,1)S(1)}, bf16[24,128,128]{2,1,0:T(8,128)(2,1)S(1)}, u32[]{:S(2)}, u32[]{:S(2)}) collective-permute-start(bf16[24,128,128]{2,1,0:T(8,128)(2,1)S(1)} %collective-permute-done.13), channel_id=1, source_target_pairs={{0,192},{1,49},{2,194},{3,51},{4,196},{5,53},{6,198},{7,55},{8,200... | collective-permute-start | bytes 2359304 | tf_op jit(solution)/shard_map/a1/ppermute | solution.py:211
  37.6 0.1 constant_dynamic-update-slice_fusion.23
  37.7 1.6 %collective-permute-start.5 = (bf16[12,128,128]{2,1,0:T(8,128)(2,1)S(1)}, bf16[12,128,128]{2,1,0:T(8,128)(2,1)S(1)}, u32[]{:S(2)}, u32[]{:S(2)}) collective-permute-start(bf16[12,128,128]{2,1,0:T(8,128)(2,1)S(1)} %collective-permute-done.4), channel_id=1, source_target_pairs={{0,2},{1,15},{2,4},{3,1},{4,6},{5,3},{6,8},{7,5},{8,10},{9,7},{10,... | collective-permute-start | bytes 1179656 | tf_op jit(solution)/shard_map/z3/ppermute | solution.py:211
  39.3 0.1 constant_dynamic-update-slice_fusion.22
  39.5 0.9 collective-permute-done.20
  40.4 0.1 constant_dynamic-update-slice_fusion.21
  40.6 0.2 constant_dynamic-update-slice_fusion.20
  40.8 0.4 collective-permute-start.22
  41.2 6.7 %collective-permute-start.23 = (bf16[24,128,128]{2,1,0:T(8,128)(2,1)S(1)}, bf16[24,128,128]{2,1,0:T(8,128)(2,1)S(1)}, u32[]{:S(2)}, u32[]{:S(2)}) collective-permute-start(bf16[24,128,128]{2,1,0:T(8,128)(2,1)S(1)} %get-tuple-element.44), channel_id=1, source_target_pairs={{0,192},{1,49},{2,194},{3,51},{4,196},{5,53},{6,198},{7,55},{8,200... | collective-permute-start | bytes 2359304 | tf_op jit(solution)/shard_map/b/ppermute | solution.py:211
  48.0 0.1 constant_dynamic-update-slice_fusion.19
  48.1 0.1 constant_dynamic-update-slice_fusion.18
  48.3 0.9 collective-permute-done.16
  49.3 0.1 pad_maximum_fusion.2
  49.4 1.8 %collective-permute-start.17 = (bf16[24,128,128]{2,1,0:T(8,128)(2,1)S(1)}, bf16[24,128,128]{2,1,0:T(8,128)(2,1)S(1)}, u32[]{:S(2)}, u32[]{:S(2)}) collective-permute-start(bf16[24,128,128]{2,1,0:T(8,128)(2,1)S(1)} %pad_maximum_fusion.2), channel_id=1, source_target_pairs={{0,192},{1,49},{2,194},{3,51},{4,196},{5,53},{6,198},{7,55},{8,200... | collective-permute-start | bytes 2359304 | tf_op jit(solution)/shard_map/ga/ppermute | solution.py:211
  51.3 0.1 collective-permute-start.15
  51.4 3.5 %collective-permute-done.6 = bf16[12,128,128]{2,1,0:T(8,128)(2,1)S(1)} collective-permute-done((bf16[12,128,128]{2,1,0:T(8,128)(2,1)S(1)}, bf16[12,128,128]{2,1,0:T(8,128)(2,1)S(1)}, u32[]{:S(2)}, u32[]{:S(2)}) %collective-permute-start.6) | collective-permute-done | bytes 393248 | tf_op jit(solution)/shard_map/z4/ppermute | solution.py:211
  54.9 1.2 %collective-permute-start.7 = (bf16[12,128,128]{2,1,0:T(8,128)(2,1)S(1)}, bf16[12,128,128]{2,1,0:T(8,128)(2,1)S(1)}, u32[]{:S(2)}, u32[]{:S(2)}) collective-permute-start(bf16[12,128,128]{2,1,0:T(8,128)(2,1)S(1)} %collective-permute-done.6), channel_id=1, source_target_pairs={{0,2},{1,15},{2,4},{3,1},{4,6},{5,3},{6,8},{7,5},{8,10},{9,7},{10,... | collective-permute-start | bytes 1179656 | tf_op jit(solution)/shard_map/z5/ppermute | solution.py:211
  56.1 0.1 constant_dynamic-update-slice_fusion.17
  56.3 0.1 constant_dynamic-update-slice_fusion.16.right
  56.4 1.0 %collective-permute-done.22 = bf16[24,128,128]{2,1,0:T(8,128)(2,1)S(1)} collective-permute-done((bf16[24,128,128]{2,1,0:T(8,128)(2,1)S(1)}, bf16[24,128,128]{2,1,0:T(8,128)(2,1)S(1)}, u32[]{:S(2)}, u32[]{:S(2)}) %collective-permute-start.22) | collective-permute-done | bytes 786464 | tf_op jit(solution)/shard_map/b/ppermute | solution.py:211
  57.5 0.1 collective-permute-start.24
  57.8 2.7 %collective-permute-start.25 = (bf16[24,128,128]{2,1,0:T(8,128)(2,1)S(1)}, bf16[24,128,128]{2,1,0:T(8,128)(2,1)S(1)}, u32[]{:S(2)}, u32[]{:S(2)}) collective-permute-start(bf16[24,128,128]{2,1,0:T(8,128)(2,1)S(1)} %pad_maximum_fusion.6), channel_id=1, source_target_pairs={{0,192},{1,49},{2,194},{3,51},{4,196},{5,53},{6,198},{7,55},{8,200... | collective-permute-start | bytes 2359304 | tf_op jit(solution)/shard_map/gh/ppermute | solution.py:211
  60.5 1.3 %collective-permute-done.7 = bf16[12,128,128]{2,1,0:T(8,128)(2,1)S(1)} collective-permute-done((bf16[12,128,128]{2,1,0:T(8,128)(2,1)S(1)}, bf16[12,128,128]{2,1,0:T(8,128)(2,1)S(1)}, u32[]{:S(2)}, u32[]{:S(2)}) %collective-permute-start.7) | collective-permute-done | bytes 393248 | tf_op jit(solution)/shard_map/z5/ppermute | solution.py:211
  61.8 2.4 %collective-permute-start.8 = (bf16[12,128,128]{2,1,0:T(8,128)(2,1)S(1)}, bf16[12,128,128]{2,1,0:T(8,128)(2,1)S(1)}, u32[]{:S(2)}, u32[]{:S(2)}) collective-permute-start(bf16[12,128,128]{2,1,0:T(8,128)(2,1)S(1)} %collective-permute-done.7), channel_id=1, source_target_pairs={{0,2},{1,15},{2,4},{3,1},{4,6},{5,3},{6,8},{7,5},{8,10},{9,7},{10,... | collective-permute-start | bytes 1179656 | tf_op jit(solution)/shard_map/z6/ppermute | solution.py:211
  64.3 0.1 constant_dynamic-update-slice_fusion.14
  64.5 1.6 %collective-permute-done.17 = bf16[24,128,128]{2,1,0:T(8,128)(2,1)S(1)} collective-permute-done((bf16[24,128,128]{2,1,0:T(8,128)(2,1)S(1)}, bf16[24,128,128]{2,1,0:T(8,128)(2,1)S(1)}, u32[]{:S(2)}, u32[]{:S(2)}) %collective-permute-start.17) | collective-permute-done | bytes 786464 | tf_op jit(solution)/shard_map/ga/ppermute | solution.py:211
  66.3 1.3 %collective-permute-start.18 = (bf16[24,128,128]{2,1,0:T(8,128)(2,1)S(1)}, bf16[24,128,128]{2,1,0:T(8,128)(2,1)S(1)}, u32[]{:S(2)}, u32[]{:S(2)}) collective-permute-start(bf16[24,128,128]{2,1,0:T(8,128)(2,1)S(1)} %pad_maximum_fusion.3), channel_id=1, source_target_pairs={{0,64},{1,17},{2,66},{3,19},{4,68},{5,21},{6,70},{7,23},{8,72},{9,... | collective-permute-start | bytes 2359304 | tf_op jit(solution)/shard_map/a2/ppermute | solution.py:211
  67.7 1.3 %collective-permute-done.8 = bf16[12,128,128]{2,1,0:T(8,128)(2,1)S(1)} collective-permute-done((bf16[12,128,128]{2,1,0:T(8,128)(2,1)S(1)}, bf16[12,128,128]{2,1,0:T(8,128)(2,1)S(1)}, u32[]{:S(2)}, u32[]{:S(2)}) %collective-permute-start.8) | collective-permute-done | bytes 393248 | tf_op jit(solution)/shard_map/z6/ppermute | solution.py:211
  69.0 3.4 %collective-permute-start.9 = (bf16[12,128,128]{2,1,0:T(8,128)(2,1)S(1)}, bf16[12,128,128]{2,1,0:T(8,128)(2,1)S(1)}, u32[]{:S(2)}, u32[]{:S(2)}) collective-permute-start(bf16[12,128,128]{2,1,0:T(8,128)(2,1)S(1)} %collective-permute-done.8), channel_id=1, source_target_pairs={{0,2},{1,15},{2,4},{3,1},{4,6},{5,3},{6,8},{7,5},{8,10},{9,7},{10,... | collective-permute-start | bytes 1179656 | tf_op jit(solution)/shard_map/z7/ppermute | solution.py:211
  72.5 2.7 %collective-permute-start.19 = (bf16[24,128,128]{2,1,0:T(8,128)(2,1)S(1)}, bf16[24,128,128]{2,1,0:T(8,128)(2,1)S(1)}, u32[]{:S(2)}, u32[]{:S(2)}) collective-permute-start(bf16[24,128,128]{2,1,0:T(8,128)(2,1)S(1)} %pad_maximum_fusion.4), channel_id=1, source_target_pairs={{0,192},{1,49},{2,194},{3,51},{4,196},{5,53},{6,198},{7,55},{8,200... | collective-permute-start | bytes 2359304 | tf_op jit(solution)/shard_map/a2/ppermute | solution.py:211
  75.3 0.1 constant_dynamic-update-slice_fusion.13
  75.4 0.1 constant_dynamic-update-slice_fusion.12
  75.5 1.6 %collective-permute-done.9 = bf16[12,128,128]{2,1,0:T(8,128)(2,1)S(1)} collective-permute-done((bf16[12,128,128]{2,1,0:T(8,128)(2,1)S(1)}, bf16[12,128,128]{2,1,0:T(8,128)(2,1)S(1)}, u32[]{:S(2)}, u32[]{:S(2)}) %collective-permute-start.9) | collective-permute-done | bytes 393248 | tf_op jit(solution)/shard_map/z7/ppermute | solution.py:211
  77.2 1.5 %products.3.refs_0_ = f32[65,128,128]{2,1,0:T(8,128)S(1)} custom-call(s32[3]{0:T(128)S(1)} %copy-done.2, s32[3,272]{1,0:T(4,128)S(1)} %copy-done.1, bf16[96,128,128]{2,1,0:T(8,128)(2,1)S(1)} %constant_dynamic-update-slice_fusion.left, bf16[192,128,128]{2,1,0:T(8,128)(2,1)S(1)} %constant_dynamic-update-slice_fusion.16.right, bf16[32,128,128]{2,1,0:T(8,128)(2,1)S(1)} %bitcast.9), custom_call_target="tpu_custom_call" | custom-call | flops 1048576 | bytes 1048576 | tf_op jit(solution)/shard_map/products/pallas_call | solution.py:189
  78.7 0.1 constant_dynamic-update-slice_fusion.11
  78.8 0.1 constant_dynamic-update-slice_fusion.10.right
  79.0 1.5 %products.4 = (f32[32,128,128]{2,1,0:T(8,128)S(1)}, f32[11,128,128]{2,1,0:T(8,128)S(1)}, f32[11,128,128]{2,1,0:T(8,128)S(1)}, f32[10,128,128]{2,1,0:T(8,128)S(1)}) custom-call(s32[3]{0:T(128)S(1)} %copy-done.2, s32[3,272]{1,0:T(4,128)S(1)} %copy-done.1, bf16[96,128,128]{2,1,0:T(8,128)(2,1)S(1)} %constant_dynamic-update-slice_fusion.left, ...), custom_call_target="tpu_custom_call" | custom-call | flops 1048576 | bytes 1048576 | tf_op jit(solution)/shard_map/products/pallas_call | solution.py:189
  80.5 9.1 %collective-permute-start.26 = (f32[11,128,128]{2,1,0:T(8,128)S(1)}, f32[11,128,128]{2,1,0:T(8,128)S(1)}, u32[]{:S(2)}, u32[]{:S(2)}) collective-permute-start(f32[11,128,128]{2,1,0:T(8,128)S(1)} %get-tuple-element.38), channel_id=1, source_target_pairs={{0,1},{1,0},{2,3},{3,2},{4,5},{5,4},{6,7},{7,6},{8,9},{9,8},{10,11... | collective-permute-start | bytes 2162696 | tf_op jit(solution)/shard_map/w3/ppermute | solution.py:211
  89.6 0.1 collective-permute-start.27
  89.7 0.4 collective-permute-start.28
  90.1 0.1 pad_maximum_fusion.right
  90.3 3.1 %collective-permute-done.28.refs_3_ = f32[10,128,128]{2,1,0:T(8,128)S(1)} collective-permute-done((f32[10,128,128]{2,1,0:T(8,128)S(1)}, f32[10,128,128]{2,1,0:T(8,128)S(1)}, u32[]{:S(2)}, u32[]{:S(2)}) %collective-permute-start.28) | collective-permute-done | bytes 655392 | tf_op jit(solution)/shard_map/w3/ppermute | solution.py:211
  93.4 2.3 %products.5 = bf16[32,128,128]{2,1,0:T(8,128)(2,1)} custom-call(s32[3]{0:T(128)S(1)} %copy-done.2, s32[3,272]{1,0:T(4,128)S(1)} %copy-done.1, bf16[96,128,128]{2,1,0:T(8,128)(2,1)S(1)} %constant_dynamic-update-slice_fusion.left, bf16[48,128,128]{2,1,0:T(8,128)(2,1)S(1)} %pad_maximum_fusion.right, f32[32,128,128]{2,1,0:T(8,128)S(1)} %get-tuple-element.37.refs_0_, ...), custom_call_target="tpu_custom_call" | custom-call | flops 1048576 | bytes 1048576 | tf_op jit(solution)/shard_map/products/pallas_call | solution.py:189
  (65 shorter events, 1.3 us)
Async XLA Ops:
  0.0 5.9 %collective-permute-start.1 = (bf16[2,12,128,128]{3,2,1,0:T(8,128)(2,1)}, bf16[2,12,128,128]{3,2,1,0:T(8,128)(2,1)S(1)}, u32[]{:S(2)}, u32[]{:S(2)}) collective-permute-start(bf16[2,12,128,128]{3,2,1,0:T(8,128)(2,1)} %bitcast.10), channel_id=1, source_target_pairs={{0,1},{1,0},{2,3},{3,2},{4,5},{5,4},{6,7},{7,6},{8,9},{9,8},{10,11... | collective-permute-start | bytes 2359304 | tf_op jit(solution)/shard_map/w0/ppermute | solution.py:211
  3.2 2.7 %collective-permute-start.2 = (bf16[2,6,128,128]{3,2,1,0:T(8,128)(2,1)}, bf16[2,6,128,128]{3,2,1,0:T(8,128)(2,1)S(1)}, u32[]{:S(2)}, u32[]{:S(2)}) collective-permute-start(bf16[2,6,128,128]{3,2,1,0:T(8,128)(2,1)} %bitcast.12), channel_id=1, source_target_pairs={{0,1},{1,0},{2,3},{3,2},{4,5},{5,4},{6,7},{7,6},{8,9},{9,8},{10,11... | collective-permute-start | bytes 1179656 | tf_op jit(solution)/shard_map/w1/ppermute | solution.py:211
  5.9 0.8 copy-start.6
  5.9 1.0 %copy-start.5 = (bf16[2,12,128,128]{3,2,1,0:T(8,128)(2,1)}, bf16[2,12,128,128]{3,2,1,0:T(8,128)(2,1)S(1)}, u32[]{:S(2)}) copy-start(bf16[2,12,128,128]{3,2,1,0:T(8,128)(2,1)S(1)} %collective-permute-done.1.got) | copy-start | bytes 2359300
  9.2 21.9 %collective-permute-start.12 = (bf16[24,128,128]{2,1,0:T(8,128)(2,1)}, bf16[24,128,128]{2,1,0:T(8,128)(2,1)S(1)}, u32[]{:S(2)}, u32[]{:S(2)}) collective-permute-start(bf16[24,128,128]{2,1,0:T(8,128)(2,1)} %get-tuple-element.26), channel_id=1, source_target_pairs={{0,16},{1,65},{2,18},{3,67},{4,20},{5,69},{6,22},{7,71},{8,24},{9,... | collective-permute-start | bytes 2359304 | tf_op jit(solution)/shard_map/s1/ppermute | solution.py:211
  10.0 23.2 %collective-permute-start.13 = (bf16[24,128,128]{2,1,0:T(8,128)(2,1)}, bf16[24,128,128]{2,1,0:T(8,128)(2,1)S(1)}, u32[]{:S(2)}, u32[]{:S(2)}) collective-permute-start(bf16[24,128,128]{2,1,0:T(8,128)(2,1)} %get-tuple-element.26), channel_id=1, source_target_pairs={{0,48},{1,193},{2,50},{3,195},{4,52},{5,197},{6,54},{7,199},{8,56}... | collective-permute-start | bytes 2359304 | tf_op jit(solution)/shard_map/s1/ppermute | solution.py:211
  12.7 21.5 %collective-permute-start.10 = (bf16[24,128,128]{2,1,0:T(8,128)(2,1)}, bf16[24,128,128]{2,1,0:T(8,128)(2,1)S(1)}, u32[]{:S(2)}, u32[]{:S(2)}) collective-permute-start(bf16[24,128,128]{2,1,0:T(8,128)(2,1)} %get-tuple-element.26), channel_id=1, source_target_pairs={{0,64},{1,17},{2,66},{3,19},{4,68},{5,21},{6,70},{7,23},{8,72},{9,... | collective-permute-start | bytes 2359304 | tf_op jit(solution)/shard_map/t/ppermute | solution.py:211
  12.7 21.5 %collective-permute-start.11 = (bf16[24,128,128]{2,1,0:T(8,128)(2,1)}, bf16[24,128,128]{2,1,0:T(8,128)(2,1)S(1)}, u32[]{:S(2)}, u32[]{:S(2)}) collective-permute-start(bf16[24,128,128]{2,1,0:T(8,128)(2,1)} %get-tuple-element.26), channel_id=1, source_target_pairs={{0,192},{1,49},{2,194},{3,51},{4,196},{5,53},{6,198},{7,55},{8,200... | collective-permute-start | bytes 2359304 | tf_op jit(solution)/shard_map/t/ppermute | solution.py:211
  16.0 6.8 %copy-start.7 = (s32[770]{0:T(1024)}, s32[770]{0:T(1024)S(1)}, u32[]{:S(2)}) copy-start(s32[770]{0:T(1024)S(1)} %pad_add_fusion.own) | copy-start | bytes 9244
  16.0 2.3 %collective-permute-start = (s32[770]{0:T(1024)S(1)}, s32[770]{0:T(1024)S(1)}, u32[]{:S(2)}, u32[]{:S(2)}) collective-permute-start(s32[770]{0:T(1024)S(1)} %pad_add_fusion.own), channel_id=1, source_target_pairs={{0,1},{1,0},{2,3},{3,2},{4,5},{5,4},{6,7},{7,6},{8,9},{9,8},{10,11... | collective-permute-start | bytes 9248 | tf_op jit(solution)/shard_map/w2/ppermute | solution.py:211
  18.4 4.5 %copy-start.8 = (s32[770]{0:T(1024)}, s32[770]{0:T(1024)S(1)}, u32[]{:S(2)}) copy-start(s32[770]{0:T(1024)S(1)} %collective-permute-done.got) | copy-start | bytes 9244
  18.4 9.6 %collective-permute-start.3 = (bf16[12,128,128]{2,1,0:T(8,128)(2,1)}, bf16[12,128,128]{2,1,0:T(8,128)(2,1)S(1)}, u32[]{:S(2)}, u32[]{:S(2)}) collective-permute-start(bf16[12,128,128]{2,1,0:T(8,128)(2,1)} %get-tuple-element.25), channel_id=1, source_target_pairs={{0,2},{1,15},{2,4},{3,1},{4,6},{5,3},{6,8},{7,5},{8,10},{9,7},{10,... | collective-permute-start | bytes 1179656 | tf_op jit(solution)/shard_map/z1/ppermute | solution.py:211
  28.0 9.7 %collective-permute-start.4 = (bf16[12,128,128]{2,1,0:T(8,128)(2,1)S(1)}, bf16[12,128,128]{2,1,0:T(8,128)(2,1)S(1)}, u32[]{:S(2)}, u32[]{:S(2)}) collective-permute-start(bf16[12,128,128]{2,1,0:T(8,128)(2,1)S(1)} %collective-permute-done.3), channel_id=1, source_target_pairs={{0,2},{1,15},{2,4},{3,1},{4,6},{5,3},{6,8},{7,5},{8,10},{9,7},{10,... | collective-permute-start | bytes 1179656 | tf_op jit(solution)/shard_map/z2/ppermute | solution.py:211
  31.2 9.2 %collective-permute-start.20 = (bf16[12,128,128]{2,1,0:T(8,128)(2,1)S(1)}, bf16[12,128,128]{2,1,0:T(8,128)(2,1)S(1)}, u32[]{:S(2)}, u32[]{:S(2)}) collective-permute-start(bf16[12,128,128]{2,1,0:T(8,128)(2,1)S(1)} %get-tuple-element.41), channel_id=1, source_target_pairs={{0,16},{1,65},{2,18},{3,67},{4,20},{5,69},{6,22},{7,71},{8,24},{9,... | collective-permute-start | bytes 1179656 | tf_op jit(solution)/shard_map/s2/ppermute | solution.py:211
  33.3 7.2 %collective-permute-start.21 = (bf16[12,128,128]{2,1,0:T(8,128)(2,1)S(1)}, bf16[12,128,128]{2,1,0:T(8,128)(2,1)S(1)}, u32[]{:S(2)}, u32[]{:S(2)}) collective-permute-start(bf16[12,128,128]{2,1,0:T(8,128)(2,1)S(1)} %slice.54), channel_id=1, source_target_pairs={{0,48},{1,193},{2,50},{3,195},{4,52},{5,197},{6,54},{7,199},{8,56}... | collective-permute-start | bytes 1179656 | tf_op jit(solution)/shard_map/s2/ppermute | solution.py:211
  34.2 13.9 %copy-start.3 = (bf16[24,128,128]{2,1,0:T(8,128)(2,1)}, bf16[24,128,128]{2,1,0:T(8,128)(2,1)S(1)}, u32[]{:S(2)}) copy-start(bf16[24,128,128]{2,1,0:T(8,128)(2,1)S(1)} %collective-permute-done.10) | copy-start | bytes 2359300
  34.2 13.9 %copy-start.4 = (bf16[24,128,128]{2,1,0:T(8,128)(2,1)}, bf16[24,128,128]{2,1,0:T(8,128)(2,1)S(1)}, u32[]{:S(2)}) copy-start(bf16[24,128,128]{2,1,0:T(8,128)(2,1)S(1)} %collective-permute-done.11) | copy-start | bytes 2359300
  34.2 17.0 %collective-permute-start.14 = (bf16[24,128,128]{2,1,0:T(8,128)(2,1)S(1)}, bf16[24,128,128]{2,1,0:T(8,128)(2,1)S(1)}, u32[]{:S(2)}, u32[]{:S(2)}) collective-permute-start(bf16[24,128,128]{2,1,0:T(8,128)(2,1)S(1)} %collective-permute-done.12), channel_id=1, source_target_pairs={{0,64},{1,17},{2,66},{3,19},{4,68},{5,21},{6,70},{7,23},{8,72},{9,... | collective-permute-start | bytes 2359304 | tf_op jit(solution)/shard_map/a1/ppermute | solution.py:211
  35.1 14.1 %collective-permute-start.16 = (bf16[24,128,128]{2,1,0:T(8,128)(2,1)S(1)}, bf16[24,128,128]{2,1,0:T(8,128)(2,1)S(1)}, u32[]{:S(2)}, u32[]{:S(2)}) collective-permute-start(bf16[24,128,128]{2,1,0:T(8,128)(2,1)S(1)} %collective-permute-done.13), channel_id=1, source_target_pairs={{0,192},{1,49},{2,194},{3,51},{4,196},{5,53},{6,198},{7,55},{8,200... | collective-permute-start | bytes 2359304 | tf_op jit(solution)/shard_map/a1/ppermute | solution.py:211
  37.7 10.3 %collective-permute-start.5 = (bf16[12,128,128]{2,1,0:T(8,128)(2,1)S(1)}, bf16[12,128,128]{2,1,0:T(8,128)(2,1)S(1)}, u32[]{:S(2)}, u32[]{:S(2)}) collective-permute-start(bf16[12,128,128]{2,1,0:T(8,128)(2,1)S(1)} %collective-permute-done.4), channel_id=1, source_target_pairs={{0,2},{1,15},{2,4},{3,1},{4,6},{5,3},{6,8},{7,5},{8,10},{9,7},{10,... | collective-permute-start | bytes 1179656 | tf_op jit(solution)/shard_map/z3/ppermute | solution.py:211
  40.8 16.6 %collective-permute-start.22 = (bf16[24,128,128]{2,1,0:T(8,128)(2,1)S(1)}, bf16[24,128,128]{2,1,0:T(8,128)(2,1)S(1)}, u32[]{:S(2)}, u32[]{:S(2)}) collective-permute-start(bf16[24,128,128]{2,1,0:T(8,128)(2,1)S(1)} %get-tuple-element.44), channel_id=1, source_target_pairs={{0,64},{1,17},{2,66},{3,19},{4,68},{5,21},{6,70},{7,23},{8,72},{9,... | collective-permute-start | bytes 2359304 | tf_op jit(solution)/shard_map/b/ppermute | solution.py:211
  41.2 16.4 %collective-permute-start.23 = (bf16[24,128,128]{2,1,0:T(8,128)(2,1)S(1)}, bf16[24,128,128]{2,1,0:T(8,128)(2,1)S(1)}, u32[]{:S(2)}, u32[]{:S(2)}) collective-permute-start(bf16[24,128,128]{2,1,0:T(8,128)(2,1)S(1)} %get-tuple-element.44), channel_id=1, source_target_pairs={{0,192},{1,49},{2,194},{3,51},{4,196},{5,53},{6,198},{7,55},{8,200... | collective-permute-start | bytes 2359304 | tf_op jit(solution)/shard_map/b/ppermute | solution.py:211
  48.0 6.9 %collective-permute-start.6 = (bf16[12,128,128]{2,1,0:T(8,128)(2,1)S(1)}, bf16[12,128,128]{2,1,0:T(8,128)(2,1)S(1)}, u32[]{:S(2)}, u32[]{:S(2)}) collective-permute-start(bf16[12,128,128]{2,1,0:T(8,128)(2,1)S(1)} %collective-permute-done.5), channel_id=1, source_target_pairs={{0,2},{1,15},{2,4},{3,1},{4,6},{5,3},{6,8},{7,5},{8,10},{9,7},{10,... | collective-permute-start | bytes 1179656 | tf_op jit(solution)/shard_map/z4/ppermute | solution.py:211
  48.3 9.1 %slice-start = ((bf16[24,128,128]{2,1,0:T(8,128)(2,1)}), bf16[12,128,128]{2,1,0:T(8,128)(2,1)S(1)}, s32[]{:S(2)}) async-start(bf16[24,128,128]{2,1,0:T(8,128)(2,1)} %copy-done.3), calls=%async_computation | async-start | bytes 786432 | tf_op jit(solution)/shard_map/gh/slice | solution.py:282
  49.3 8.3 %slice-start.1 = ((bf16[24,128,128]{2,1,0:T(8,128)(2,1)}), bf16[12,128,128]{2,1,0:T(8,128)(2,1)S(1)}, s32[]{:S(2)}) async-start(bf16[24,128,128]{2,1,0:T(8,128)(2,1)} %copy-done.4), calls=%async_computation.1 | async-start | bytes 786432 | tf_op jit(solution)/shard_map/gh/slice | solution.py:282
  49.4 16.7 %collective-permute-start.17 = (bf16[24,128,128]{2,1,0:T(8,128)(2,1)S(1)}, bf16[24,128,128]{2,1,0:T(8,128)(2,1)S(1)}, u32[]{:S(2)}, u32[]{:S(2)}) collective-permute-start(bf16[24,128,128]{2,1,0:T(8,128)(2,1)S(1)} %pad_maximum_fusion.2), channel_id=1, source_target_pairs={{0,192},{1,49},{2,194},{3,51},{4,196},{5,53},{6,198},{7,55},{8,200... | collective-permute-start | bytes 2359304 | tf_op jit(solution)/shard_map/ga/ppermute | solution.py:211
  51.3 14.8 %collective-permute-start.15 = (bf16[24,128,128]{2,1,0:T(8,128)(2,1)S(1)}, bf16[24,128,128]{2,1,0:T(8,128)(2,1)S(1)}, u32[]{:S(2)}, u32[]{:S(2)}) collective-permute-start(bf16[24,128,128]{2,1,0:T(8,128)(2,1)S(1)} %pad_maximum_fusion.1), channel_id=1, source_target_pairs={{0,64},{1,17},{2,66},{3,19},{4,68},{5,21},{6,70},{7,23},{8,72},{9,... | collective-permute-start | bytes 2359304 | tf_op jit(solution)/shard_map/ga/ppermute | solution.py:211
  54.9 6.9 %collective-permute-start.7 = (bf16[12,128,128]{2,1,0:T(8,128)(2,1)S(1)}, bf16[12,128,128]{2,1,0:T(8,128)(2,1)S(1)}, u32[]{:S(2)}, u32[]{:S(2)}) collective-permute-start(bf16[12,128,128]{2,1,0:T(8,128)(2,1)S(1)} %collective-permute-done.6), channel_id=1, source_target_pairs={{0,2},{1,15},{2,4},{3,1},{4,6},{5,3},{6,8},{7,5},{8,10},{9,7},{10,... | collective-permute-start | bytes 1179656 | tf_op jit(solution)/shard_map/z5/ppermute | solution.py:211
  57.5 21.2 %collective-permute-start.24 = (bf16[24,128,128]{2,1,0:T(8,128)(2,1)S(1)}, bf16[24,128,128]{2,1,0:T(8,128)(2,1)S(1)}, u32[]{:S(2)}, u32[]{:S(2)}) collective-permute-start(bf16[24,128,128]{2,1,0:T(8,128)(2,1)S(1)} %pad_maximum_fusion.5), channel_id=1, source_target_pairs={{0,64},{1,17},{2,66},{3,19},{4,68},{5,21},{6,70},{7,23},{8,72},{9,... | collective-permute-start | bytes 2359304 | tf_op jit(solution)/shard_map/gh/ppermute | solution.py:211
  57.8 21.1 %collective-permute-start.25 = (bf16[24,128,128]{2,1,0:T(8,128)(2,1)S(1)}, bf16[24,128,128]{2,1,0:T(8,128)(2,1)S(1)}, u32[]{:S(2)}, u32[]{:S(2)}) collective-permute-start(bf16[24,128,128]{2,1,0:T(8,128)(2,1)S(1)} %pad_maximum_fusion.6), channel_id=1, source_target_pairs={{0,192},{1,49},{2,194},{3,51},{4,196},{5,53},{6,198},{7,55},{8,200... | collective-permute-start | bytes 2359304 | tf_op jit(solution)/shard_map/gh/ppermute | solution.py:211
  61.8 7.1 %collective-permute-start.8 = (bf16[12,128,128]{2,1,0:T(8,128)(2,1)S(1)}, bf16[12,128,128]{2,1,0:T(8,128)(2,1)S(1)}, u32[]{:S(2)}, u32[]{:S(2)}) collective-permute-start(bf16[12,128,128]{2,1,0:T(8,128)(2,1)S(1)} %collective-permute-done.7), channel_id=1, source_target_pairs={{0,2},{1,15},{2,4},{3,1},{4,6},{5,3},{6,8},{7,5},{8,10},{9,7},{10,... | collective-permute-start | bytes 1179656 | tf_op jit(solution)/shard_map/z6/ppermute | solution.py:211
  66.2 11.0 %copy-start = (bf16[1,32,128,128]{3,2,1,0:T(8,128)(2,1)S(1)}, bf16[1,32,128,128]{3,2,1,0:T(8,128)(2,1)}, u32[]{:S(2)}) copy-start(bf16[1,32,128,128]{3,2,1,0:T(8,128)(2,1)} %param.8) | copy-start | bytes 3145732
  66.2 11.0 %copy-start.1 = (s32[3,272]{1,0:T(4,128)S(1)}, s32[3,272]{1,0:T(4,128)}, u32[]{:S(2)}) copy-start(s32[3,272]{1,0:T(4,128)} %get-tuple-element.24.entries) | copy-start | bytes 9796
  66.2 11.0 %copy-start.2 = (s32[3]{0:T(128)S(1)}, s32[3]{0:T(128)}, u32[]{:S(2)}) copy-start(s32[3]{0:T(128)} %get-tuple-element.23.groups) | copy-start | bytes 40
  66.3 23.8 %collective-permute-start.18 = (bf16[24,128,128]{2,1,0:T(8,128)(2,1)S(1)}, bf16[24,128,128]{2,1,0:T(8,128)(2,1)S(1)}, u32[]{:S(2)}, u32[]{:S(2)}) collective-permute-start(bf16[24,128,128]{2,1,0:T(8,128)(2,1)S(1)} %pad_maximum_fusion.3), channel_id=1, source_target_pairs={{0,64},{1,17},{2,66},{3,19},{4,68},{5,21},{6,70},{7,23},{8,72},{9,... | collective-permute-start | bytes 2359304 | tf_op jit(solution)/shard_map/a2/ppermute | solution.py:211
  69.0 8.1 %collective-permute-start.9 = (bf16[12,128,128]{2,1,0:T(8,128)(2,1)S(1)}, bf16[12,128,128]{2,1,0:T(8,128)(2,1)S(1)}, u32[]{:S(2)}, u32[]{:S(2)}) collective-permute-start(bf16[12,128,128]{2,1,0:T(8,128)(2,1)S(1)} %collective-permute-done.8), channel_id=1, source_target_pairs={{0,2},{1,15},{2,4},{3,1},{4,6},{5,3},{6,8},{7,5},{8,10},{9,7},{10,... | collective-permute-start | bytes 1179656 | tf_op jit(solution)/shard_map/z7/ppermute | solution.py:211
  72.5 17.7 %collective-permute-start.19 = (bf16[24,128,128]{2,1,0:T(8,128)(2,1)S(1)}, bf16[24,128,128]{2,1,0:T(8,128)(2,1)S(1)}, u32[]{:S(2)}, u32[]{:S(2)}) collective-permute-start(bf16[24,128,128]{2,1,0:T(8,128)(2,1)S(1)} %pad_maximum_fusion.4), channel_id=1, source_target_pairs={{0,192},{1,49},{2,194},{3,51},{4,196},{5,53},{6,198},{7,55},{8,200... | collective-permute-start | bytes 2359304 | tf_op jit(solution)/shard_map/a2/ppermute | solution.py:211
  80.5 12.9 %collective-permute-start.26 = (f32[11,128,128]{2,1,0:T(8,128)S(1)}, f32[11,128,128]{2,1,0:T(8,128)S(1)}, u32[]{:S(2)}, u32[]{:S(2)}) collective-permute-start(f32[11,128,128]{2,1,0:T(8,128)S(1)} %get-tuple-element.38), channel_id=1, source_target_pairs={{0,1},{1,0},{2,3},{3,2},{4,5},{5,4},{6,7},{7,6},{8,9},{9,8},{10,11... | collective-permute-start | bytes 2162696 | tf_op jit(solution)/shard_map/w3/ppermute | solution.py:211
  89.6 3.8 %collective-permute-start.27 = (f32[11,128,128]{2,1,0:T(8,128)S(1)}, f32[11,128,128]{2,1,0:T(8,128)S(1)}, u32[]{:S(2)}, u32[]{:S(2)}) collective-permute-start(f32[11,128,128]{2,1,0:T(8,128)S(1)} %get-tuple-element.39), channel_id=1, source_target_pairs={{0,1},{1,0},{2,3},{3,2},{4,5},{5,4},{6,7},{7,6},{8,9},{9,8},{10,11... | collective-permute-start | bytes 2162696 | tf_op jit(solution)/shard_map/w3/ppermute | solution.py:211
  89.7 3.7 %collective-permute-start.28 = (f32[10,128,128]{2,1,0:T(8,128)S(1)}, f32[10,128,128]{2,1,0:T(8,128)S(1)}, u32[]{:S(2)}, u32[]{:S(2)}) collective-permute-start(f32[10,128,128]{2,1,0:T(8,128)S(1)} %get-tuple-element.40), channel_id=1, source_target_pairs={{0,1},{1,0},{2,3},{3,2},{4,5},{5,4},{6,7},{7,6},{8,9},{9,8},{10,11... | collective-permute-start | bytes 1966088 | tf_op jit(solution)/shard_map/w3/ppermute | solution.py:211
where the time goes:
time: 97.2 us; the launch traced here: 95.6 us
  starting transfers between devices  57.6 us (59%)
  waiting for transfers between devices  19 us (20%)
  Pallas kernels  10.5 us (11%)
  local copies, waits for them, and re-layouts  6.17 us (6%)
  other arithmetic  1.84 us (2%)
    ppermute x29, starting transfers between devices, move(): return lax.ppermute(blocks, ('row', 'col'), pairs)  57.6 us
    ppermute x29, waiting for transfers between devices, move(): return lax.ppermute(blocks, ('row', 'col'), pairs)  19 us
    unnamed x39, local copies, waits for them, and re-layouts  5.58 us
    pallas_call x3, Pallas kernels, add_products(): pl.pallas_call(functools.partial(products_kernel, stage), out_shape=outs,...  5.28 us
    pallas_call x1, Pallas kernels, sort_lists(): pl.pallas_call(functools.partial(sort_kernel, left_shard, shard, depth, p...  2.96 us
    pallas_call x1, Pallas kernels, select_panel(): pl.pallas_call(select_kernel, out_shape=(jax.ShapeDtypeStruct((2 * own.sh...  2.3 us
  transfers between devices with their start and end apart: 29, of which 12 were waited for; matrix products, arithmetic and copies ran while one was open for 7% of the time, Pallas kernels for 6%

commit v1 on v0

--- a/solution.py
+++ b/solution.py
@@ -40,33 +40,42 @@
             for dx in range(SIDE):
                 for dy in range(SIDE):
                     stage, slot = UNITS[(dx, dy) if core == 0 else (dy, dx)][column]
-                    right[core, column, dx, dy] = stage << 12 | slot * shard
+                    right[core, column, dx, dy] = stage << 16 | slot * shard << 8
     return right.reshape(-1)
 
 
-def sort_kernel(left_shard, shard, depth, pairs, slots, here, right_at, own, got, entries, groups, lengths):
+def sort_kernel(left_shard, shard, depth, pairs, slots, here, right_at, own, got, entries, groups, lengths, left_of, right_of):
     x, y, z, core = here[0], here[1], here[2], here[3]
     way = 2 * core - 1
     for stage in range(STAGES):
         lengths[stage] = 0
+
+    def place(owner, carry):
+        steps = (((owner >> 1) - z) * way) & (depth - 1)
+        other = (owner & 1) ^ core
+        far = depth + 2 + 2 * (depth - 1 - steps) + 1 - other
+        at = jnp.where(steps <= depth // 2, 2 * steps + other, far)
+        left_of[owner] = (at - owner) * left_shard
+        dx = (owner - x) & (SIDE - 1)
+        dy = ((owner >> 2) - y) & (SIDE - 1)
+        for column in range(2):
+            found = right_at[((core * 2 + column) * SIDE + dx) * SIDE + dy]
+            right_of[column, owner] = found - (owner * shard << 8)
+        return carry
+
+    lax.fori_loop(0, SIDE * SIDE, place, 0)
+    base = core * 3 * pairs
     for column, lists in enumerate((own, got)):
-        base = core * 3 * pairs
-
-        def add(e, carry, column=column, lists=lists, base=base):
+
+        def add(e, carry, column=column, lists=lists):
             first = lists[base + e]
             second = lists[base + pairs + e]
             slot = lists[base + 2 * pairs + e] + column * slots
-            owner = (first * (2**16 // left_shard + 1)) >> 16
-            steps = (((owner >> 1) - z) * way) & (depth - 1)
-            left = first + (2 * steps + ((owner & 1) ^ core) - owner) * left_shard
-            owner = (second * (2**16 // shard + 1)) >> 16
-            dx = (owner - x) & (SIDE - 1)
-            dy = ((owner >> 2) - y) & (SIDE - 1)
-            found = right_at[((core * 2 + column) * SIDE + dx) * SIDE + dy]
-            stage = found >> 12
-            place = (found & 4095) + second - owner * shard
+            left = first + left_of[(first * (2**16 // left_shard + 1)) >> 16]
+            found = right_of[column, (second * (2**16 // shard + 1)) >> 16] + (second << 8)
+            stage = found >> 16
             at = lengths[stage]
-            entries[stage, at] = left | place << 8 | slot << 16
+            entries[stage, at] = left | (found & 0xFF00) | slot << 16
             lengths[stage] = at + 1
             return carry
 
@@ -89,20 +98,24 @@
         ),
         in_specs=[smem] * 4,
         out_specs=(smem, smem),
-        scratch_shapes=[pltpu.SMEM((STAGES,), jnp.int32)],
+        scratch_shapes=[
+            pltpu.SMEM((STAGES,), jnp.int32),
+            pltpu.SMEM((SIDE * SIDE,), jnp.int32),
+            pltpu.SMEM((2, SIDE * SIDE), jnp.int32),
+        ],
         cost_estimate=pl.CostEstimate(flops=0, bytes_accessed=8 * 2**20, transcendentals=0),
         name="sort_lists",
     )(here, jnp.asarray(place_right(shard)), own, got)
 
 
-def select_kernel(core, own, got, own_left, got_left, unit, pair, sems):
+def select_kernel(core, own, own_left, keep, give, left, sems):
     c = core[0]
-    shard, left_shard = own.shape[1], own_left.shape[1]
+    size = own_left.shape[1]
     copies = [
-        pltpu.make_async_copy(own.at[c], unit.at[pl.ds(0, shard)], sems.at[0]),
-        pltpu.make_async_copy(got.at[c], unit.at[pl.ds(shard, shard)], sems.at[1]),
-        pltpu.make_async_copy(own_left.at[c], pair.at[pl.ds(0, left_shard)], sems.at[2]),
-        pltpu.make_async_copy(got_left.at[c], pair.at[pl.ds(left_shard, left_shard)], sems.at[3]),
+        pltpu.make_async_copy(own.at[1 - c], give, sems.at[0]),
+        pltpu.make_async_copy(own.at[c], keep, sems.at[1]),
+        pltpu.make_async_copy(own_left.at[c], left.at[pl.ds(0, size)], sems.at[2]),
+        pltpu.make_async_copy(own_left.at[1 - c], left.at[pl.ds(size, size)], sems.at[3]),
     ]
     for copy in copies:
         copy.start()
@@ -110,22 +123,19 @@
         copy.wait()
 
 
-def select_panel(core, own, got, own_left, got_left):
+def select_panels(core, own, own_left):
     hbm = pl.BlockSpec(memory_space=pl.ANY)
     vmem = pl.BlockSpec(memory_space=pltpu.VMEM)
-    block = own.shape[-2:]
+    shard, left_shard, *block = own.shape[1], own_left.shape[1], *own.shape[2:]
     return pl.pallas_call(
         select_kernel,
-        out_shape=(
-            jax.ShapeDtypeStruct((2 * own.shape[1], *block), own.dtype),
-            jax.ShapeDtypeStruct((2 * own_left.shape[1], *block), own.dtype),
-        ),
-        in_specs=[pl.BlockSpec(memory_space=pltpu.SMEM)] + [hbm] * 4,
-        out_specs=(vmem, vmem),
+        out_shape=[jax.ShapeDtypeStruct((n, *block), own.dtype) for n in (shard, shard, 2 * left_shard)],
+        in_specs=[pl.BlockSpec(memory_space=pltpu.SMEM), hbm, hbm],
+        out_specs=[vmem] * 3,
         scratch_shapes=[pltpu.SemaphoreType.DMA((4,))],
         cost_estimate=pl.CostEstimate(flops=0, bytes_accessed=2**20, transcendentals=0),
-        name="select_panel",
-    )(core.reshape(1), own, got, own_left, got_left)
+        name="select_panels",
+    )(core.reshape(1), own, own_left)
 
 
 def products_kernel(stage, groups, entries, left, right, *refs):
@@ -193,7 +203,7 @@
         out_specs=[vmem] * len(outs),
         scratch_shapes=scratch,
         cost_estimate=pl.CostEstimate(flops=2**20, bytes_accessed=2**20, transcendentals=0),
-        compiler_params=pltpu.CompilerParams(vmem_limit_bytes=28 * 2**20),
+        compiler_params=pltpu.CompilerParams(vmem_limit_bytes=8 * 2**20),
         name="products",
     )(groups, entries, left, right, *starts)
 
@@ -249,28 +259,38 @@
     scope = jax.named_scope
 
     own, own_left = square_panels[:, 0], x_panels[:, 0]
+    keep, give, own_left = select_panels(core, own, own_left)
     with scope("w0"):
-        got = sibling(own)
+        got = sibling(give)
     with scope("w1"):
         got_left = sibling(own_left)
     lists = join(pair_lists.reshape(-1), pair_counts.reshape(-1))
     with scope("w2"):
         got_lists = sibling(lists)
-    unit, pair = select_panel(core, own, got, own_left, got_left)
-
+    unit = join(keep, got)
+    pair = join(own_left[:left_shard], got_left[left_shard:], own_left[left_shard:], got_left[:left_shard])
+
+    unit, pair = order(unit), order(pair)
     with scope("s1"):
         r1, l1 = first(unit, unit)
     with scope("t"):
         t = second(unit, unit)
     entries, groups = sort_lists(here, lists, got_lists, left_shard, shard, depth, pairs, slots)
-    passed = [pair]
-    for step in range(1, depth):
-        with scope(f"z{step}"):
-            passed.append(onward(passed[-1]))
-    left = join(*passed)
+    half = 2 * left_shard
+    with scope("z1"):
+        z1 = onward(pair)
+    with scope("z2"):
+        z2 = onward(z1)
+    with scope("z3"):
+        z3 = onward(z2)
+    with scope("z4"):
+        z4 = onward(z3[:half])
+    with scope("w4"):
+        swapped = sibling(join(z1[half:], z2[half:], z3[half:]))
+    left = join(pair[:half], z1[:half], z2[:half], z3[:half], z4, swapped)
     with scope("s2"):
         s2 = first(r1[:shard], l1[shard:])
-    t, ar, al = order((t, r1, l1))
+    t, ar, al, entries, groups = order((t, r1, l1, entries, groups))
     with scope("a1"):
         a1 = second(ar, al)
     x2 = join(*s2)

time: 97.2 us -> 90.8 us (0.934); the launches traced: 95.6 us -> 90.7 us
  starting transfers between devices: 57.6 us -> 39.1 us
  Pallas kernels: 10.5 us -> 15.9 us
  waiting for transfers between devices: 19 us -> 22.6 us
  local copies, waits for them, and re-layouts: 6.17 us -> 8.58 us
  other arithmetic: 1.84 us -> 4 us
    ppermute x29 -> x27, starting transfers between devices: 57.6 us -> 39.1 us  [move(): return lax.ppermute(blocks, ('row', 'col'), pairs)]
    ppermute x29 -> x27, waiting for transfers between devices: 19 us -> 22.6 us  [move(): return lax.ppermute(blocks, ('row', 'col'), pairs)]
    pallas_call x3, Pallas kernels: 5.28 us -> 8.38 us  [add_products(): pl.pallas_call(functools.partial(products_kernel, stage), out_shape=outs,...]
    slice x0 -> x5, local copies, waits for them, and re-layouts: none -> 2.52 us  [the longest x3 1.45 us: on_device(): swapped = sibling(join(z1[half:], z2[half:], z3[half:]))]
    pallas_call x1, Pallas kernels: 2.96 us -> 5.19 us  [sort_lists(): pl.pallas_call(functools.partial(sort_kernel, left_shard, shard, depth, p...]
    concatenate x8 -> x11, other arithmetic: 1.22 us -> 3.4 us  [join(): return jnp.concatenate(pieces)]
    unnamed x39 -> x28, local copies, waits for them, and re-layouts: 5.58 us -> 4.35 us
    slice x2 -> x1, local copies, waits for them, and re-layouts: 0.01 us -> 1.02 us  [on_device(): t[1][shard:]]
  transfers between devices with their start and end apart: 29 -> 27, of which waited for: 12 -> 8; matrix products, arithmetic and copies ran while one was open for 7% -> 14% of each run, Pallas kernels for 6% -> 12%
where the time goes in v1:
time: 90.8 us; the launch traced here: 90.7 us
  starting transfers between devices  39.1 us (43%)
  waiting for transfers between devices  22.6 us (25%)
  Pallas kernels  15.9 us (18%)
  local copies, waits for them, and re-layouts  8.58 us (9%)
  other arithmetic  4 us (4%)
    ppermute x27, starting transfers between devices, move(): return lax.ppermute(blocks, ('row', 'col'), pairs)  39.1 us
    ppermute x27, waiting for transfers between devices, move(): return lax.ppermute(blocks, ('row', 'col'), pairs)  22.6 us
    pallas_call x3, Pallas kernels, add_products(): pl.pallas_call(functools.partial(products_kernel, stage), out_shape=outs,...  8.38 us
    pallas_call x1, Pallas kernels, sort_lists(): pl.pallas_call(functools.partial(sort_kernel, left_shard, shard, depth, p...  5.19 us
    unnamed x28, local copies, waits for them, and re-layouts  4.35 us
    concatenate x11, other arithmetic, join(): return jnp.concatenate(pieces)  3.4 us
    pallas_call x1, Pallas kernels, select_panels(): pl.pallas_call(select_kernel, out_shape=[jax.ShapeDtypeStruct((n, *block)...  2.28 us
  transfers between devices with their start and end apart: 27, of which 8 were waited for; matrix products, arithmetic and copies ran while one was open for 14% of the time, Pallas kernels for 12%

profile of v1, /device:TPU:1, one launch (start us, length us, event | category | flops | bytes accessed | tf_op | source)
XLA Modules:
  0.0 90.7 jit_solution(6034121510249414784)
XLA Ops:
  0.0 2.3 %select_panels.1 = (bf16[12,128,128]{2,1,0:T(8,128)(2,1)}, bf16[12,128,128]{2,1,0:T(8,128)(2,1)}, bf16[12,128,128]{2,1,0:T(8,128)(2,1)}) custom-call(s32[1]{0:T(128)} %bitcast.core, bf16[2,12,128,128]{3,2,1,0:T(8,128)(2,1)} %bitcast.10, bf16[2,6,128,128]{3,2,1,0:T(8,128)(2,1)} %bitcast.11), custom_call_target="tpu_custom_call" | custom-call | bytes 1048576 | tf_op jit(solution)/shard_map/select_panels/pallas_call | solution.py:130
  2.3 3.3 %collective-permute-start = (bf16[12,128,128]{2,1,0:T(8,128)(2,1)}, bf16[12,128,128]{2,1,0:T(8,128)(2,1)S(1)}, u32[]{:S(2)}, u32[]{:S(2)}) collective-permute-start(bf16[12,128,128]{2,1,0:T(8,128)(2,1)} %get-tuple-element.27), channel_id=1, source_target_pairs={{0,1},{1,0},{2,3},{3,2},{4,5},{5,4},{6,7},{7,6},{8,9},{9,8},{10,11... | collective-permute-start | bytes 1179656 | tf_op jit(solution)/shard_map/w0/ppermute | solution.py:221
  5.6 0.1 collective-permute-start.6
  5.7 0.7 copy.7
  6.4 0.7 pad_add_fusion.own
  7.1 0.4 collective-permute-start.5
  7.5 1.0 %fusion.4 = (bf16[6,128,128]{2,1,0:T(8,128)(2,1)S(1)}, bf16[6,128,128]{2,1,0:T(8,128)(2,1)S(1)}) fusion(bf16[12,128,128]{2,1,0:T(8,128)(2,1)} %get-tuple-element.32), kind=kLoop, calls=%fused_computation.39 | loop fusion | bytes 786432 | tf_op jit(solution)/shard_map/slice | solution.py:271
  8.5 1.1 %pad_maximum_fusion.2 = bf16[24,128,128]{2,1,0:T(8,128)(2,1)S(1)} fusion(bf16[12,128,128]{2,1,0:T(8,128)(2,1)S(1)} %collective-permute-done, bf16[12,128,128]{2,1,0:T(8,128)(2,1)} %get-tuple-element.26), kind=kLoop, calls=%fused_computation.2 | loop fusion | flops 393216 | bytes 1572864 | tf_op jit(solution)/shard_map/concatenate | solution.py:247
  9.6 0.1 collective-permute-start.3
  9.7 2.7 %collective-permute-start.4 = (bf16[24,128,128]{2,1,0:T(8,128)(2,1)S(1)}, bf16[24,128,128]{2,1,0:T(8,128)(2,1)S(1)}, u32[]{:S(2)}, u32[]{:S(2)}) collective-permute-start(bf16[24,128,128]{2,1,0:T(8,128)(2,1)S(1)} %pad_maximum_fusion.2), channel_id=1, source_target_pairs={{0,48},{1,193},{2,50},{3,195},{4,52},{5,197},{6,54},{7,199},{8,56}... | collective-permute-start | bytes 2359304 | tf_op jit(solution)/shard_map/s1/ppermute | solution.py:221
  12.4 2.7 %collective-permute-start.2 = (bf16[24,128,128]{2,1,0:T(8,128)(2,1)S(1)}, bf16[24,128,128]{2,1,0:T(8,128)(2,1)}, u32[]{:S(2)}, u32[]{:S(2)}) collective-permute-start(bf16[24,128,128]{2,1,0:T(8,128)(2,1)S(1)} %pad_maximum_fusion.2), channel_id=1, source_target_pairs={{0,192},{1,49},{2,194},{3,51},{4,196},{5,53},{6,198},{7,55},{8,200... | collective-permute-start | bytes 2359304 | tf_op jit(solution)/shard_map/t/ppermute | solution.py:221
  15.1 1.0 %pad_maximum_fusion.3 = bf16[24,128,128]{2,1,0:T(8,128)(2,1)} fusion(bf16[6,128,128]{2,1,0:T(8,128)(2,1)S(1)} %get-tuple-element.63, bf16[6,128,128]{2,1,0:T(8,128)(2,1)S(1)} %get-tuple-element.61, bf16[6,128,128]{2,1,0:T(8,128)(2,1)S(1)} %get-tuple-element.62, bf16[6,128,128]{2,1,0:T(8,128)(2,1)S(1)} %get-tuple-element.60), kind=kLoop, calls=%fused_computation.3 | loop fusion | flops 1179648 | bytes 1572864 | tf_op jit(solution)/shard_map/concatenate | solution.py:247
  16.1 4.0 %collective-permute-start.7 = (bf16[24,128,128]{2,1,0:T(8,128)(2,1)}, bf16[24,128,128]{2,1,0:T(8,128)(2,1)}, u32[]{:S(2)}, u32[]{:S(2)}) collective-permute-start(bf16[24,128,128]{2,1,0:T(8,128)(2,1)} %pad_maximum_fusion.3), channel_id=1, source_target_pairs={{0,2},{1,15},{2,4},{3,1},{4,6},{5,3},{6,8},{7,5},{8,10},{9,7},{10,... | collective-permute-start | bytes 2359304 | tf_op jit(solution)/shard_map/z1/ppermute | solution.py:221
  20.1 0.6 pad_add_fusion.1.here
  20.7 5.2 %sort_lists.1 = (s32[3,272]{1,0:T(4,128)}, s32[3]{0:T(128)}) custom-call(s32[4]{0:T(128)} %pad_add_fusion.1.here, s32[64]{0:T(128)} %constant.51.clone.right_at, s32[770]{0:T(1024)} %copy-done.4, s32[770]{0:T(1024)} %copy-done.5), custom_call_target="tpu_custom_call" | custom-call | bytes 8388608 | tf_op jit(solution)/shard_map/sort_lists/pallas_call | solution.py:93
  25.9 1.0 %slice_dynamic-update-slice_fusion.2 = bf16[96,128,128]{2,1,0:T(8,128)(2,1)S(1)} fusion(bf16[24,128,128]{2,1,0:T(8,128)(2,1)} %pad_maximum_fusion.3), kind=kLoop, calls=%fused_computation.12 | loop fusion | bytes 786432
  27.1 0.1 collective-permute-start.18
  27.2 2.7 %collective-permute-start.19 = (bf16[12,128,128]{2,1,0:T(8,128)(2,1)S(1)}, bf16[12,128,128]{2,1,0:T(8,128)(2,1)S(1)}, u32[]{:S(2)}, u32[]{:S(2)}) collective-permute-start(bf16[12,128,128]{2,1,0:T(8,128)(2,1)S(1)} %slice.108), channel_id=1, source_target_pairs={{0,48},{1,193},{2,50},{3,195},{4,52},{5,197},{6,54},{7,199},{8,56}... | collective-permute-start | bytes 1179656 | tf_op jit(solution)/shard_map/s2/ppermute | solution.py:221
  29.9 1.2 %collective-permute-done.1 = bf16[24,128,128]{2,1,0:T(8,128)(2,1)S(1)} collective-permute-done((bf16[24,128,128]{2,1,0:T(8,128)(2,1)S(1)}, bf16[24,128,128]{2,1,0:T(8,128)(2,1)S(1)}, u32[]{:S(2)}, u32[]{:S(2)}) %collective-permute-start.1) | collective-permute-done | bytes 786464 | tf_op jit(solution)/shard_map/t/ppermute | solution.py:221
  31.1 2.7 %collective-permute-start.14 = (bf16[24,128,128]{2,1,0:T(8,128)(2,1)S(1)}, bf16[24,128,128]{2,1,0:T(8,128)(2,1)S(1)}, u32[]{:S(2)}, u32[]{:S(2)}) collective-permute-start(bf16[24,128,128]{2,1,0:T(8,128)(2,1)S(1)} %collective-permute-done.4), channel_id=1, source_target_pairs={{0,192},{1,49},{2,194},{3,51},{4,196},{5,53},{6,198},{7,55},{8,200... | collective-permute-start | bytes 2359304 | tf_op jit(solution)/shard_map/a1/ppermute | solution.py:221
  33.8 1.0 %slice.96 = bf16[12,128,128]{2,1,0:T(8,128)(2,1)S(1)} slice(bf16[24,128,128]{2,1,0:T(8,128)(2,1)} %collective-permute-done.2), slice={[12:24], [0:128], [0:128]} | slice | bytes 786432 | tf_op jit(solution)/shard_map/gh/slice | solution.py:302
  34.9 4.2 %collective-permute-start.8 = (bf16[24,128,128]{2,1,0:T(8,128)(2,1)}, bf16[24,128,128]{2,1,0:T(8,128)(2,1)S(1)}, u32[]{:S(2)}, u32[]{:S(2)}) collective-permute-start(bf16[24,128,128]{2,1,0:T(8,128)(2,1)} %collective-permute-done.7), channel_id=1, source_target_pairs={{0,2},{1,15},{2,4},{3,1},{4,6},{5,3},{6,8},{7,5},{8,10},{9,7},{10,... | collective-permute-start | bytes 2359304 | tf_op jit(solution)/shard_map/z2/ppermute | solution.py:221
  39.0 1.2 %fusion.1 = (bf16[12,128,128]{2,1,0:T(8,128)(2,1)S(1)}, bf16[96,128,128]{2,1,0:T(8,128)(2,1)S(1)}) fusion(bf16[24,128,128]{2,1,0:T(8,128)(2,1)} %collective-permute-done.7, bf16[96,128,128]{2,1,0:T(8,128)(2,1)S(1)} %slice_dynamic-update-slice_fusion.2), kind=kLoop, calls=%fused_computation.36 | loop fusion | bytes 1572864 | tf_op jit(solution)/shard_map/w4/slice | solution.py:289
  40.2 0.1 constant_dynamic-update-slice_fusion.18
  40.3 0.1 constant_dynamic-update-slice_fusion.17
  40.5 0.1 constant_dynamic-update-slice_fusion.16
  40.6 0.2 constant_dynamic-update-slice_fusion.15
  40.8 0.1 collective-permute-start.20
  40.9 2.7 %collective-permute-start.21 = (bf16[24,128,128]{2,1,0:T(8,128)(2,1)S(1)}, bf16[24,128,128]{2,1,0:T(8,128)(2,1)S(1)}, u32[]{:S(2)}, u32[]{:S(2)}) collective-permute-start(bf16[24,128,128]{2,1,0:T(8,128)(2,1)S(1)} %get-tuple-element.57), channel_id=1, source_target_pairs={{0,192},{1,49},{2,194},{3,51},{4,196},{5,53},{6,198},{7,55},{8,200... | collective-permute-start | bytes 2359304 | tf_op jit(solution)/shard_map/b/ppermute | solution.py:221
  43.6 0.1 constant_dynamic-update-slice_fusion.14
  43.7 1.3 %constant_dynamic-update-slice_fusion.13 = bf16[192,128,128]{2,1,0:T(8,128)(2,1)S(1)} fusion(bf16[192,128,128]{2,1,0:T(8,128)(2,1)S(1)} %constant_dynamic-update-slice_fusion.14, bf16[24,128,128]{2,1,0:T(8,128)(2,1)} %collective-permute-done.2), kind=kLoop, calls=%fused_computation.26 | loop fusion | bytes 1572864
  45.0 3.3 %collective-permute-done.8 = bf16[24,128,128]{2,1,0:T(8,128)(2,1)S(1)} collective-permute-done((bf16[24,128,128]{2,1,0:T(8,128)(2,1)}, bf16[24,128,128]{2,1,0:T(8,128)(2,1)S(1)}, u32[]{:S(2)}, u32[]{:S(2)}) %collective-permute-start.8) | collective-permute-done | bytes 786464 | tf_op jit(solution)/shard_map/z2/ppermute | solution.py:221
  48.3 3.0 %collective-permute-start.9 = (bf16[24,128,128]{2,1,0:T(8,128)(2,1)S(1)}, bf16[24,128,128]{2,1,0:T(8,128)(2,1)S(1)}, u32[]{:S(2)}, u32[]{:S(2)}) collective-permute-start(bf16[24,128,128]{2,1,0:T(8,128)(2,1)S(1)} %collective-permute-done.8), channel_id=1, source_target_pairs={{0,2},{1,15},{2,4},{3,1},{4,6},{5,3},{6,8},{7,5},{8,10},{9,7},{10,... | collective-permute-start | bytes 2359304 | tf_op jit(solution)/shard_map/z3/ppermute | solution.py:221
  51.4 1.3 %collective-permute-start.15 = (bf16[24,128,128]{2,1,0:T(8,128)(2,1)S(1)}, bf16[24,128,128]{2,1,0:T(8,128)(2,1)S(1)}, u32[]{:S(2)}, u32[]{:S(2)}) collective-permute-start(bf16[24,128,128]{2,1,0:T(8,128)(2,1)S(1)} %pad_maximum_fusion.5), channel_id=1, source_target_pairs={{0,192},{1,49},{2,194},{3,51},{4,196},{5,53},{6,198},{7,55},{8,200... | collective-permute-start | bytes 2359304 | tf_op jit(solution)/shard_map/ga/ppermute | solution.py:221
  52.8 0.3 collective-permute-start.13
  53.1 0.1 constant_dynamic-update-slice_fusion.12
  53.2 0.1 constant_dynamic-update-slice_fusion.11.right
  53.3 0.1 fusion.2
  53.4 1.3 %collective-permute-done.20 = bf16[24,128,128]{2,1,0:T(8,128)(2,1)S(1)} collective-permute-done((bf16[24,128,128]{2,1,0:T(8,128)(2,1)S(1)}, bf16[24,128,128]{2,1,0:T(8,128)(2,1)S(1)}, u32[]{:S(2)}, u32[]{:S(2)}) %collective-permute-start.20) | collective-permute-done | bytes 786464 | tf_op jit(solution)/shard_map/b/ppermute | solution.py:221
  54.8 0.1 collective-permute-start.22
  55.0 5.2 %collective-permute-done.9 = bf16[24,128,128]{2,1,0:T(8,128)(2,1)S(1)} collective-permute-done((bf16[24,128,128]{2,1,0:T(8,128)(2,1)S(1)}, bf16[24,128,128]{2,1,0:T(8,128)(2,1)S(1)}, u32[]{:S(2)}, u32[]{:S(2)}) %collective-permute-start.9) | collective-permute-done | bytes 786464 | tf_op jit(solution)/shard_map/z3/ppermute | solution.py:221
  60.2 0.2 fusion.3
  60.4 0.1 pad_maximum_fusion.1
  60.5 5.9 %collective-permute-start.11 = (bf16[36,128,128]{2,1,0:T(8,128)(2,1)S(1)}, bf16[36,128,128]{2,1,0:T(8,128)(2,1)S(1)}, u32[]{:S(2)}, u32[]{:S(2)}) collective-permute-start(bf16[36,128,128]{2,1,0:T(8,128)(2,1)S(1)} %pad_maximum_fusion.1), channel_id=1, source_target_pairs={{0,1},{1,0},{2,3},{3,2},{4,5},{5,4},{6,7},{7,6},{8,9},{9,8},{10,11... | collective-permute-start | bytes 3538952 | tf_op jit(solution)/shard_map/w4/ppermute | solution.py:221
  66.5 0.3 collective-permute-start.23
  66.8 0.1 constant_dynamic-update-slice_fusion.9
  66.9 1.8 %collective-permute-start.10 = (bf16[12,128,128]{2,1,0:T(8,128)(2,1)S(1)}, bf16[12,128,128]{2,1,0:T(8,128)(2,1)S(1)}, u32[]{:S(2)}, u32[]{:S(2)}) collective-permute-start(bf16[12,128,128]{2,1,0:T(8,128)(2,1)S(1)} %get-tuple-element.55), channel_id=1, source_target_pairs={{0,2},{1,15},{2,4},{3,1},{4,6},{5,3},{6,8},{7,5},{8,10},{9,7},{10,... | collective-permute-start | bytes 1179656 | tf_op jit(solution)/shard_map/z4/ppermute | solution.py:221
  68.9 0.1 collective-permute-start.16
  69.1 0.1 constant_dynamic-update-slice_fusion.8
  69.2 0.1 constant_dynamic-update-slice_fusion.7
  69.4 4.2 %collective-permute-done.22 = bf16[24,128,128]{2,1,0:T(8,128)(2,1)S(1)} collective-permute-done((bf16[24,128,128]{2,1,0:T(8,128)(2,1)S(1)}, bf16[24,128,128]{2,1,0:T(8,128)(2,1)S(1)}, u32[]{:S(2)}, u32[]{:S(2)}) %collective-permute-start.22) | collective-permute-done | bytes 786464 | tf_op jit(solution)/shard_map/gh/ppermute | solution.py:221
  73.6 0.1 constant_dynamic-update-slice_fusion.6
  73.8 3.9 %collective-permute-done.23 = bf16[24,128,128]{2,1,0:T(8,128)(2,1)S(1)} collective-permute-done((bf16[24,128,128]{2,1,0:T(8,128)(2,1)S(1)}, bf16[24,128,128]{2,1,0:T(8,128)(2,1)S(1)}, u32[]{:S(2)}, u32[]{:S(2)}) %collective-permute-start.23) | collective-permute-done | bytes 786464 | tf_op jit(solution)/shard_map/gh/ppermute | solution.py:221
  77.7 0.1 constant_dynamic-update-slice_fusion.5.right
  77.9 0.2 constant_dynamic-update-slice_fusion.left
  78.1 2.7 %products.3.refs_0_ = f32[65,128,128]{2,1,0:T(8,128)S(1)} custom-call(s32[3]{0:T(128)S(1)} %copy-done.2, s32[3,272]{1,0:T(4,128)S(1)} %copy-done.1, bf16[96,128,128]{2,1,0:T(8,128)(2,1)S(1)} %constant_dynamic-update-slice_fusion.left, bf16[192,128,128]{2,1,0:T(8,128)(2,1)S(1)} %constant_dynamic-update-slice_fusion.11.right, bf16[32,128,128]{2,1,0:T(8,128)(2,1)S(1)} %bitcast.9), custom_call_target="tpu_custom_call" | custom-call | flops 1048576 | bytes 1048576 | tf_op jit(solution)/shard_map/products/pallas_call | solution.py:199
  80.8 3.1 %products.4 = (f32[32,128,128]{2,1,0:T(8,128)S(1)}, f32[11,128,128]{2,1,0:T(8,128)S(1)}, f32[11,128,128]{2,1,0:T(8,128)S(1)}, f32[10,128,128]{2,1,0:T(8,128)S(1)}) custom-call(s32[3]{0:T(128)S(1)} %copy-done.2, s32[3,272]{1,0:T(4,128)S(1)} %copy-done.1, bf16[96,128,128]{2,1,0:T(8,128)(2,1)S(1)} %constant_dynamic-update-slice_fusion.left, ...), custom_call_target="tpu_custom_call" | custom-call | flops 1048576 | bytes 1048576 | tf_op jit(solution)/shard_map/products/pallas_call | solution.py:199
  83.9 0.1 collective-permute-start.24
  84.0 0.5 collective-permute-start.25
  84.5 0.1 collective-permute-start.26
  84.6 1.5 %collective-permute-done.17 = bf16[24,128,128]{2,1,0:T(8,128)(2,1)S(1)} collective-permute-done((bf16[24,128,128]{2,1,0:T(8,128)(2,1)S(1)}, bf16[24,128,128]{2,1,0:T(8,128)(2,1)S(1)}, u32[]{:S(2)}, u32[]{:S(2)}) %collective-permute-start.17) | collective-permute-done | bytes 786464 | tf_op jit(solution)/shard_map/a2/ppermute | solution.py:221
  86.1 0.1 pad_maximum_fusion.right
  86.2 1.9 %collective-permute-done.26.refs_3_ = f32[10,128,128]{2,1,0:T(8,128)S(1)} collective-permute-done((f32[10,128,128]{2,1,0:T(8,128)S(1)}, f32[10,128,128]{2,1,0:T(8,128)S(1)}, u32[]{:S(2)}, u32[]{:S(2)}) %collective-permute-start.26) | collective-permute-done | bytes 655392 | tf_op jit(solution)/shard_map/w3/ppermute | solution.py:221
  88.1 2.6 %products.5 = bf16[32,128,128]{2,1,0:T(8,128)(2,1)} custom-call(s32[3]{0:T(128)S(1)} %copy-done.2, s32[3,272]{1,0:T(4,128)S(1)} %copy-done.1, bf16[96,128,128]{2,1,0:T(8,128)(2,1)S(1)} %constant_dynamic-update-slice_fusion.left, bf16[48,128,128]{2,1,0:T(8,128)(2,1)S(1)} %pad_maximum_fusion.right, f32[32,128,128]{2,1,0:T(8,128)S(1)} %get-tuple-element.43.refs_0_, ...), custom_call_target="tpu_custom_call" | custom-call | flops 1048576 | bytes 1048576 | tf_op jit(solution)/shard_map/products/pallas_call | solution.py:199
  (57 shorter events, 1.0 us)
Async XLA Ops:
  2.3 6.3 %collective-permute-start = (bf16[12,128,128]{2,1,0:T(8,128)(2,1)}, bf16[12,128,128]{2,1,0:T(8,128)(2,1)S(1)}, u32[]{:S(2)}, u32[]{:S(2)}) collective-permute-start(bf16[12,128,128]{2,1,0:T(8,128)(2,1)} %get-tuple-element.27), channel_id=1, source_target_pairs={{0,1},{1,0},{2,3},{3,2},{4,5},{5,4},{6,7},{7,6},{8,9},{9,8},{10,11... | collective-permute-start | bytes 1179656 | tf_op jit(solution)/shard_map/w0/ppermute | solution.py:221
  5.6 6.8 %collective-permute-start.6 = (bf16[12,128,128]{2,1,0:T(8,128)(2,1)}, bf16[12,128,128]{2,1,0:T(8,128)(2,1)S(1)}, u32[]{:S(2)}, u32[]{:S(2)}) collective-permute-start(bf16[12,128,128]{2,1,0:T(8,128)(2,1)} %get-tuple-element.32), channel_id=1, source_target_pairs={{0,1},{1,0},{2,3},{3,2},{4,5},{5,4},{6,7},{7,6},{8,9},{9,8},{10,11... | collective-permute-start | bytes 1179656 | tf_op jit(solution)/shard_map/w1/ppermute | solution.py:221
  7.1 13.6 %copy-start.4 = (s32[770]{0:T(1024)}, s32[770]{0:T(1024)S(1)}, u32[]{:S(2)}) copy-start(s32[770]{0:T(1024)S(1)} %pad_add_fusion.own) | copy-start | bytes 9244
  7.1 9.0 %collective-permute-start.5 = (s32[770]{0:T(1024)S(1)}, s32[770]{0:T(1024)S(1)}, u32[]{:S(2)}, u32[]{:S(2)}) collective-permute-start(s32[770]{0:T(1024)S(1)} %pad_add_fusion.own), channel_id=1, source_target_pairs={{0,1},{1,0},{2,3},{3,2},{4,5},{5,4},{6,7},{7,6},{8,9},{9,8},{10,11... | collective-permute-start | bytes 9248 | tf_op jit(solution)/shard_map/w2/ppermute | solution.py:221
  9.6 17.4 %collective-permute-start.3 = (bf16[24,128,128]{2,1,0:T(8,128)(2,1)S(1)}, bf16[24,128,128]{2,1,0:T(8,128)(2,1)S(1)}, u32[]{:S(2)}, u32[]{:S(2)}) collective-permute-start(bf16[24,128,128]{2,1,0:T(8,128)(2,1)S(1)} %pad_maximum_fusion.2), channel_id=1, source_target_pairs={{0,16},{1,65},{2,18},{3,67},{4,20},{5,69},{6,22},{7,71},{8,24},{9,... | collective-permute-start | bytes 2359304 | tf_op jit(solution)/shard_map/s1/ppermute | solution.py:221
  9.7 17.4 %collective-permute-start.4 = (bf16[24,128,128]{2,1,0:T(8,128)(2,1)S(1)}, bf16[24,128,128]{2,1,0:T(8,128)(2,1)S(1)}, u32[]{:S(2)}, u32[]{:S(2)}) collective-permute-start(bf16[24,128,128]{2,1,0:T(8,128)(2,1)S(1)} %pad_maximum_fusion.2), channel_id=1, source_target_pairs={{0,48},{1,193},{2,50},{3,195},{4,52},{5,197},{6,54},{7,199},{8,56}... | collective-permute-start | bytes 2359304 | tf_op jit(solution)/shard_map/s1/ppermute | solution.py:221
  12.4 18.8 %collective-permute-start.1 = (bf16[24,128,128]{2,1,0:T(8,128)(2,1)S(1)}, bf16[24,128,128]{2,1,0:T(8,128)(2,1)S(1)}, u32[]{:S(2)}, u32[]{:S(2)}) collective-permute-start(bf16[24,128,128]{2,1,0:T(8,128)(2,1)S(1)} %pad_maximum_fusion.2), channel_id=1, source_target_pairs={{0,64},{1,17},{2,66},{3,19},{4,68},{5,21},{6,70},{7,23},{8,72},{9,... | collective-permute-start | bytes 2359304 | tf_op jit(solution)/shard_map/t/ppermute | solution.py:221
  12.4 18.8 %collective-permute-start.2 = (bf16[24,128,128]{2,1,0:T(8,128)(2,1)S(1)}, bf16[24,128,128]{2,1,0:T(8,128)(2,1)}, u32[]{:S(2)}, u32[]{:S(2)}) collective-permute-start(bf16[24,128,128]{2,1,0:T(8,128)(2,1)S(1)} %pad_maximum_fusion.2), channel_id=1, source_target_pairs={{0,192},{1,49},{2,194},{3,51},{4,196},{5,53},{6,198},{7,55},{8,200... | collective-permute-start | bytes 2359304 | tf_op jit(solution)/shard_map/t/ppermute | solution.py:221
  16.1 4.6 %copy-start.5 = (s32[770]{0:T(1024)}, s32[770]{0:T(1024)S(1)}, u32[]{:S(2)}) copy-start(s32[770]{0:T(1024)S(1)} %collective-permute-done.5.got) | copy-start | bytes 9244
  16.1 18.8 %collective-permute-start.7 = (bf16[24,128,128]{2,1,0:T(8,128)(2,1)}, bf16[24,128,128]{2,1,0:T(8,128)(2,1)}, u32[]{:S(2)}, u32[]{:S(2)}) collective-permute-start(bf16[24,128,128]{2,1,0:T(8,128)(2,1)} %pad_maximum_fusion.3), channel_id=1, source_target_pairs={{0,2},{1,15},{2,4},{3,1},{4,6},{5,3},{6,8},{7,5},{8,10},{9,7},{10,... | collective-permute-start | bytes 2359304 | tf_op jit(solution)/shard_map/z1/ppermute | solution.py:221
  27.1 13.4 %collective-permute-start.18 = (bf16[12,128,128]{2,1,0:T(8,128)(2,1)S(1)}, bf16[12,128,128]{2,1,0:T(8,128)(2,1)S(1)}, u32[]{:S(2)}, u32[]{:S(2)}) collective-permute-start(bf16[12,128,128]{2,1,0:T(8,128)(2,1)S(1)} %get-tuple-element.47), channel_id=1, source_target_pairs={{0,16},{1,65},{2,18},{3,67},{4,20},{5,69},{6,22},{7,71},{8,24},{9,... | collective-permute-start | bytes 1179656 | tf_op jit(solution)/shard_map/s2/ppermute | solution.py:221
  27.2 13.4 %collective-permute-start.19 = (bf16[12,128,128]{2,1,0:T(8,128)(2,1)S(1)}, bf16[12,128,128]{2,1,0:T(8,128)(2,1)S(1)}, u32[]{:S(2)}, u32[]{:S(2)}) collective-permute-start(bf16[12,128,128]{2,1,0:T(8,128)(2,1)S(1)} %slice.108), channel_id=1, source_target_pairs={{0,48},{1,193},{2,50},{3,195},{4,52},{5,197},{6,54},{7,199},{8,56}... | collective-permute-start | bytes 1179656 | tf_op jit(solution)/shard_map/s2/ppermute | solution.py:221
  31.1 12.6 %copy-start.3 = (bf16[24,128,128]{2,1,0:T(8,128)(2,1)}, bf16[24,128,128]{2,1,0:T(8,128)(2,1)S(1)}, u32[]{:S(2)}) copy-start(bf16[24,128,128]{2,1,0:T(8,128)(2,1)S(1)} %collective-permute-done.1) | copy-start | bytes 2359300
  31.1 21.5 %collective-permute-start.12 = (bf16[24,128,128]{2,1,0:T(8,128)(2,1)S(1)}, bf16[24,128,128]{2,1,0:T(8,128)(2,1)S(1)}, u32[]{:S(2)}, u32[]{:S(2)}) collective-permute-start(bf16[24,128,128]{2,1,0:T(8,128)(2,1)S(1)} %collective-permute-done.3), channel_id=1, source_target_pairs={{0,64},{1,17},{2,66},{3,19},{4,68},{5,21},{6,70},{7,23},{8,72},{9,... | collective-permute-start | bytes 2359304 | tf_op jit(solution)/shard_map/a1/ppermute | solution.py:221
  31.1 20.1 %collective-permute-start.14 = (bf16[24,128,128]{2,1,0:T(8,128)(2,1)S(1)}, bf16[24,128,128]{2,1,0:T(8,128)(2,1)S(1)}, u32[]{:S(2)}, u32[]{:S(2)}) collective-permute-start(bf16[24,128,128]{2,1,0:T(8,128)(2,1)S(1)} %collective-permute-done.4), channel_id=1, source_target_pairs={{0,192},{1,49},{2,194},{3,51},{4,196},{5,53},{6,198},{7,55},{8,200... | collective-permute-start | bytes 2359304 | tf_op jit(solution)/shard_map/a1/ppermute | solution.py:221
  34.9 13.4 %collective-permute-start.8 = (bf16[24,128,128]{2,1,0:T(8,128)(2,1)}, bf16[24,128,128]{2,1,0:T(8,128)(2,1)S(1)}, u32[]{:S(2)}, u32[]{:S(2)}) collective-permute-start(bf16[24,128,128]{2,1,0:T(8,128)(2,1)} %collective-permute-done.7), channel_id=1, source_target_pairs={{0,2},{1,15},{2,4},{3,1},{4,6},{5,3},{6,8},{7,5},{8,10},{9,7},{10,... | collective-permute-start | bytes 2359304 | tf_op jit(solution)/shard_map/z2/ppermute | solution.py:221
  40.8 13.9 %collective-permute-start.20 = (bf16[24,128,128]{2,1,0:T(8,128)(2,1)S(1)}, bf16[24,128,128]{2,1,0:T(8,128)(2,1)S(1)}, u32[]{:S(2)}, u32[]{:S(2)}) collective-permute-start(bf16[24,128,128]{2,1,0:T(8,128)(2,1)S(1)} %get-tuple-element.57), channel_id=1, source_target_pairs={{0,64},{1,17},{2,66},{3,19},{4,68},{5,21},{6,70},{7,23},{8,72},{9,... | collective-permute-start | bytes 2359304 | tf_op jit(solution)/shard_map/b/ppermute | solution.py:221
  40.9 14.0 %collective-permute-start.21 = (bf16[24,128,128]{2,1,0:T(8,128)(2,1)S(1)}, bf16[24,128,128]{2,1,0:T(8,128)(2,1)S(1)}, u32[]{:S(2)}, u32[]{:S(2)}) collective-permute-start(bf16[24,128,128]{2,1,0:T(8,128)(2,1)S(1)} %get-tuple-element.57), channel_id=1, source_target_pairs={{0,192},{1,49},{2,194},{3,51},{4,196},{5,53},{6,198},{7,55},{8,200... | collective-permute-start | bytes 2359304 | tf_op jit(solution)/shard_map/b/ppermute | solution.py:221
  48.3 11.9 %collective-permute-start.9 = (bf16[24,128,128]{2,1,0:T(8,128)(2,1)S(1)}, bf16[24,128,128]{2,1,0:T(8,128)(2,1)S(1)}, u32[]{:S(2)}, u32[]{:S(2)}) collective-permute-start(bf16[24,128,128]{2,1,0:T(8,128)(2,1)S(1)} %collective-permute-done.8), channel_id=1, source_target_pairs={{0,2},{1,15},{2,4},{3,1},{4,6},{5,3},{6,8},{7,5},{8,10},{9,7},{10,... | collective-permute-start | bytes 2359304 | tf_op jit(solution)/shard_map/z3/ppermute | solution.py:221
  51.3 3.5 %slice-start = ((bf16[24,128,128]{2,1,0:T(8,128)(2,1)}), bf16[12,128,128]{2,1,0:T(8,128)(2,1)S(1)}, s32[]{:S(2)}) async-start(bf16[24,128,128]{2,1,0:T(8,128)(2,1)} %copy-done.3), calls=%async_computation | async-start | bytes 786432 | tf_op jit(solution)/shard_map/gh/slice | solution.py:302
  51.4 15.5 %collective-permute-start.15 = (bf16[24,128,128]{2,1,0:T(8,128)(2,1)S(1)}, bf16[24,128,128]{2,1,0:T(8,128)(2,1)S(1)}, u32[]{:S(2)}, u32[]{:S(2)}) collective-permute-start(bf16[24,128,128]{2,1,0:T(8,128)(2,1)S(1)} %pad_maximum_fusion.5), channel_id=1, source_target_pairs={{0,192},{1,49},{2,194},{3,51},{4,196},{5,53},{6,198},{7,55},{8,200... | collective-permute-start | bytes 2359304 | tf_op jit(solution)/shard_map/ga/ppermute | solution.py:221
  52.8 15.9 %collective-permute-start.13 = (bf16[24,128,128]{2,1,0:T(8,128)(2,1)S(1)}, bf16[24,128,128]{2,1,0:T(8,128)(2,1)S(1)}, u32[]{:S(2)}, u32[]{:S(2)}) collective-permute-start(bf16[24,128,128]{2,1,0:T(8,128)(2,1)S(1)} %pad_maximum_fusion.4), channel_id=1, source_target_pairs={{0,64},{1,17},{2,66},{3,19},{4,68},{5,21},{6,70},{7,23},{8,72},{9,... | collective-permute-start | bytes 2359304 | tf_op jit(solution)/shard_map/ga/ppermute | solution.py:221
  54.8 18.8 %collective-permute-start.22 = (bf16[24,128,128]{2,1,0:T(8,128)(2,1)S(1)}, bf16[24,128,128]{2,1,0:T(8,128)(2,1)S(1)}, u32[]{:S(2)}, u32[]{:S(2)}) collective-permute-start(bf16[24,128,128]{2,1,0:T(8,128)(2,1)S(1)} %pad_maximum_fusion.8), channel_id=1, source_target_pairs={{0,64},{1,17},{2,66},{3,19},{4,68},{5,21},{6,70},{7,23},{8,72},{9,... | collective-permute-start | bytes 2359304 | tf_op jit(solution)/shard_map/gh/ppermute | solution.py:221
  60.5 17.3 %collective-permute-start.11 = (bf16[36,128,128]{2,1,0:T(8,128)(2,1)S(1)}, bf16[36,128,128]{2,1,0:T(8,128)(2,1)S(1)}, u32[]{:S(2)}, u32[]{:S(2)}) collective-permute-start(bf16[36,128,128]{2,1,0:T(8,128)(2,1)S(1)} %pad_maximum_fusion.1), channel_id=1, source_target_pairs={{0,1},{1,0},{2,3},{3,2},{4,5},{5,4},{6,7},{7,6},{8,9},{9,8},{10,11... | collective-permute-start | bytes 3538952 | tf_op jit(solution)/shard_map/w4/ppermute | solution.py:221
  66.5 11.2 %collective-permute-start.23 = (bf16[24,128,128]{2,1,0:T(8,128)(2,1)S(1)}, bf16[24,128,128]{2,1,0:T(8,128)(2,1)S(1)}, u32[]{:S(2)}, u32[]{:S(2)}) collective-permute-start(bf16[24,128,128]{2,1,0:T(8,128)(2,1)S(1)} %pad_maximum_fusion.9), channel_id=1, source_target_pairs={{0,192},{1,49},{2,194},{3,51},{4,196},{5,53},{6,198},{7,55},{8,200... | collective-permute-start | bytes 2359304 | tf_op jit(solution)/shard_map/gh/ppermute | solution.py:221
  66.9 10.9 %collective-permute-start.10 = (bf16[12,128,128]{2,1,0:T(8,128)(2,1)S(1)}, bf16[12,128,128]{2,1,0:T(8,128)(2,1)S(1)}, u32[]{:S(2)}, u32[]{:S(2)}) collective-permute-start(bf16[12,128,128]{2,1,0:T(8,128)(2,1)S(1)} %get-tuple-element.55), channel_id=1, source_target_pairs={{0,2},{1,15},{2,4},{3,1},{4,6},{5,3},{6,8},{7,5},{8,10},{9,7},{10,... | collective-permute-start | bytes 1179656 | tf_op jit(solution)/shard_map/z4/ppermute | solution.py:221
  68.9 15.7 %collective-permute-start.16 = (bf16[24,128,128]{2,1,0:T(8,128)(2,1)S(1)}, bf16[24,128,128]{2,1,0:T(8,128)(2,1)S(1)}, u32[]{:S(2)}, u32[]{:S(2)}) collective-permute-start(bf16[24,128,128]{2,1,0:T(8,128)(2,1)S(1)} %pad_maximum_fusion.6), channel_id=1, source_target_pairs={{0,64},{1,17},{2,66},{3,19},{4,68},{5,21},{6,70},{7,23},{8,72},{9,... | collective-permute-start | bytes 2359304 | tf_op jit(solution)/shard_map/a2/ppermute | solution.py:221
  69.2 8.8 %copy-start = (bf16[1,32,128,128]{3,2,1,0:T(8,128)(2,1)S(1)}, bf16[1,32,128,128]{3,2,1,0:T(8,128)(2,1)}, u32[]{:S(2)}) copy-start(bf16[1,32,128,128]{3,2,1,0:T(8,128)(2,1)} %param.8) | copy-start | bytes 3145732
  69.2 8.8 %copy-start.1 = (s32[3,272]{1,0:T(4,128)S(1)}, s32[3,272]{1,0:T(4,128)}, u32[]{:S(2)}) copy-start(s32[3,272]{1,0:T(4,128)} %get-tuple-element.31.entries) | copy-start | bytes 9796
  69.2 8.8 %copy-start.2 = (s32[3]{0:T(128)S(1)}, s32[3]{0:T(128)}, u32[]{:S(2)}) copy-start(s32[3]{0:T(128)} %get-tuple-element.30.groups) | copy-start | bytes 40
  73.6 12.5 %collective-permute-start.17 = (bf16[24,128,128]{2,1,0:T(8,128)(2,1)S(1)}, bf16[24,128,128]{2,1,0:T(8,128)(2,1)S(1)}, u32[]{:S(2)}, u32[]{:S(2)}) collective-permute-start(bf16[24,128,128]{2,1,0:T(8,128)(2,1)S(1)} %pad_maximum_fusion.7), channel_id=1, source_target_pairs={{0,192},{1,49},{2,194},{3,51},{4,196},{5,53},{6,198},{7,55},{8,200... | collective-permute-start | bytes 2359304 | tf_op jit(solution)/shard_map/a2/ppermute | solution.py:221
  83.9 4.2 %collective-permute-start.24 = (f32[11,128,128]{2,1,0:T(8,128)S(1)}, f32[11,128,128]{2,1,0:T(8,128)S(1)}, u32[]{:S(2)}, u32[]{:S(2)}) collective-permute-start(f32[11,128,128]{2,1,0:T(8,128)S(1)} %get-tuple-element.44), channel_id=1, source_target_pairs={{0,1},{1,0},{2,3},{3,2},{4,5},{5,4},{6,7},{7,6},{8,9},{9,8},{10,11... | collective-permute-start | bytes 2162696 | tf_op jit(solution)/shard_map/w3/ppermute | solution.py:221
  84.0 4.2 %collective-permute-start.25 = (f32[11,128,128]{2,1,0:T(8,128)S(1)}, f32[11,128,128]{2,1,0:T(8,128)S(1)}, u32[]{:S(2)}, u32[]{:S(2)}) collective-permute-start(f32[11,128,128]{2,1,0:T(8,128)S(1)} %get-tuple-element.45), channel_id=1, source_target_pairs={{0,1},{1,0},{2,3},{3,2},{4,5},{5,4},{6,7},{7,6},{8,9},{9,8},{10,11... | collective-permute-start | bytes 2162696 | tf_op jit(solution)/shard_map/w3/ppermute | solution.py:221
  84.5 3.6 %collective-permute-start.26 = (f32[10,128,128]{2,1,0:T(8,128)S(1)}, f32[10,128,128]{2,1,0:T(8,128)S(1)}, u32[]{:S(2)}, u32[]{:S(2)}) collective-permute-start(f32[10,128,128]{2,1,0:T(8,128)S(1)} %get-tuple-element.46), channel_id=1, source_target_pairs={{0,1},{1,0},{2,3},{3,2},{4,5},{5,4},{6,7},{7,6},{8,9},{9,8},{10,11... | collective-permute-start | bytes 1966088 | tf_op jit(solution)/shard_map/w3/ppermute | solution.py:221

commit v2 on v1

--- a/solution.py
+++ b/solution.py
@@ -288,8 +288,9 @@
     with scope("w4"):
         swapped = sibling(join(z1[half:], z2[half:], z3[half:]))
     left = join(pair[:half], z1[:half], z2[:half], z3[:half], z4, swapped)
+    near1, z1 = order(((r1, l1), z1))
     with scope("s2"):
-        s2 = first(r1[:shard], l1[shard:])
+        s2 = first(near1[0][:shard], near1[1][shard:])
     t, ar, al, entries, groups = order((t, r1, l1, entries, groups))
     with scope("a1"):
         a1 = second(ar, al)

time: 90.8 us -> 89.6 us (0.987)
  waiting for transfers between devices: 22.6 us -> 20.7 us
  starting transfers between devices: 39.1 us -> 40.1 us
    ppermute x27, waiting for transfers between devices: 22.6 us -> 20.7 us  [move(): return lax.ppermute(blocks, ('row', 'col'), pairs)]
    ppermute x27, starting transfers between devices: 39.1 us -> 40.1 us  [move(): return lax.ppermute(blocks, ('row', 'col'), pairs)]
  transfers between devices with their start and end apart: 27 -> 27, of which waited for: 8 -> 7; matrix products, arithmetic and copies ran while one was open for 14% -> 14% of each run, Pallas kernels for 12% -> 12%
where the time goes in v2:
time: 89.6 us; the launch traced here: 89.7 us
  starting transfers between devices  40.1 us (45%)
  waiting for transfers between devices  20.7 us (23%)
  Pallas kernels  15.7 us (18%)
  local copies, waits for them, and re-layouts  8.66 us (10%)
  other arithmetic  3.98 us (4%)
    ppermute x27, starting transfers between devices, move(): return lax.ppermute(blocks, ('row', 'col'), pairs)  40.1 us
    ppermute x27, waiting for transfers between devices, move(): return lax.ppermute(blocks, ('row', 'col'), pairs)  20.7 us
    pallas_call x3, Pallas kernels, add_products(): pl.pallas_call(functools.partial(products_kernel, stage), out_shape=outs,...  8.38 us
    pallas_call x1, Pallas kernels, sort_lists(): pl.pallas_call(functools.partial(sort_kernel, left_shard, shard, depth, p...  5.06 us
    unnamed x28, local copies, waits for them, and re-layouts  4.42 us
    concatenate x11, other arithmetic, join(): return jnp.concatenate(pieces)  3.4 us
    pallas_call x1, Pallas kernels, select_panels(): pl.pallas_call(select_kernel, out_shape=[jax.ShapeDtypeStruct((n, *block)...  2.28 us
  transfers between devices with their start and end apart: 27, of which 7 were waited for; matrix products, arithmetic and copies ran while one was open for 14% of the time, Pallas kernels for 12%

profile of v2, /device:TPU:1, one launch (start us, length us, event | category | flops | bytes accessed | tf_op | source)
XLA Modules:
  0.0 89.7 jit_solution(7167643574176576316)
XLA Ops:
  0.0 2.3 %select_panels.1 = (bf16[12,128,128]{2,1,0:T(8,128)(2,1)}, bf16[12,128,128]{2,1,0:T(8,128)(2,1)}, bf16[12,128,128]{2,1,0:T(8,128)(2,1)}) custom-call(s32[1]{0:T(128)} %bitcast.core, bf16[2,12,128,128]{3,2,1,0:T(8,128)(2,1)} %bitcast.10, bf16[2,6,128,128]{3,2,1,0:T(8,128)(2,1)} %bitcast.11), custom_call_target="tpu_custom_call" | custom-call | bytes 1048576 | tf_op jit(solution)/shard_map/select_panels/pallas_call | solution.py:130
  2.3 3.3 %collective-permute-start = (bf16[12,128,128]{2,1,0:T(8,128)(2,1)}, bf16[12,128,128]{2,1,0:T(8,128)(2,1)S(1)}, u32[]{:S(2)}, u32[]{:S(2)}) collective-permute-start(bf16[12,128,128]{2,1,0:T(8,128)(2,1)} %get-tuple-element.29), channel_id=1, source_target_pairs={{0,1},{1,0},{2,3},{3,2},{4,5},{5,4},{6,7},{7,6},{8,9},{9,8},{10,11... | collective-permute-start | bytes 1179656 | tf_op jit(solution)/shard_map/w0/ppermute | solution.py:221
  5.6 0.1 collective-permute-start.6
  5.7 0.7 copy.7
  6.4 0.7 pad_add_fusion.own
  7.1 0.4 collective-permute-start.5
  7.5 1.0 %fusion.3 = (bf16[6,128,128]{2,1,0:T(8,128)(2,1)S(1)}, bf16[6,128,128]{2,1,0:T(8,128)(2,1)S(1)}) fusion(bf16[12,128,128]{2,1,0:T(8,128)(2,1)} %get-tuple-element.34), kind=kLoop, calls=%fused_computation.38 | loop fusion | bytes 786432 | tf_op jit(solution)/shard_map/slice | solution.py:271
  8.6 1.1 %pad_maximum_fusion.2 = bf16[24,128,128]{2,1,0:T(8,128)(2,1)S(1)} fusion(bf16[12,128,128]{2,1,0:T(8,128)(2,1)S(1)} %collective-permute-done, bf16[12,128,128]{2,1,0:T(8,128)(2,1)} %get-tuple-element.28), kind=kLoop, calls=%fused_computation.2 | loop fusion | flops 393216 | bytes 1572864 | tf_op jit(solution)/shard_map/concatenate | solution.py:247
  9.6 0.1 collective-permute-start.3
  9.7 2.7 %collective-permute-start.4 = (bf16[24,128,128]{2,1,0:T(8,128)(2,1)S(1)}, bf16[24,128,128]{2,1,0:T(8,128)(2,1)S(1)}, u32[]{:S(2)}, u32[]{:S(2)}) collective-permute-start(bf16[24,128,128]{2,1,0:T(8,128)(2,1)S(1)} %pad_maximum_fusion.2), channel_id=1, source_target_pairs={{0,48},{1,193},{2,50},{3,195},{4,52},{5,197},{6,54},{7,199},{8,56}... | collective-permute-start | bytes 2359304 | tf_op jit(solution)/shard_map/s1/ppermute | solution.py:221
  12.4 1.0 %pad_maximum_fusion.3 = bf16[24,128,128]{2,1,0:T(8,128)(2,1)} fusion(bf16[6,128,128]{2,1,0:T(8,128)(2,1)S(1)} %get-tuple-element.65, bf16[6,128,128]{2,1,0:T(8,128)(2,1)S(1)} %get-tuple-element.63, bf16[6,128,128]{2,1,0:T(8,128)(2,1)S(1)} %get-tuple-element.64, bf16[6,128,128]{2,1,0:T(8,128)(2,1)S(1)} %get-tuple-element.62), kind=kLoop, calls=%fused_computation.3 | loop fusion | flops 1179648 | bytes 1572864 | tf_op jit(solution)/shard_map/concatenate | solution.py:247
  13.4 4.0 %collective-permute-start.7 = (bf16[24,128,128]{2,1,0:T(8,128)(2,1)}, bf16[24,128,128]{2,1,0:T(8,128)(2,1)}, u32[]{:S(2)}, u32[]{:S(2)}) collective-permute-start(bf16[24,128,128]{2,1,0:T(8,128)(2,1)} %pad_maximum_fusion.3), channel_id=1, source_target_pairs={{0,2},{1,15},{2,4},{3,1},{4,6},{5,3},{6,8},{7,5},{8,10},{9,7},{10,... | collective-permute-start | bytes 2359304 | tf_op jit(solution)/shard_map/z1/ppermute | solution.py:221
  17.4 1.2 %collective-permute-start.1 = (bf16[24,128,128]{2,1,0:T(8,128)(2,1)S(1)}, bf16[24,128,128]{2,1,0:T(8,128)(2,1)S(1)}, u32[]{:S(2)}, u32[]{:S(2)}) collective-permute-start(bf16[24,128,128]{2,1,0:T(8,128)(2,1)S(1)} %pad_maximum_fusion.2), channel_id=1, source_target_pairs={{0,64},{1,17},{2,66},{3,19},{4,68},{5,21},{6,70},{7,23},{8,72},{9,... | collective-permute-start | bytes 2359304 | tf_op jit(solution)/shard_map/t/ppermute | solution.py:221
  18.6 1.5 %collective-permute-start.2 = (bf16[24,128,128]{2,1,0:T(8,128)(2,1)S(1)}, bf16[24,128,128]{2,1,0:T(8,128)(2,1)}, u32[]{:S(2)}, u32[]{:S(2)}) collective-permute-start(bf16[24,128,128]{2,1,0:T(8,128)(2,1)S(1)} %pad_maximum_fusion.2), channel_id=1, source_target_pairs={{0,192},{1,49},{2,194},{3,51},{4,196},{5,53},{6,198},{7,55},{8,200... | collective-permute-start | bytes 2359304 | tf_op jit(solution)/shard_map/t/ppermute | solution.py:221
  20.1 0.6 pad_add_fusion.1.here
  20.7 5.1 %sort_lists.1 = (s32[3,272]{1,0:T(4,128)}, s32[3]{0:T(128)}) custom-call(s32[4]{0:T(128)} %pad_add_fusion.1.here, s32[64]{0:T(128)} %constant.51.clone.right_at, s32[770]{0:T(1024)} %copy-done.4, s32[770]{0:T(1024)} %copy-done.5), custom_call_target="tpu_custom_call" | custom-call | bytes 8388608 | tf_op jit(solution)/shard_map/sort_lists/pallas_call | solution.py:93
  25.8 1.0 %slice_dynamic-update-slice_fusion.2 = bf16[96,128,128]{2,1,0:T(8,128)(2,1)S(1)} fusion(bf16[24,128,128]{2,1,0:T(8,128)(2,1)} %pad_maximum_fusion.3), kind=kLoop, calls=%fused_computation.12 | loop fusion | bytes 786432
  26.9 0.1 collective-permute-start.18
  27.0 2.7 %collective-permute-start.19 = (bf16[12,128,128]{2,1,0:T(8,128)(2,1)S(1)}, bf16[12,128,128]{2,1,0:T(8,128)(2,1)S(1)}, u32[]{:S(2)}, u32[]{:S(2)}) collective-permute-start(bf16[12,128,128]{2,1,0:T(8,128)(2,1)S(1)} %slice.96), channel_id=1, source_target_pairs={{0,48},{1,193},{2,50},{3,195},{4,52},{5,197},{6,54},{7,199},{8,56}... | collective-permute-start | bytes 1179656 | tf_op jit(solution)/shard_map/s2/ppermute | solution.py:221
  29.7 1.0 %collective-permute-done.1 = bf16[24,128,128]{2,1,0:T(8,128)(2,1)S(1)} collective-permute-done((bf16[24,128,128]{2,1,0:T(8,128)(2,1)S(1)}, bf16[24,128,128]{2,1,0:T(8,128)(2,1)S(1)}, u32[]{:S(2)}, u32[]{:S(2)}) %collective-permute-start.1) | collective-permute-done | bytes 786464 | tf_op jit(solution)/shard_map/t/ppermute | solution.py:221
  30.8 3.0 %collective-permute-start.14 = (bf16[24,128,128]{2,1,0:T(8,128)(2,1)S(1)}, bf16[24,128,128]{2,1,0:T(8,128)(2,1)S(1)}, u32[]{:S(2)}, u32[]{:S(2)}) collective-permute-start(bf16[24,128,128]{2,1,0:T(8,128)(2,1)S(1)} %collective-permute-done.4), channel_id=1, source_target_pairs={{0,192},{1,49},{2,194},{3,51},{4,196},{5,53},{6,198},{7,55},{8,200... | collective-permute-start | bytes 2359304 | tf_op jit(solution)/shard_map/a1/ppermute | solution.py:221
  33.8 1.0 %slice.99 = bf16[12,128,128]{2,1,0:T(8,128)(2,1)S(1)} slice(bf16[24,128,128]{2,1,0:T(8,128)(2,1)} %collective-permute-done.2), slice={[12:24], [0:128], [0:128]} | slice | bytes 786432 | tf_op jit(solution)/shard_map/gh/slice | solution.py:303
  34.8 4.2 %collective-permute-start.8 = (bf16[24,128,128]{2,1,0:T(8,128)(2,1)}, bf16[24,128,128]{2,1,0:T(8,128)(2,1)S(1)}, u32[]{:S(2)}, u32[]{:S(2)}) collective-permute-start(bf16[24,128,128]{2,1,0:T(8,128)(2,1)} %collective-permute-done.7), channel_id=1, source_target_pairs={{0,2},{1,15},{2,4},{3,1},{4,6},{5,3},{6,8},{7,5},{8,10},{9,7},{10,... | collective-permute-start | bytes 2359304 | tf_op jit(solution)/shard_map/z2/ppermute | solution.py:221
  39.1 1.2 %fusion = (bf16[12,128,128]{2,1,0:T(8,128)(2,1)S(1)}, bf16[96,128,128]{2,1,0:T(8,128)(2,1)S(1)}) fusion(bf16[24,128,128]{2,1,0:T(8,128)(2,1)} %collective-permute-done.7, bf16[96,128,128]{2,1,0:T(8,128)(2,1)S(1)} %slice_dynamic-update-slice_fusion.2), kind=kLoop, calls=%fused_computation.35 | loop fusion | bytes 1572864 | tf_op jit(solution)/shard_map/w4/slice | solution.py:289
  40.3 0.1 constant_dynamic-update-slice_fusion.18
  40.4 0.1 constant_dynamic-update-slice_fusion.17
  40.5 0.2 constant_dynamic-update-slice_fusion.16
  40.8 0.2 constant_dynamic-update-slice_fusion.15
  41.0 0.1 collective-permute-start.20
  41.1 2.7 %collective-permute-start.21 = (bf16[24,128,128]{2,1,0:T(8,128)(2,1)S(1)}, bf16[24,128,128]{2,1,0:T(8,128)(2,1)S(1)}, u32[]{:S(2)}, u32[]{:S(2)}) collective-permute-start(bf16[24,128,128]{2,1,0:T(8,128)(2,1)S(1)} %get-tuple-element.59), channel_id=1, source_target_pairs={{0,192},{1,49},{2,194},{3,51},{4,196},{5,53},{6,198},{7,55},{8,200... | collective-permute-start | bytes 2359304 | tf_op jit(solution)/shard_map/b/ppermute | solution.py:221
  43.7 0.1 constant_dynamic-update-slice_fusion.14
  43.9 1.3 %constant_dynamic-update-slice_fusion.13 = bf16[192,128,128]{2,1,0:T(8,128)(2,1)S(1)} fusion(bf16[192,128,128]{2,1,0:T(8,128)(2,1)S(1)} %constant_dynamic-update-slice_fusion.14, bf16[24,128,128]{2,1,0:T(8,128)(2,1)} %collective-permute-done.2), kind=kLoop, calls=%fused_computation.26 | loop fusion | bytes 1572864
  45.1 3.2 %collective-permute-done.8 = bf16[24,128,128]{2,1,0:T(8,128)(2,1)S(1)} collective-permute-done((bf16[24,128,128]{2,1,0:T(8,128)(2,1)}, bf16[24,128,128]{2,1,0:T(8,128)(2,1)S(1)}, u32[]{:S(2)}, u32[]{:S(2)}) %collective-permute-start.8) | collective-permute-done | bytes 786464 | tf_op jit(solution)/shard_map/z2/ppermute | solution.py:221
  48.3 3.3 %collective-permute-start.9 = (bf16[24,128,128]{2,1,0:T(8,128)(2,1)S(1)}, bf16[24,128,128]{2,1,0:T(8,128)(2,1)S(1)}, u32[]{:S(2)}, u32[]{:S(2)}) collective-permute-start(bf16[24,128,128]{2,1,0:T(8,128)(2,1)S(1)} %collective-permute-done.8), channel_id=1, source_target_pairs={{0,2},{1,15},{2,4},{3,1},{4,6},{5,3},{6,8},{7,5},{8,10},{9,7},{10,... | collective-permute-start | bytes 2359304 | tf_op jit(solution)/shard_map/z3/ppermute | solution.py:221
  51.7 0.1 collective-permute-start.13
  51.9 2.7 %collective-permute-start.15 = (bf16[24,128,128]{2,1,0:T(8,128)(2,1)S(1)}, bf16[24,128,128]{2,1,0:T(8,128)(2,1)S(1)}, u32[]{:S(2)}, u32[]{:S(2)}) collective-permute-start(bf16[24,128,128]{2,1,0:T(8,128)(2,1)S(1)} %pad_maximum_fusion.5), channel_id=1, source_target_pairs={{0,192},{1,49},{2,194},{3,51},{4,196},{5,53},{6,198},{7,55},{8,200... | collective-permute-start | bytes 2359304 | tf_op jit(solution)/shard_map/ga/ppermute | solution.py:221
  54.7 0.1 constant_dynamic-update-slice_fusion.12
  54.8 0.1 constant_dynamic-update-slice_fusion.11.right
  54.9 0.1 fusion.1
  55.1 0.1 collective-permute-start.22
  55.3 5.3 %collective-permute-done.9 = bf16[24,128,128]{2,1,0:T(8,128)(2,1)S(1)} collective-permute-done((bf16[24,128,128]{2,1,0:T(8,128)(2,1)S(1)}, bf16[24,128,128]{2,1,0:T(8,128)(2,1)S(1)}, u32[]{:S(2)}, u32[]{:S(2)}) %collective-permute-start.9) | collective-permute-done | bytes 786464 | tf_op jit(solution)/shard_map/z3/ppermute | solution.py:221
  60.5 0.2 fusion.2
  60.7 0.1 pad_maximum_fusion.1
  60.8 4.1 %collective-permute-start.11 = (bf16[36,128,128]{2,1,0:T(8,128)(2,1)S(1)}, bf16[36,128,128]{2,1,0:T(8,128)(2,1)S(1)}, u32[]{:S(2)}, u32[]{:S(2)}) collective-permute-start(bf16[36,128,128]{2,1,0:T(8,128)(2,1)S(1)} %pad_maximum_fusion.1), channel_id=1, source_target_pairs={{0,1},{1,0},{2,3},{3,2},{4,5},{5,4},{6,7},{7,6},{8,9},{9,8},{10,11... | collective-permute-start | bytes 3538952 | tf_op jit(solution)/shard_map/w4/ppermute | solution.py:221
  65.0 1.5 %collective-permute-start.23 = (bf16[24,128,128]{2,1,0:T(8,128)(2,1)S(1)}, bf16[24,128,128]{2,1,0:T(8,128)(2,1)S(1)}, u32[]{:S(2)}, u32[]{:S(2)}) collective-permute-start(bf16[24,128,128]{2,1,0:T(8,128)(2,1)S(1)} %pad_maximum_fusion.9), channel_id=1, source_target_pairs={{0,192},{1,49},{2,194},{3,51},{4,196},{5,53},{6,198},{7,55},{8,200... | collective-permute-start | bytes 2359304 | tf_op jit(solution)/shard_map/gh/ppermute | solution.py:221
  66.6 0.1 constant_dynamic-update-slice_fusion.9
  66.7 0.6 collective-permute-start.10
  67.5 0.1 collective-permute-start.16
  67.6 0.1 constant_dynamic-update-slice_fusion.8
  67.8 0.1 constant_dynamic-update-slice_fusion.7
  68.0 4.6 %collective-permute-done.22 = bf16[24,128,128]{2,1,0:T(8,128)(2,1)S(1)} collective-permute-done((bf16[24,128,128]{2,1,0:T(8,128)(2,1)S(1)}, bf16[24,128,128]{2,1,0:T(8,128)(2,1)S(1)}, u32[]{:S(2)}, u32[]{:S(2)}) %collective-permute-start.22) | collective-permute-done | bytes 786464 | tf_op jit(solution)/shard_map/gh/ppermute | solution.py:221
  72.6 0.1 constant_dynamic-update-slice_fusion.6
  72.7 3.5 %collective-permute-done.23 = bf16[24,128,128]{2,1,0:T(8,128)(2,1)S(1)} collective-permute-done((bf16[24,128,128]{2,1,0:T(8,128)(2,1)S(1)}, bf16[24,128,128]{2,1,0:T(8,128)(2,1)S(1)}, u32[]{:S(2)}, u32[]{:S(2)}) %collective-permute-start.23) | collective-permute-done | bytes 786464 | tf_op jit(solution)/shard_map/gh/ppermute | solution.py:221
  76.2 0.1 constant_dynamic-update-slice_fusion.5.right
  76.4 0.2 constant_dynamic-update-slice_fusion.left
  76.6 2.7 %products.3.refs_0_ = f32[65,128,128]{2,1,0:T(8,128)S(1)} custom-call(s32[3]{0:T(128)S(1)} %copy-done.2, s32[3,272]{1,0:T(4,128)S(1)} %copy-done.1, bf16[96,128,128]{2,1,0:T(8,128)(2,1)S(1)} %constant_dynamic-update-slice_fusion.left, bf16[192,128,128]{2,1,0:T(8,128)(2,1)S(1)} %constant_dynamic-update-slice_fusion.11.right, bf16[32,128,128]{2,1,0:T(8,128)(2,1)S(1)} %bitcast.9), custom_call_target="tpu_custom_call" | custom-call | flops 1048576 | bytes 1048576 | tf_op jit(solution)/shard_map/products/pallas_call | solution.py:199
  79.3 2.8 %products.4 = (f32[32,128,128]{2,1,0:T(8,128)S(1)}, f32[11,128,128]{2,1,0:T(8,128)S(1)}, f32[11,128,128]{2,1,0:T(8,128)S(1)}, f32[10,128,128]{2,1,0:T(8,128)S(1)}) custom-call(s32[3]{0:T(128)S(1)} %copy-done.2, s32[3,272]{1,0:T(4,128)S(1)} %copy-done.1, bf16[96,128,128]{2,1,0:T(8,128)(2,1)S(1)} %constant_dynamic-update-slice_fusion.left, ...), custom_call_target="tpu_custom_call" | custom-call | flops 1048576 | bytes 1048576 | tf_op jit(solution)/shard_map/products/pallas_call | solution.py:199
  82.1 1.0 %collective-permute-start.24 = (f32[11,128,128]{2,1,0:T(8,128)S(1)}, f32[11,128,128]{2,1,0:T(8,128)S(1)}, u32[]{:S(2)}, u32[]{:S(2)}) collective-permute-start(f32[11,128,128]{2,1,0:T(8,128)S(1)} %get-tuple-element.48), channel_id=1, source_target_pairs={{0,1},{1,0},{2,3},{3,2},{4,5},{5,4},{6,7},{7,6},{8,9},{9,8},{10,11... | collective-permute-start | bytes 2162696 | tf_op jit(solution)/shard_map/w3/ppermute | solution.py:221
  83.0 0.1 collective-permute-start.25
  83.1 0.4 collective-permute-start.26
  83.6 1.1 %collective-permute-done.17 = bf16[24,128,128]{2,1,0:T(8,128)(2,1)S(1)} collective-permute-done((bf16[24,128,128]{2,1,0:T(8,128)(2,1)S(1)}, bf16[24,128,128]{2,1,0:T(8,128)(2,1)S(1)}, u32[]{:S(2)}, u32[]{:S(2)}) %collective-permute-start.17) | collective-permute-done | bytes 786464 | tf_op jit(solution)/shard_map/a2/ppermute | solution.py:221
  84.6 0.1 pad_maximum_fusion.right
  84.8 2.1 %collective-permute-done.26.refs_3_ = f32[10,128,128]{2,1,0:T(8,128)S(1)} collective-permute-done((f32[10,128,128]{2,1,0:T(8,128)S(1)}, f32[10,128,128]{2,1,0:T(8,128)S(1)}, u32[]{:S(2)}, u32[]{:S(2)}) %collective-permute-start.26) | collective-permute-done | bytes 655392 | tf_op jit(solution)/shard_map/w3/ppermute | solution.py:221
  86.8 2.9 %products.5 = bf16[32,128,128]{2,1,0:T(8,128)(2,1)} custom-call(s32[3]{0:T(128)S(1)} %copy-done.2, s32[3,272]{1,0:T(4,128)S(1)} %copy-done.1, bf16[96,128,128]{2,1,0:T(8,128)(2,1)S(1)} %constant_dynamic-update-slice_fusion.left, bf16[48,128,128]{2,1,0:T(8,128)(2,1)S(1)} %pad_maximum_fusion.right, f32[32,128,128]{2,1,0:T(8,128)S(1)} %get-tuple-element.47.refs_0_, ...), custom_call_target="tpu_custom_call" | custom-call | flops 1048576 | bytes 1048576 | tf_op jit(solution)/shard_map/products/pallas_call | solution.py:199
  (59 shorter events, 1.1 us)
Async XLA Ops:
  2.3 6.3 %collective-permute-start = (bf16[12,128,128]{2,1,0:T(8,128)(2,1)}, bf16[12,128,128]{2,1,0:T(8,128)(2,1)S(1)}, u32[]{:S(2)}, u32[]{:S(2)}) collective-permute-start(bf16[12,128,128]{2,1,0:T(8,128)(2,1)} %get-tuple-element.29), channel_id=1, source_target_pairs={{0,1},{1,0},{2,3},{3,2},{4,5},{5,4},{6,7},{7,6},{8,9},{9,8},{10,11... | collective-permute-start | bytes 1179656 | tf_op jit(solution)/shard_map/w0/ppermute | solution.py:221
  5.6 6.8 %collective-permute-start.6 = (bf16[12,128,128]{2,1,0:T(8,128)(2,1)}, bf16[12,128,128]{2,1,0:T(8,128)(2,1)S(1)}, u32[]{:S(2)}, u32[]{:S(2)}) collective-permute-start(bf16[12,128,128]{2,1,0:T(8,128)(2,1)} %get-tuple-element.34), channel_id=1, source_target_pairs={{0,1},{1,0},{2,3},{3,2},{4,5},{5,4},{6,7},{7,6},{8,9},{9,8},{10,11... | collective-permute-start | bytes 1179656 | tf_op jit(solution)/shard_map/w1/ppermute | solution.py:221
  7.1 13.6 %copy-start.4 = (s32[770]{0:T(1024)}, s32[770]{0:T(1024)S(1)}, u32[]{:S(2)}) copy-start(s32[770]{0:T(1024)S(1)} %pad_add_fusion.own) | copy-start | bytes 9244
  7.1 11.5 %collective-permute-start.5 = (s32[770]{0:T(1024)S(1)}, s32[770]{0:T(1024)S(1)}, u32[]{:S(2)}, u32[]{:S(2)}) collective-permute-start(s32[770]{0:T(1024)S(1)} %pad_add_fusion.own), channel_id=1, source_target_pairs={{0,1},{1,0},{2,3},{3,2},{4,5},{5,4},{6,7},{7,6},{8,9},{9,8},{10,11... | collective-permute-start | bytes 9248 | tf_op jit(solution)/shard_map/w2/ppermute | solution.py:221
  9.6 17.2 %collective-permute-start.3 = (bf16[24,128,128]{2,1,0:T(8,128)(2,1)S(1)}, bf16[24,128,128]{2,1,0:T(8,128)(2,1)S(1)}, u32[]{:S(2)}, u32[]{:S(2)}) collective-permute-start(bf16[24,128,128]{2,1,0:T(8,128)(2,1)S(1)} %pad_maximum_fusion.2), channel_id=1, source_target_pairs={{0,16},{1,65},{2,18},{3,67},{4,20},{5,69},{6,22},{7,71},{8,24},{9,... | collective-permute-start | bytes 2359304 | tf_op jit(solution)/shard_map/s1/ppermute | solution.py:221
  9.7 17.1 %collective-permute-start.4 = (bf16[24,128,128]{2,1,0:T(8,128)(2,1)S(1)}, bf16[24,128,128]{2,1,0:T(8,128)(2,1)S(1)}, u32[]{:S(2)}, u32[]{:S(2)}) collective-permute-start(bf16[24,128,128]{2,1,0:T(8,128)(2,1)S(1)} %pad_maximum_fusion.2), channel_id=1, source_target_pairs={{0,48},{1,193},{2,50},{3,195},{4,52},{5,197},{6,54},{7,199},{8,56}... | collective-permute-start | bytes 2359304 | tf_op jit(solution)/shard_map/s1/ppermute | solution.py:221
  13.4 13.4 %collective-permute-start.7 = (bf16[24,128,128]{2,1,0:T(8,128)(2,1)}, bf16[24,128,128]{2,1,0:T(8,128)(2,1)}, u32[]{:S(2)}, u32[]{:S(2)}) collective-permute-start(bf16[24,128,128]{2,1,0:T(8,128)(2,1)} %pad_maximum_fusion.3), channel_id=1, source_target_pairs={{0,2},{1,15},{2,4},{3,1},{4,6},{5,3},{6,8},{7,5},{8,10},{9,7},{10,... | collective-permute-start | bytes 2359304 | tf_op jit(solution)/shard_map/z1/ppermute | solution.py:221
  17.4 13.4 %collective-permute-start.1 = (bf16[24,128,128]{2,1,0:T(8,128)(2,1)S(1)}, bf16[24,128,128]{2,1,0:T(8,128)(2,1)S(1)}, u32[]{:S(2)}, u32[]{:S(2)}) collective-permute-start(bf16[24,128,128]{2,1,0:T(8,128)(2,1)S(1)} %pad_maximum_fusion.2), channel_id=1, source_target_pairs={{0,64},{1,17},{2,66},{3,19},{4,68},{5,21},{6,70},{7,23},{8,72},{9,... | collective-permute-start | bytes 2359304 | tf_op jit(solution)/shard_map/t/ppermute | solution.py:221
  18.6 2.1 %copy-start.5 = (s32[770]{0:T(1024)}, s32[770]{0:T(1024)S(1)}, u32[]{:S(2)}) copy-start(s32[770]{0:T(1024)S(1)} %collective-permute-done.5.got) | copy-start | bytes 9244
  18.6 12.1 %collective-permute-start.2 = (bf16[24,128,128]{2,1,0:T(8,128)(2,1)S(1)}, bf16[24,128,128]{2,1,0:T(8,128)(2,1)}, u32[]{:S(2)}, u32[]{:S(2)}) collective-permute-start(bf16[24,128,128]{2,1,0:T(8,128)(2,1)S(1)} %pad_maximum_fusion.2), channel_id=1, source_target_pairs={{0,192},{1,49},{2,194},{3,51},{4,196},{5,53},{6,198},{7,55},{8,200... | collective-permute-start | bytes 2359304 | tf_op jit(solution)/shard_map/t/ppermute | solution.py:221
  26.9 13.7 %collective-permute-start.18 = (bf16[12,128,128]{2,1,0:T(8,128)(2,1)S(1)}, bf16[12,128,128]{2,1,0:T(8,128)(2,1)S(1)}, u32[]{:S(2)}, u32[]{:S(2)}) collective-permute-start(bf16[12,128,128]{2,1,0:T(8,128)(2,1)S(1)} %slice.95), channel_id=1, source_target_pairs={{0,16},{1,65},{2,18},{3,67},{4,20},{5,69},{6,22},{7,71},{8,24},{9,... | collective-permute-start | bytes 1179656 | tf_op jit(solution)/shard_map/s2/ppermute | solution.py:221
  27.0 13.7 %collective-permute-start.19 = (bf16[12,128,128]{2,1,0:T(8,128)(2,1)S(1)}, bf16[12,128,128]{2,1,0:T(8,128)(2,1)S(1)}, u32[]{:S(2)}, u32[]{:S(2)}) collective-permute-start(bf16[12,128,128]{2,1,0:T(8,128)(2,1)S(1)} %slice.96), channel_id=1, source_target_pairs={{0,48},{1,193},{2,50},{3,195},{4,52},{5,197},{6,54},{7,199},{8,56}... | collective-permute-start | bytes 1179656 | tf_op jit(solution)/shard_map/s2/ppermute | solution.py:221
  30.7 13.0 %copy-start.3 = (bf16[24,128,128]{2,1,0:T(8,128)(2,1)}, bf16[24,128,128]{2,1,0:T(8,128)(2,1)S(1)}, u32[]{:S(2)}) copy-start(bf16[24,128,128]{2,1,0:T(8,128)(2,1)S(1)} %collective-permute-done.1) | copy-start | bytes 2359300
  30.7 20.9 %collective-permute-start.12 = (bf16[24,128,128]{2,1,0:T(8,128)(2,1)S(1)}, bf16[24,128,128]{2,1,0:T(8,128)(2,1)S(1)}, u32[]{:S(2)}, u32[]{:S(2)}) collective-permute-start(bf16[24,128,128]{2,1,0:T(8,128)(2,1)S(1)} %collective-permute-done.3), channel_id=1, source_target_pairs={{0,64},{1,17},{2,66},{3,19},{4,68},{5,21},{6,70},{7,23},{8,72},{9,... | collective-permute-start | bytes 2359304 | tf_op jit(solution)/shard_map/a1/ppermute | solution.py:221
  30.8 21.0 %collective-permute-start.14 = (bf16[24,128,128]{2,1,0:T(8,128)(2,1)S(1)}, bf16[24,128,128]{2,1,0:T(8,128)(2,1)S(1)}, u32[]{:S(2)}, u32[]{:S(2)}) collective-permute-start(bf16[24,128,128]{2,1,0:T(8,128)(2,1)S(1)} %collective-permute-done.4), channel_id=1, source_target_pairs={{0,192},{1,49},{2,194},{3,51},{4,196},{5,53},{6,198},{7,55},{8,200... | collective-permute-start | bytes 2359304 | tf_op jit(solution)/shard_map/a1/ppermute | solution.py:221
  34.8 13.5 %collective-permute-start.8 = (bf16[24,128,128]{2,1,0:T(8,128)(2,1)}, bf16[24,128,128]{2,1,0:T(8,128)(2,1)S(1)}, u32[]{:S(2)}, u32[]{:S(2)}) collective-permute-start(bf16[24,128,128]{2,1,0:T(8,128)(2,1)} %collective-permute-done.7), channel_id=1, source_target_pairs={{0,2},{1,15},{2,4},{3,1},{4,6},{5,3},{6,8},{7,5},{8,10},{9,7},{10,... | collective-permute-start | bytes 2359304 | tf_op jit(solution)/shard_map/z2/ppermute | solution.py:221
  41.0 14.0 %collective-permute-start.20 = (bf16[24,128,128]{2,1,0:T(8,128)(2,1)S(1)}, bf16[24,128,128]{2,1,0:T(8,128)(2,1)S(1)}, u32[]{:S(2)}, u32[]{:S(2)}) collective-permute-start(bf16[24,128,128]{2,1,0:T(8,128)(2,1)S(1)} %get-tuple-element.59), channel_id=1, source_target_pairs={{0,64},{1,17},{2,66},{3,19},{4,68},{5,21},{6,70},{7,23},{8,72},{9,... | collective-permute-start | bytes 2359304 | tf_op jit(solution)/shard_map/b/ppermute | solution.py:221
  41.1 14.1 %collective-permute-start.21 = (bf16[24,128,128]{2,1,0:T(8,128)(2,1)S(1)}, bf16[24,128,128]{2,1,0:T(8,128)(2,1)S(1)}, u32[]{:S(2)}, u32[]{:S(2)}) collective-permute-start(bf16[24,128,128]{2,1,0:T(8,128)(2,1)S(1)} %get-tuple-element.59), channel_id=1, source_target_pairs={{0,192},{1,49},{2,194},{3,51},{4,196},{5,53},{6,198},{7,55},{8,200... | collective-permute-start | bytes 2359304 | tf_op jit(solution)/shard_map/b/ppermute | solution.py:221
  48.3 12.2 %collective-permute-start.9 = (bf16[24,128,128]{2,1,0:T(8,128)(2,1)S(1)}, bf16[24,128,128]{2,1,0:T(8,128)(2,1)S(1)}, u32[]{:S(2)}, u32[]{:S(2)}) collective-permute-start(bf16[24,128,128]{2,1,0:T(8,128)(2,1)S(1)} %collective-permute-done.8), channel_id=1, source_target_pairs={{0,2},{1,15},{2,4},{3,1},{4,6},{5,3},{6,8},{7,5},{8,10},{9,7},{10,... | collective-permute-start | bytes 2359304 | tf_op jit(solution)/shard_map/z3/ppermute | solution.py:221
  51.6 3.4 %slice-start = ((bf16[24,128,128]{2,1,0:T(8,128)(2,1)}), bf16[12,128,128]{2,1,0:T(8,128)(2,1)S(1)}, s32[]{:S(2)}) async-start(bf16[24,128,128]{2,1,0:T(8,128)(2,1)} %copy-done.3), calls=%async_computation | async-start | bytes 786432 | tf_op jit(solution)/shard_map/gh/slice | solution.py:303
  51.7 15.0 %collective-permute-start.13 = (bf16[24,128,128]{2,1,0:T(8,128)(2,1)S(1)}, bf16[24,128,128]{2,1,0:T(8,128)(2,1)S(1)}, u32[]{:S(2)}, u32[]{:S(2)}) collective-permute-start(bf16[24,128,128]{2,1,0:T(8,128)(2,1)S(1)} %pad_maximum_fusion.4), channel_id=1, source_target_pairs={{0,64},{1,17},{2,66},{3,19},{4,68},{5,21},{6,70},{7,23},{8,72},{9,... | collective-permute-start | bytes 2359304 | tf_op jit(solution)/shard_map/ga/ppermute | solution.py:221
  51.9 15.4 %collective-permute-start.15 = (bf16[24,128,128]{2,1,0:T(8,128)(2,1)S(1)}, bf16[24,128,128]{2,1,0:T(8,128)(2,1)S(1)}, u32[]{:S(2)}, u32[]{:S(2)}) collective-permute-start(bf16[24,128,128]{2,1,0:T(8,128)(2,1)S(1)} %pad_maximum_fusion.5), channel_id=1, source_target_pairs={{0,192},{1,49},{2,194},{3,51},{4,196},{5,53},{6,198},{7,55},{8,200... | collective-permute-start | bytes 2359304 | tf_op jit(solution)/shard_map/ga/ppermute | solution.py:221
  55.1 17.5 %collective-permute-start.22 = (bf16[24,128,128]{2,1,0:T(8,128)(2,1)S(1)}, bf16[24,128,128]{2,1,0:T(8,128)(2,1)S(1)}, u32[]{:S(2)}, u32[]{:S(2)}) collective-permute-start(bf16[24,128,128]{2,1,0:T(8,128)(2,1)S(1)} %pad_maximum_fusion.8), channel_id=1, source_target_pairs={{0,64},{1,17},{2,66},{3,19},{4,68},{5,21},{6,70},{7,23},{8,72},{9,... | collective-permute-start | bytes 2359304 | tf_op jit(solution)/shard_map/gh/ppermute | solution.py:221
  60.8 15.5 %collective-permute-start.11 = (bf16[36,128,128]{2,1,0:T(8,128)(2,1)S(1)}, bf16[36,128,128]{2,1,0:T(8,128)(2,1)S(1)}, u32[]{:S(2)}, u32[]{:S(2)}) collective-permute-start(bf16[36,128,128]{2,1,0:T(8,128)(2,1)S(1)} %pad_maximum_fusion.1), channel_id=1, source_target_pairs={{0,1},{1,0},{2,3},{3,2},{4,5},{5,4},{6,7},{7,6},{8,9},{9,8},{10,11... | collective-permute-start | bytes 3538952 | tf_op jit(solution)/shard_map/w4/ppermute | solution.py:221
  65.0 11.2 %collective-permute-start.23 = (bf16[24,128,128]{2,1,0:T(8,128)(2,1)S(1)}, bf16[24,128,128]{2,1,0:T(8,128)(2,1)S(1)}, u32[]{:S(2)}, u32[]{:S(2)}) collective-permute-start(bf16[24,128,128]{2,1,0:T(8,128)(2,1)S(1)} %pad_maximum_fusion.9), channel_id=1, source_target_pairs={{0,192},{1,49},{2,194},{3,51},{4,196},{5,53},{6,198},{7,55},{8,200... | collective-permute-start | bytes 2359304 | tf_op jit(solution)/shard_map/gh/ppermute | solution.py:221
  66.7 9.6 %collective-permute-start.10 = (bf16[12,128,128]{2,1,0:T(8,128)(2,1)S(1)}, bf16[12,128,128]{2,1,0:T(8,128)(2,1)S(1)}, u32[]{:S(2)}, u32[]{:S(2)}) collective-permute-start(bf16[12,128,128]{2,1,0:T(8,128)(2,1)S(1)} %get-tuple-element.57), channel_id=1, source_target_pairs={{0,2},{1,15},{2,4},{3,1},{4,6},{5,3},{6,8},{7,5},{8,10},{9,7},{10,... | collective-permute-start | bytes 1179656 | tf_op jit(solution)/shard_map/z4/ppermute | solution.py:221
  67.5 16.1 %collective-permute-start.16 = (bf16[24,128,128]{2,1,0:T(8,128)(2,1)S(1)}, bf16[24,128,128]{2,1,0:T(8,128)(2,1)S(1)}, u32[]{:S(2)}, u32[]{:S(2)}) collective-permute-start(bf16[24,128,128]{2,1,0:T(8,128)(2,1)S(1)} %pad_maximum_fusion.6), channel_id=1, source_target_pairs={{0,64},{1,17},{2,66},{3,19},{4,68},{5,21},{6,70},{7,23},{8,72},{9,... | collective-permute-start | bytes 2359304 | tf_op jit(solution)/shard_map/a2/ppermute | solution.py:221
  67.7 8.8 %copy-start = (bf16[1,32,128,128]{3,2,1,0:T(8,128)(2,1)S(1)}, bf16[1,32,128,128]{3,2,1,0:T(8,128)(2,1)}, u32[]{:S(2)}) copy-start(bf16[1,32,128,128]{3,2,1,0:T(8,128)(2,1)} %param.8) | copy-start | bytes 3145732
  67.8 8.8 %copy-start.1 = (s32[3,272]{1,0:T(4,128)S(1)}, s32[3,272]{1,0:T(4,128)}, u32[]{:S(2)}) copy-start(s32[3,272]{1,0:T(4,128)} %get-tuple-element.33.entries) | copy-start | bytes 9796
  67.8 8.8 %copy-start.2 = (s32[3]{0:T(128)S(1)}, s32[3]{0:T(128)}, u32[]{:S(2)}) copy-start(s32[3]{0:T(128)} %get-tuple-element.32.groups) | copy-start | bytes 40
  72.6 12.0 %collective-permute-start.17 = (bf16[24,128,128]{2,1,0:T(8,128)(2,1)S(1)}, bf16[24,128,128]{2,1,0:T(8,128)(2,1)S(1)}, u32[]{:S(2)}, u32[]{:S(2)}) collective-permute-start(bf16[24,128,128]{2,1,0:T(8,128)(2,1)S(1)} %pad_maximum_fusion.7), channel_id=1, source_target_pairs={{0,192},{1,49},{2,194},{3,51},{4,196},{5,53},{6,198},{7,55},{8,200... | collective-permute-start | bytes 2359304 | tf_op jit(solution)/shard_map/a2/ppermute | solution.py:221
  82.1 4.8 %collective-permute-start.24 = (f32[11,128,128]{2,1,0:T(8,128)S(1)}, f32[11,128,128]{2,1,0:T(8,128)S(1)}, u32[]{:S(2)}, u32[]{:S(2)}) collective-permute-start(f32[11,128,128]{2,1,0:T(8,128)S(1)} %get-tuple-element.48), channel_id=1, source_target_pairs={{0,1},{1,0},{2,3},{3,2},{4,5},{5,4},{6,7},{7,6},{8,9},{9,8},{10,11... | collective-permute-start | bytes 2162696 | tf_op jit(solution)/shard_map/w3/ppermute | solution.py:221
  83.0 3.8 %collective-permute-start.25 = (f32[11,128,128]{2,1,0:T(8,128)S(1)}, f32[11,128,128]{2,1,0:T(8,128)S(1)}, u32[]{:S(2)}, u32[]{:S(2)}) collective-permute-start(f32[11,128,128]{2,1,0:T(8,128)S(1)} %get-tuple-element.49), channel_id=1, source_target_pairs={{0,1},{1,0},{2,3},{3,2},{4,5},{5,4},{6,7},{7,6},{8,9},{9,8},{10,11... | collective-permute-start | bytes 2162696 | tf_op jit(solution)/shard_map/w3/ppermute | solution.py:221
  83.1 3.7 %collective-permute-start.26 = (f32[10,128,128]{2,1,0:T(8,128)S(1)}, f32[10,128,128]{2,1,0:T(8,128)S(1)}, u32[]{:S(2)}, u32[]{:S(2)}) collective-permute-start(f32[10,128,128]{2,1,0:T(8,128)S(1)} %get-tuple-element.50), channel_id=1, source_target_pairs={{0,1},{1,0},{2,3},{3,2},{4,5},{5,4},{6,7},{7,6},{8,9},{9,8},{10,11... | collective-permute-start | bytes 1966088 | tf_op jit(solution)/shard_map/w3/ppermute | solution.py:221

commit v3 on v2

--- a/solution.py
+++ b/solution.py
@@ -108,36 +108,6 @@
     )(here, jnp.asarray(place_right(shard)), own, got)
 
 
-def select_kernel(core, own, own_left, keep, give, left, sems):
-    c = core[0]
-    size = own_left.shape[1]
-    copies = [
-        pltpu.make_async_copy(own.at[1 - c], give, sems.at[0]),
-        pltpu.make_async_copy(own.at[c], keep, sems.at[1]),
-        pltpu.make_async_copy(own_left.at[c], left.at[pl.ds(0, size)], sems.at[2]),
-        pltpu.make_async_copy(own_left.at[1 - c], left.at[pl.ds(size, size)], sems.at[3]),
-    ]
-    for copy in copies:
-        copy.start()
-    for copy in copies:
-        copy.wait()
-
-
-def select_panels(core, own, own_left):
-    hbm = pl.BlockSpec(memory_space=pl.ANY)
-    vmem = pl.BlockSpec(memory_space=pltpu.VMEM)
-    shard, left_shard, *block = own.shape[1], own_left.shape[1], *own.shape[2:]
-    return pl.pallas_call(
-        select_kernel,
-        out_shape=[jax.ShapeDtypeStruct((n, *block), own.dtype) for n in (shard, shard, 2 * left_shard)],
-        in_specs=[pl.BlockSpec(memory_space=pltpu.SMEM), hbm, hbm],
-        out_specs=[vmem] * 3,
-        scratch_shapes=[pltpu.SemaphoreType.DMA((4,))],
-        cost_estimate=pl.CostEstimate(flops=0, bytes_accessed=2**20, transcendentals=0),
-        name="select_panels",
-    )(core.reshape(1), own, own_left)
-
-
 def products_kernel(stage, groups, entries, left, right, *refs):
     if stage == 0:
         start, acc = refs
@@ -259,18 +229,21 @@
     scope = jax.named_scope
 
     own, own_left = square_panels[:, 0], x_panels[:, 0]
-    keep, give, own_left = select_panels(core, own, own_left)
     with scope("w0"):
-        got = sibling(give)
+        got = sibling(own)
     with scope("w1"):
         got_left = sibling(own_left)
     lists = join(pair_lists.reshape(-1), pair_counts.reshape(-1))
     with scope("w2"):
         got_lists = sibling(lists)
-    unit = join(keep, got)
-    pair = join(own_left[:left_shard], got_left[left_shard:], own_left[left_shard:], got_left[:left_shard])
-
-    unit, pair = order(unit), order(pair)
+
+    def panel(blocks, other=False):
+        return jnp.where((core == 1) != other, blocks[1], blocks[0])
+
+    unit = join(panel(own), panel(got))
+    pair = join(panel(own_left), panel(got_left), panel(own_left, True), panel(got_left, True))
+
+    unit, pair = order((unit, pair))
     with scope("s1"):
         r1, l1 = first(unit, unit)
     with scope("t"):
@@ -288,7 +261,7 @@
     with scope("w4"):
         swapped = sibling(join(z1[half:], z2[half:], z3[half:]))
     left = join(pair[:half], z1[:half], z2[:half], z3[:half], z4, swapped)
-    near1, z1 = order(((r1, l1), z1))
+    near1 = r1, l1
     with scope("s2"):
         s2 = first(near1[0][:shard], near1[1][shard:])
     t, ar, al, entries, groups = order((t, r1, l1, entries, groups))

time: 89.6 us -> 88.2 us (0.984)
  the two profiles are of different devices: /device:TPU:1 before, /device:TPU:96 now
where the time goes in v3:
time: 88.2 us; the launch traced here: 88 us
  starting transfers between devices  41.8 us (47%)
  waiting for transfers between devices  20.8 us (24%)
  Pallas kernels  13.4 us (15%)
  local copies, waits for them, and re-layouts  6.83 us (8%)
  other arithmetic  4.71 us (5%)
    ppermute x27, starting transfers between devices, move(): return lax.ppermute(blocks, ('row', 'col'), pairs)  41.8 us
    ppermute x27, waiting for transfers between devices, move(): return lax.ppermute(blocks, ('row', 'col'), pairs)  20.8 us
    pallas_call x3, Pallas kernels, add_products(): pl.pallas_call(functools.partial(products_kernel, stage), out_shape=outs,...  8.37 us
    pallas_call x1, Pallas kernels, sort_lists(): pl.pallas_call(functools.partial(sort_kernel, left_shard, shard, depth, p...  5.06 us
    unnamed x32, local copies, waits for them, and re-layouts  3.68 us
    select_n x4, other arithmetic, panel(): return jnp.where((core == 1) != other, blocks[1], blocks[0])  2.29 us
  transfers between devices with their start and end apart: 27, of which 8 were waited for; matrix products, arithmetic and copies ran while one was open for 13% of the time, Pallas kernels for 12%

profile of v3, /device:TPU:96, one launch (start us, length us, event | category | flops | bytes accessed | tf_op | source)
XLA Modules:
  0.0 88.0 jit_solution(307005681076321164)
XLA Ops:
  0.0 0.5 collective-permute-start
  0.5 1.1 %select_bitcast_fusion.4 = (bf16[6,128,128]{2,1,0:T(8,128)(2,1)S(1)}, bf16[6,128,128]{2,1,0:T(8,128)(2,1)S(1)}) fusion(pred[]{:T(512)S(6)} %eq.5, bf16[2,1,6,128,128]{4,3,2,1,0:T(8,128)(2,1)} %param.6, pred[]{:T(512)S(6)} %ne.25), kind=kLoop, calls=%fused_computation.19 | loop fusion | flops 196608 | bytes 786434 | tf_op jit(solution)/shard_map/jit(_where)/select_n | solution.py:241
  1.6 1.2 %select_bitcast_fusion = bf16[12,128,128]{2,1,0:T(8,128)(2,1)S(1)} fusion(bf16[2,1,12,128,128]{4,3,2,1,0:T(8,128)(2,1)} %param.7, pred[]{:T(512)S(6)} %eq.5), kind=kLoop, calls=%fused_computation.15 | loop fusion | flops 196608 | bytes 1179649 | tf_op jit(solution)/shard_map/jit(_where)/select_n | solution.py:241
  2.8 1.0 %pad_maximum_fusion.3 = bf16[24,128,128]{2,1,0:T(8,128)(2,1)} fusion(bf16[6,128,128]{2,1,0:T(8,128)(2,1)S(1)} %get-tuple-element.61, bf16[6,128,128]{2,1,0:T(8,128)(2,1)S(1)} %get-tuple-element.59, bf16[6,128,128]{2,1,0:T(8,128)(2,1)S(1)} %get-tuple-element.60, bf16[6,128,128]{2,1,0:T(8,128)(2,1)S(1)} %get-tuple-element.58), kind=kLoop, calls=%fused_computation.3 | loop fusion | flops 1179648 | bytes 1572864 | tf_op jit(solution)/shard_map/concatenate | solution.py:217
  3.8 0.1 pad_maximum_fusion.2
  3.9 1.6 %collective-permute-start.4 = (bf16[24,128,128]{2,1,0:T(8,128)(2,1)S(1)}, bf16[24,128,128]{2,1,0:T(8,128)(2,1)S(1)}, u32[]{:S(2)}, u32[]{:S(2)}) collective-permute-start(bf16[24,128,128]{2,1,0:T(8,128)(2,1)S(1)} %pad_maximum_fusion.2), channel_id=1, source_target_pairs={{0,16},{1,65},{2,18},{3,67},{4,20},{5,69},{6,22},{7,71},{8,24},{9,... | collective-permute-start | bytes 2359304 | tf_op jit(solution)/shard_map/s1/ppermute | solution.py:191
  5.5 0.1 collective-permute-start.6
  5.6 2.6 %collective-permute-start.5 = (bf16[24,128,128]{2,1,0:T(8,128)(2,1)S(1)}, bf16[24,128,128]{2,1,0:T(8,128)(2,1)S(1)}, u32[]{:S(2)}, u32[]{:S(2)}) collective-permute-start(bf16[24,128,128]{2,1,0:T(8,128)(2,1)S(1)} %pad_maximum_fusion.2), channel_id=1, source_target_pairs={{0,48},{1,193},{2,50},{3,195},{4,52},{5,197},{6,54},{7,199},{8,56}... | collective-permute-start | bytes 2359304 | tf_op jit(solution)/shard_map/s1/ppermute | solution.py:191
  8.2 1.6 %collective-permute-start.2 = (bf16[24,128,128]{2,1,0:T(8,128)(2,1)S(1)}, bf16[24,128,128]{2,1,0:T(8,128)(2,1)S(1)}, u32[]{:S(2)}, u32[]{:S(2)}) collective-permute-start(bf16[24,128,128]{2,1,0:T(8,128)(2,1)S(1)} %pad_maximum_fusion.2), channel_id=1, source_target_pairs={{0,64},{1,17},{2,66},{3,19},{4,68},{5,21},{6,70},{7,23},{8,72},{9,... | collective-permute-start | bytes 2359304 | tf_op jit(solution)/shard_map/t/ppermute | solution.py:191
  9.8 1.7 %collective-permute-start.3 = (bf16[24,128,128]{2,1,0:T(8,128)(2,1)S(1)}, bf16[24,128,128]{2,1,0:T(8,128)(2,1)}, u32[]{:S(2)}, u32[]{:S(2)}) collective-permute-start(bf16[24,128,128]{2,1,0:T(8,128)(2,1)S(1)} %pad_maximum_fusion.2), channel_id=1, source_target_pairs={{0,192},{1,49},{2,194},{3,51},{4,196},{5,53},{6,198},{7,55},{8,200... | collective-permute-start | bytes 2359304 | tf_op jit(solution)/shard_map/t/ppermute | solution.py:191
  11.5 3.1 %collective-permute-start.7 = (bf16[24,128,128]{2,1,0:T(8,128)(2,1)}, bf16[24,128,128]{2,1,0:T(8,128)(2,1)}, u32[]{:S(2)}, u32[]{:S(2)}) collective-permute-start(bf16[24,128,128]{2,1,0:T(8,128)(2,1)} %pad_maximum_fusion.3), channel_id=1, source_target_pairs={{0,2},{1,15},{2,4},{3,1},{4,6},{5,3},{6,8},{7,5},{8,10},{9,7},{10,... | collective-permute-start | bytes 2359304 | tf_op jit(solution)/shard_map/z1/ppermute | solution.py:191
  14.6 0.7 pad_add_fusion.1.here
  15.3 5.1 %sort_lists.1 = (s32[3,272]{1,0:T(4,128)}, s32[3]{0:T(128)}) custom-call(s32[4]{0:T(128)} %pad_add_fusion.1.here, s32[64]{0:T(128)} %constant.54.clone.right_at, s32[770]{0:T(1024)} %copy-done.4, s32[770]{0:T(1024)} %copy-done.5), custom_call_target="tpu_custom_call" | custom-call | bytes 8388608 | tf_op jit(solution)/shard_map/sort_lists/pallas_call | solution.py:93
  20.4 1.0 %slice_dynamic-update-slice_fusion.2 = bf16[96,128,128]{2,1,0:T(8,128)(2,1)S(1)} fusion(bf16[24,128,128]{2,1,0:T(8,128)(2,1)} %pad_maximum_fusion.3), kind=kLoop, calls=%fused_computation.14 | loop fusion | bytes 786432
  21.5 0.2 collective-permute-done.4
  21.7 0.4 collective-permute-start.18
  22.1 1.5 %collective-permute-done.5 = bf16[24,128,128]{2,1,0:T(8,128)(2,1)S(1)} collective-permute-done((bf16[24,128,128]{2,1,0:T(8,128)(2,1)S(1)}, bf16[24,128,128]{2,1,0:T(8,128)(2,1)S(1)}, u32[]{:S(2)}, u32[]{:S(2)}) %collective-permute-start.5) | collective-permute-done | bytes 786464 | tf_op jit(solution)/shard_map/s1/ppermute | solution.py:191
  23.6 3.8 %collective-permute-start.19 = (bf16[12,128,128]{2,1,0:T(8,128)(2,1)S(1)}, bf16[12,128,128]{2,1,0:T(8,128)(2,1)S(1)}, u32[]{:S(2)}, u32[]{:S(2)}) collective-permute-start(bf16[12,128,128]{2,1,0:T(8,128)(2,1)S(1)} %slice.133), channel_id=1, source_target_pairs={{0,48},{1,193},{2,50},{3,195},{4,52},{5,197},{6,54},{7,199},{8,56}... | collective-permute-start | bytes 1179656 | tf_op jit(solution)/shard_map/s2/ppermute | solution.py:191
  27.3 4.3 %collective-permute-start.12 = (bf16[24,128,128]{2,1,0:T(8,128)(2,1)S(1)}, bf16[24,128,128]{2,1,0:T(8,128)(2,1)S(1)}, u32[]{:S(2)}, u32[]{:S(2)}) collective-permute-start(bf16[24,128,128]{2,1,0:T(8,128)(2,1)S(1)} %collective-permute-done.4), channel_id=1, source_target_pairs={{0,64},{1,17},{2,66},{3,19},{4,68},{5,21},{6,70},{7,23},{8,72},{9,... | collective-permute-start | bytes 2359304 | tf_op jit(solution)/shard_map/a1/ppermute | solution.py:191
  31.6 1.0 %slice.120 = bf16[12,128,128]{2,1,0:T(8,128)(2,1)S(1)} slice(bf16[24,128,128]{2,1,0:T(8,128)(2,1)} %collective-permute-done.3), slice={[12:24], [0:128], [0:128]} | slice | bytes 786432 | tf_op jit(solution)/shard_map/gh/slice | solution.py:276
  32.7 3.2 %collective-permute-start.8 = (bf16[24,128,128]{2,1,0:T(8,128)(2,1)}, bf16[24,128,128]{2,1,0:T(8,128)(2,1)S(1)}, u32[]{:S(2)}, u32[]{:S(2)}) collective-permute-start(bf16[24,128,128]{2,1,0:T(8,128)(2,1)} %collective-permute-done.7), channel_id=1, source_target_pairs={{0,2},{1,15},{2,4},{3,1},{4,6},{5,3},{6,8},{7,5},{8,10},{9,7},{10,... | collective-permute-start | bytes 2359304 | tf_op jit(solution)/shard_map/z2/ppermute | solution.py:191
  35.9 1.2 %fusion.2 = (bf16[12,128,128]{2,1,0:T(8,128)(2,1)S(1)}, bf16[96,128,128]{2,1,0:T(8,128)(2,1)S(1)}) fusion(bf16[24,128,128]{2,1,0:T(8,128)(2,1)} %collective-permute-done.7, bf16[96,128,128]{2,1,0:T(8,128)(2,1)S(1)} %slice_dynamic-update-slice_fusion.2), kind=kLoop, calls=%fused_computation.43 | loop fusion | bytes 1572864 | tf_op jit(solution)/shard_map/w4/slice | solution.py:262
  37.1 0.1 constant_dynamic-update-slice_fusion.18
  37.2 0.1 constant_dynamic-update-slice_fusion.17
  37.3 0.1 constant_dynamic-update-slice_fusion.16
  37.5 0.2 constant_dynamic-update-slice_fusion.15
  37.7 3.6 %collective-permute-start.20 = (bf16[24,128,128]{2,1,0:T(8,128)(2,1)S(1)}, bf16[24,128,128]{2,1,0:T(8,128)(2,1)S(1)}, u32[]{:S(2)}, u32[]{:S(2)}) collective-permute-start(bf16[24,128,128]{2,1,0:T(8,128)(2,1)S(1)} %get-tuple-element.55), channel_id=1, source_target_pairs={{0,64},{1,17},{2,66},{3,19},{4,68},{5,21},{6,70},{7,23},{8,72},{9,... | collective-permute-start | bytes 2359304 | tf_op jit(solution)/shard_map/b/ppermute | solution.py:191
  41.4 0.1 constant_dynamic-update-slice_fusion.14
  41.5 1.3 %constant_dynamic-update-slice_fusion.13 = bf16[192,128,128]{2,1,0:T(8,128)(2,1)S(1)} fusion(bf16[192,128,128]{2,1,0:T(8,128)(2,1)S(1)} %constant_dynamic-update-slice_fusion.14, bf16[24,128,128]{2,1,0:T(8,128)(2,1)} %collective-permute-done.3), kind=kLoop, calls=%fused_computation.33 | loop fusion | bytes 1572864
  42.7 3.0 %collective-permute-done.8 = bf16[24,128,128]{2,1,0:T(8,128)(2,1)S(1)} collective-permute-done((bf16[24,128,128]{2,1,0:T(8,128)(2,1)}, bf16[24,128,128]{2,1,0:T(8,128)(2,1)S(1)}, u32[]{:S(2)}, u32[]{:S(2)}) %collective-permute-start.8) | collective-permute-done | bytes 786464 | tf_op jit(solution)/shard_map/z2/ppermute | solution.py:191
  45.7 3.6 %collective-permute-start.9 = (bf16[24,128,128]{2,1,0:T(8,128)(2,1)S(1)}, bf16[24,128,128]{2,1,0:T(8,128)(2,1)S(1)}, u32[]{:S(2)}, u32[]{:S(2)}) collective-permute-start(bf16[24,128,128]{2,1,0:T(8,128)(2,1)S(1)} %collective-permute-done.8), channel_id=1, source_target_pairs={{0,2},{1,15},{2,4},{3,1},{4,6},{5,3},{6,8},{7,5},{8,10},{9,7},{10,... | collective-permute-start | bytes 2359304 | tf_op jit(solution)/shard_map/z3/ppermute | solution.py:191
  49.3 0.1 pad_maximum_fusion.5
  49.4 1.8 %collective-permute-start.15 = (bf16[24,128,128]{2,1,0:T(8,128)(2,1)S(1)}, bf16[24,128,128]{2,1,0:T(8,128)(2,1)S(1)}, u32[]{:S(2)}, u32[]{:S(2)}) collective-permute-start(bf16[24,128,128]{2,1,0:T(8,128)(2,1)S(1)} %pad_maximum_fusion.5), channel_id=1, source_target_pairs={{0,192},{1,49},{2,194},{3,51},{4,196},{5,53},{6,198},{7,55},{8,200... | collective-permute-start | bytes 2359304 | tf_op jit(solution)/shard_map/ga/ppermute | solution.py:191
  51.2 0.1 pad_maximum_fusion.4
  51.3 0.4 collective-permute-start.13
  51.7 0.1 constant_dynamic-update-slice_fusion.12
  51.8 0.1 constant_dynamic-update-slice_fusion.11.right
  52.0 0.1 fusion.3
  52.2 2.1 %collective-permute-start.22 = (bf16[24,128,128]{2,1,0:T(8,128)(2,1)S(1)}, bf16[24,128,128]{2,1,0:T(8,128)(2,1)S(1)}, u32[]{:S(2)}, u32[]{:S(2)}) collective-permute-start(bf16[24,128,128]{2,1,0:T(8,128)(2,1)S(1)} %pad_maximum_fusion.8), channel_id=1, source_target_pairs={{0,64},{1,17},{2,66},{3,19},{4,68},{5,21},{6,70},{7,23},{8,72},{9,... | collective-permute-start | bytes 2359304 | tf_op jit(solution)/shard_map/gh/ppermute | solution.py:191
  54.3 4.5 %collective-permute-done.9 = bf16[24,128,128]{2,1,0:T(8,128)(2,1)S(1)} collective-permute-done((bf16[24,128,128]{2,1,0:T(8,128)(2,1)S(1)}, bf16[24,128,128]{2,1,0:T(8,128)(2,1)S(1)}, u32[]{:S(2)}, u32[]{:S(2)}) %collective-permute-start.9) | collective-permute-done | bytes 786464 | tf_op jit(solution)/shard_map/z3/ppermute | solution.py:191
  58.8 0.2 fusion.4
  59.0 0.1 pad_maximum_fusion.1
  59.1 0.1 collective-permute-start.11
  59.3 1.8 %collective-permute-start.23 = (bf16[24,128,128]{2,1,0:T(8,128)(2,1)S(1)}, bf16[24,128,128]{2,1,0:T(8,128)(2,1)S(1)}, u32[]{:S(2)}, u32[]{:S(2)}) collective-permute-start(bf16[24,128,128]{2,1,0:T(8,128)(2,1)S(1)} %pad_maximum_fusion.9), channel_id=1, source_target_pairs={{0,192},{1,49},{2,194},{3,51},{4,196},{5,53},{6,198},{7,55},{8,200... | collective-permute-start | bytes 2359304 | tf_op jit(solution)/shard_map/gh/ppermute | solution.py:191
  61.1 0.1 constant_dynamic-update-slice_fusion.9
  61.2 0.5 collective-permute-done.15
  61.8 3.2 %collective-permute-start.10 = (bf16[12,128,128]{2,1,0:T(8,128)(2,1)S(1)}, bf16[12,128,128]{2,1,0:T(8,128)(2,1)S(1)}, u32[]{:S(2)}, u32[]{:S(2)}) collective-permute-start(bf16[12,128,128]{2,1,0:T(8,128)(2,1)S(1)} %get-tuple-element.53), channel_id=1, source_target_pairs={{0,2},{1,15},{2,4},{3,1},{4,6},{5,3},{6,8},{7,5},{8,10},{9,7},{10,... | collective-permute-start | bytes 1179656 | tf_op jit(solution)/shard_map/z4/ppermute | solution.py:191
  65.2 0.9 %collective-permute-start.16 = (bf16[24,128,128]{2,1,0:T(8,128)(2,1)S(1)}, bf16[24,128,128]{2,1,0:T(8,128)(2,1)S(1)}, u32[]{:S(2)}, u32[]{:S(2)}) collective-permute-start(bf16[24,128,128]{2,1,0:T(8,128)(2,1)S(1)} %pad_maximum_fusion.6), channel_id=1, source_target_pairs={{0,64},{1,17},{2,66},{3,19},{4,68},{5,21},{6,70},{7,23},{8,72},{9,... | collective-permute-start | bytes 2359304 | tf_op jit(solution)/shard_map/a2/ppermute | solution.py:191
  66.2 0.1 constant_dynamic-update-slice_fusion.8
  66.3 0.1 constant_dynamic-update-slice_fusion.7
  66.5 6.5 %collective-permute-done.22 = bf16[24,128,128]{2,1,0:T(8,128)(2,1)S(1)} collective-permute-done((bf16[24,128,128]{2,1,0:T(8,128)(2,1)S(1)}, bf16[24,128,128]{2,1,0:T(8,128)(2,1)S(1)}, u32[]{:S(2)}, u32[]{:S(2)}) %collective-permute-start.22) | collective-permute-done | bytes 786464 | tf_op jit(solution)/shard_map/gh/ppermute | solution.py:191
  73.0 0.7 collective-permute-start.17
  73.7 0.1 constant_dynamic-update-slice_fusion.6
  73.8 0.1 constant_dynamic-update-slice_fusion.5.right
  74.0 0.2 constant_dynamic-update-slice_fusion.left
  74.2 3.0 %products.3.refs_0_ = f32[65,128,128]{2,1,0:T(8,128)S(1)} custom-call(s32[3]{0:T(128)S(1)} %copy-done.2, s32[3,272]{1,0:T(4,128)S(1)} %copy-done.1, bf16[96,128,128]{2,1,0:T(8,128)(2,1)S(1)} %constant_dynamic-update-slice_fusion.left, bf16[192,128,128]{2,1,0:T(8,128)(2,1)S(1)} %constant_dynamic-update-slice_fusion.11.right, bf16[32,128,128]{2,1,0:T(8,128)(2,1)S(1)} %bitcast.21), custom_call_target="tpu_custom_call" | custom-call | flops 1048576 | bytes 1048576 | tf_op jit(solution)/shard_map/products/pallas_call | solution.py:169
  77.3 2.4 %products.4 = (f32[32,128,128]{2,1,0:T(8,128)S(1)}, f32[11,128,128]{2,1,0:T(8,128)S(1)}, f32[11,128,128]{2,1,0:T(8,128)S(1)}, f32[10,128,128]{2,1,0:T(8,128)S(1)}) custom-call(s32[3]{0:T(128)S(1)} %copy-done.2, s32[3,272]{1,0:T(4,128)S(1)} %copy-done.1, bf16[96,128,128]{2,1,0:T(8,128)(2,1)S(1)} %constant_dynamic-update-slice_fusion.left, ...), custom_call_target="tpu_custom_call" | custom-call | flops 1048576 | bytes 1048576 | tf_op jit(solution)/shard_map/products/pallas_call | solution.py:169
  79.7 0.1 collective-permute-start.24
  79.8 0.5 collective-permute-start.25
  80.3 0.1 collective-permute-start.26
  80.4 1.0 %collective-permute-done.16 = bf16[24,128,128]{2,1,0:T(8,128)(2,1)S(1)} collective-permute-done((bf16[24,128,128]{2,1,0:T(8,128)(2,1)S(1)}, bf16[24,128,128]{2,1,0:T(8,128)(2,1)S(1)}, u32[]{:S(2)}, u32[]{:S(2)}) %collective-permute-start.16) | collective-permute-done | bytes 786464 | tf_op jit(solution)/shard_map/a2/ppermute | solution.py:191
  81.4 3.6 %collective-permute-done.17 = bf16[24,128,128]{2,1,0:T(8,128)(2,1)S(1)} collective-permute-done((bf16[24,128,128]{2,1,0:T(8,128)(2,1)S(1)}, bf16[24,128,128]{2,1,0:T(8,128)(2,1)S(1)}, u32[]{:S(2)}, u32[]{:S(2)}) %collective-permute-start.17) | collective-permute-done | bytes 786464 | tf_op jit(solution)/shard_map/a2/ppermute | solution.py:191
  85.0 0.1 pad_maximum_fusion.right
  85.2 2.9 %products.5 = bf16[32,128,128]{2,1,0:T(8,128)(2,1)} custom-call(s32[3]{0:T(128)S(1)} %copy-done.2, s32[3,272]{1,0:T(4,128)S(1)} %copy-done.1, bf16[96,128,128]{2,1,0:T(8,128)(2,1)S(1)} %constant_dynamic-update-slice_fusion.left, bf16[48,128,128]{2,1,0:T(8,128)(2,1)S(1)} %pad_maximum_fusion.right, f32[32,128,128]{2,1,0:T(8,128)S(1)} %get-tuple-element.41.refs_0_, ...), custom_call_target="tpu_custom_call" | custom-call | flops 1048576 | bytes 1048576 | tf_op jit(solution)/shard_map/products/pallas_call | solution.py:169
  (62 shorter events, 1.0 us)
Async XLA Ops:
  0.0 5.5 %copy-start.6 = (s32[1,1,2,3,128]{4,2,3,1,0:T(2,128)S(1)}, s32[1,1,2,3,128]{4,2,3,1,0:T(2,128)}, u32[]{:S(2)}) copy-start(s32[1,1,2,3,128]{4,2,3,1,0:T(2,128)} %param.9) | copy-start | bytes 9220
  0.0 5.5 %copy-start.7 = (s32[1,1,2]{2,1,0:T(1,128)S(1)}, s32[1,1,2]{2,1,0:T(1,128)}, u32[]{:S(2)}) copy-start(s32[1,1,2]{2,1,0:T(1,128)} %param.10) | copy-start | bytes 28
  0.0 2.7 %collective-permute-start.1 = (bf16[2,6,128,128]{3,2,1,0:T(8,128)(2,1)}, bf16[2,6,128,128]{3,2,1,0:T(8,128)(2,1)S(1)}, u32[]{:S(2)}, u32[]{:S(2)}) collective-permute-start(bf16[2,6,128,128]{3,2,1,0:T(8,128)(2,1)} %bitcast.23), channel_id=1, source_target_pairs={{0,1},{1,0},{2,3},{3,2},{4,5},{5,4},{6,7},{7,6},{8,9},{9,8},{10,11... | collective-permute-start | bytes 1179656 | tf_op jit(solution)/shard_map/w1/ppermute | solution.py:191
  0.0 3.8 %collective-permute-start = (bf16[2,12,128,128]{3,2,1,0:T(8,128)(2,1)}, bf16[2,12,128,128]{3,2,1,0:T(8,128)(2,1)S(1)}, u32[]{:S(2)}, u32[]{:S(2)}) collective-permute-start(bf16[2,12,128,128]{3,2,1,0:T(8,128)(2,1)} %bitcast.22), channel_id=1, source_target_pairs={{0,1},{1,0},{2,3},{3,2},{4,5},{5,4},{6,7},{7,6},{8,9},{9,8},{10,11... | collective-permute-start | bytes 2359304 | tf_op jit(solution)/shard_map/w0/ppermute | solution.py:191
  3.9 17.7 %collective-permute-start.4 = (bf16[24,128,128]{2,1,0:T(8,128)(2,1)S(1)}, bf16[24,128,128]{2,1,0:T(8,128)(2,1)S(1)}, u32[]{:S(2)}, u32[]{:S(2)}) collective-permute-start(bf16[24,128,128]{2,1,0:T(8,128)(2,1)S(1)} %pad_maximum_fusion.2), channel_id=1, source_target_pairs={{0,16},{1,65},{2,18},{3,67},{4,20},{5,69},{6,22},{7,71},{8,24},{9,... | collective-permute-start | bytes 2359304 | tf_op jit(solution)/shard_map/s1/ppermute | solution.py:191
  5.5 9.8 %copy-start.4 = (s32[770]{0:T(1024)}, s32[770]{0:T(1024)S(1)}, u32[]{:S(2)}) copy-start(s32[770]{0:T(1024)S(1)} %pad_add_fusion.own) | copy-start | bytes 9244
  5.5 6.0 %collective-permute-start.6 = (s32[770]{0:T(1024)S(1)}, s32[770]{0:T(1024)S(1)}, u32[]{:S(2)}, u32[]{:S(2)}) collective-permute-start(s32[770]{0:T(1024)S(1)} %pad_add_fusion.own), channel_id=1, source_target_pairs={{0,1},{1,0},{2,3},{3,2},{4,5},{5,4},{6,7},{7,6},{8,9},{9,8},{10,11... | collective-permute-start | bytes 9248 | tf_op jit(solution)/shard_map/w2/ppermute | solution.py:191
  5.6 17.9 %collective-permute-start.5 = (bf16[24,128,128]{2,1,0:T(8,128)(2,1)S(1)}, bf16[24,128,128]{2,1,0:T(8,128)(2,1)S(1)}, u32[]{:S(2)}, u32[]{:S(2)}) collective-permute-start(bf16[24,128,128]{2,1,0:T(8,128)(2,1)S(1)} %pad_maximum_fusion.2), channel_id=1, source_target_pairs={{0,48},{1,193},{2,50},{3,195},{4,52},{5,197},{6,54},{7,199},{8,56}... | collective-permute-start | bytes 2359304 | tf_op jit(solution)/shard_map/s1/ppermute | solution.py:191
  8.2 19.1 %collective-permute-start.2 = (bf16[24,128,128]{2,1,0:T(8,128)(2,1)S(1)}, bf16[24,128,128]{2,1,0:T(8,128)(2,1)S(1)}, u32[]{:S(2)}, u32[]{:S(2)}) collective-permute-start(bf16[24,128,128]{2,1,0:T(8,128)(2,1)S(1)} %pad_maximum_fusion.2), channel_id=1, source_target_pairs={{0,64},{1,17},{2,66},{3,19},{4,68},{5,21},{6,70},{7,23},{8,72},{9,... | collective-permute-start | bytes 2359304 | tf_op jit(solution)/shard_map/t/ppermute | solution.py:191
  9.8 17.5 %collective-permute-start.3 = (bf16[24,128,128]{2,1,0:T(8,128)(2,1)S(1)}, bf16[24,128,128]{2,1,0:T(8,128)(2,1)}, u32[]{:S(2)}, u32[]{:S(2)}) collective-permute-start(bf16[24,128,128]{2,1,0:T(8,128)(2,1)S(1)} %pad_maximum_fusion.2), channel_id=1, source_target_pairs={{0,192},{1,49},{2,194},{3,51},{4,196},{5,53},{6,198},{7,55},{8,200... | collective-permute-start | bytes 2359304 | tf_op jit(solution)/shard_map/t/ppermute | solution.py:191
  11.5 3.8 %copy-start.5 = (s32[770]{0:T(1024)}, s32[770]{0:T(1024)S(1)}, u32[]{:S(2)}) copy-start(s32[770]{0:T(1024)S(1)} %collective-permute-done.6.got) | copy-start | bytes 9244
  11.5 21.2 %collective-permute-start.7 = (bf16[24,128,128]{2,1,0:T(8,128)(2,1)}, bf16[24,128,128]{2,1,0:T(8,128)(2,1)}, u32[]{:S(2)}, u32[]{:S(2)}) collective-permute-start(bf16[24,128,128]{2,1,0:T(8,128)(2,1)} %pad_maximum_fusion.3), channel_id=1, source_target_pairs={{0,2},{1,15},{2,4},{3,1},{4,6},{5,3},{6,8},{7,5},{8,10},{9,7},{10,... | collective-permute-start | bytes 2359304 | tf_op jit(solution)/shard_map/z1/ppermute | solution.py:191
  21.7 15.6 %collective-permute-start.18 = (bf16[12,128,128]{2,1,0:T(8,128)(2,1)S(1)}, bf16[12,128,128]{2,1,0:T(8,128)(2,1)S(1)}, u32[]{:S(2)}, u32[]{:S(2)}) collective-permute-start(bf16[12,128,128]{2,1,0:T(8,128)(2,1)S(1)} %get-tuple-element.45), channel_id=1, source_target_pairs={{0,16},{1,65},{2,18},{3,67},{4,20},{5,69},{6,22},{7,71},{8,24},{9,... | collective-permute-start | bytes 1179656 | tf_op jit(solution)/shard_map/s2/ppermute | solution.py:191
  23.6 13.9 %collective-permute-start.19 = (bf16[12,128,128]{2,1,0:T(8,128)(2,1)S(1)}, bf16[12,128,128]{2,1,0:T(8,128)(2,1)S(1)}, u32[]{:S(2)}, u32[]{:S(2)}) collective-permute-start(bf16[12,128,128]{2,1,0:T(8,128)(2,1)S(1)} %slice.133), channel_id=1, source_target_pairs={{0,48},{1,193},{2,50},{3,195},{4,52},{5,197},{6,54},{7,199},{8,56}... | collective-permute-start | bytes 1179656 | tf_op jit(solution)/shard_map/s2/ppermute | solution.py:191
  27.3 14.1 %copy-start.3 = (bf16[24,128,128]{2,1,0:T(8,128)(2,1)}, bf16[24,128,128]{2,1,0:T(8,128)(2,1)S(1)}, u32[]{:S(2)}) copy-start(bf16[24,128,128]{2,1,0:T(8,128)(2,1)S(1)} %collective-permute-done.2) | copy-start | bytes 2359300
  27.3 23.8 %collective-permute-start.12 = (bf16[24,128,128]{2,1,0:T(8,128)(2,1)S(1)}, bf16[24,128,128]{2,1,0:T(8,128)(2,1)S(1)}, u32[]{:S(2)}, u32[]{:S(2)}) collective-permute-start(bf16[24,128,128]{2,1,0:T(8,128)(2,1)S(1)} %collective-permute-done.4), channel_id=1, source_target_pairs={{0,64},{1,17},{2,66},{3,19},{4,68},{5,21},{6,70},{7,23},{8,72},{9,... | collective-permute-start | bytes 2359304 | tf_op jit(solution)/shard_map/a1/ppermute | solution.py:191
  31.6 17.7 %collective-permute-start.14 = (bf16[24,128,128]{2,1,0:T(8,128)(2,1)S(1)}, bf16[24,128,128]{2,1,0:T(8,128)(2,1)S(1)}, u32[]{:S(2)}, u32[]{:S(2)}) collective-permute-start(bf16[24,128,128]{2,1,0:T(8,128)(2,1)S(1)} %collective-permute-done.5), channel_id=1, source_target_pairs={{0,192},{1,49},{2,194},{3,51},{4,196},{5,53},{6,198},{7,55},{8,200... | collective-permute-start | bytes 2359304 | tf_op jit(solution)/shard_map/a1/ppermute | solution.py:191
  32.7 13.0 %collective-permute-start.8 = (bf16[24,128,128]{2,1,0:T(8,128)(2,1)}, bf16[24,128,128]{2,1,0:T(8,128)(2,1)S(1)}, u32[]{:S(2)}, u32[]{:S(2)}) collective-permute-start(bf16[24,128,128]{2,1,0:T(8,128)(2,1)} %collective-permute-done.7), channel_id=1, source_target_pairs={{0,2},{1,15},{2,4},{3,1},{4,6},{5,3},{6,8},{7,5},{8,10},{9,7},{10,... | collective-permute-start | bytes 2359304 | tf_op jit(solution)/shard_map/z2/ppermute | solution.py:191
  37.7 14.4 %collective-permute-start.20 = (bf16[24,128,128]{2,1,0:T(8,128)(2,1)S(1)}, bf16[24,128,128]{2,1,0:T(8,128)(2,1)S(1)}, u32[]{:S(2)}, u32[]{:S(2)}) collective-permute-start(bf16[24,128,128]{2,1,0:T(8,128)(2,1)S(1)} %get-tuple-element.55), channel_id=1, source_target_pairs={{0,64},{1,17},{2,66},{3,19},{4,68},{5,21},{6,70},{7,23},{8,72},{9,... | collective-permute-start | bytes 2359304 | tf_op jit(solution)/shard_map/b/ppermute | solution.py:191
  41.3 12.9 %collective-permute-start.21 = (bf16[24,128,128]{2,1,0:T(8,128)(2,1)S(1)}, bf16[24,128,128]{2,1,0:T(8,128)(2,1)S(1)}, u32[]{:S(2)}, u32[]{:S(2)}) collective-permute-start(bf16[24,128,128]{2,1,0:T(8,128)(2,1)S(1)} %get-tuple-element.55), channel_id=1, source_target_pairs={{0,192},{1,49},{2,194},{3,51},{4,196},{5,53},{6,198},{7,55},{8,200... | collective-permute-start | bytes 2359304 | tf_op jit(solution)/shard_map/b/ppermute | solution.py:191
  45.7 13.1 %collective-permute-start.9 = (bf16[24,128,128]{2,1,0:T(8,128)(2,1)S(1)}, bf16[24,128,128]{2,1,0:T(8,128)(2,1)S(1)}, u32[]{:S(2)}, u32[]{:S(2)}) collective-permute-start(bf16[24,128,128]{2,1,0:T(8,128)(2,1)S(1)} %collective-permute-done.8), channel_id=1, source_target_pairs={{0,2},{1,15},{2,4},{3,1},{4,6},{5,3},{6,8},{7,5},{8,10},{9,7},{10,... | collective-permute-start | bytes 2359304 | tf_op jit(solution)/shard_map/z3/ppermute | solution.py:191
  49.3 2.8 %slice-start = ((bf16[24,128,128]{2,1,0:T(8,128)(2,1)}), bf16[12,128,128]{2,1,0:T(8,128)(2,1)S(1)}, s32[]{:S(2)}) async-start(bf16[24,128,128]{2,1,0:T(8,128)(2,1)} %copy-done.3), calls=%async_computation | async-start | bytes 786432 | tf_op jit(solution)/shard_map/gh/slice | solution.py:276
  49.4 12.3 %collective-permute-start.15 = (bf16[24,128,128]{2,1,0:T(8,128)(2,1)S(1)}, bf16[24,128,128]{2,1,0:T(8,128)(2,1)S(1)}, u32[]{:S(2)}, u32[]{:S(2)}) collective-permute-start(bf16[24,128,128]{2,1,0:T(8,128)(2,1)S(1)} %pad_maximum_fusion.5), channel_id=1, source_target_pairs={{0,192},{1,49},{2,194},{3,51},{4,196},{5,53},{6,198},{7,55},{8,200... | collective-permute-start | bytes 2359304 | tf_op jit(solution)/shard_map/ga/ppermute | solution.py:191
  51.3 13.7 %collective-permute-start.13 = (bf16[24,128,128]{2,1,0:T(8,128)(2,1)S(1)}, bf16[24,128,128]{2,1,0:T(8,128)(2,1)S(1)}, u32[]{:S(2)}, u32[]{:S(2)}) collective-permute-start(bf16[24,128,128]{2,1,0:T(8,128)(2,1)S(1)} %pad_maximum_fusion.4), channel_id=1, source_target_pairs={{0,64},{1,17},{2,66},{3,19},{4,68},{5,21},{6,70},{7,23},{8,72},{9,... | collective-permute-start | bytes 2359304 | tf_op jit(solution)/shard_map/ga/ppermute | solution.py:191
  52.2 20.8 %collective-permute-start.22 = (bf16[24,128,128]{2,1,0:T(8,128)(2,1)S(1)}, bf16[24,128,128]{2,1,0:T(8,128)(2,1)S(1)}, u32[]{:S(2)}, u32[]{:S(2)}) collective-permute-start(bf16[24,128,128]{2,1,0:T(8,128)(2,1)S(1)} %pad_maximum_fusion.8), channel_id=1, source_target_pairs={{0,64},{1,17},{2,66},{3,19},{4,68},{5,21},{6,70},{7,23},{8,72},{9,... | collective-permute-start | bytes 2359304 | tf_op jit(solution)/shard_map/gh/ppermute | solution.py:191
  59.1 14.9 %collective-permute-start.11 = (bf16[36,128,128]{2,1,0:T(8,128)(2,1)S(1)}, bf16[36,128,128]{2,1,0:T(8,128)(2,1)S(1)}, u32[]{:S(2)}, u32[]{:S(2)}) collective-permute-start(bf16[36,128,128]{2,1,0:T(8,128)(2,1)S(1)} %pad_maximum_fusion.1), channel_id=1, source_target_pairs={{0,1},{1,0},{2,3},{3,2},{4,5},{5,4},{6,7},{7,6},{8,9},{9,8},{10,11... | collective-permute-start | bytes 3538952 | tf_op jit(solution)/shard_map/w4/ppermute | solution.py:191
  59.3 14.5 %collective-permute-start.23 = (bf16[24,128,128]{2,1,0:T(8,128)(2,1)S(1)}, bf16[24,128,128]{2,1,0:T(8,128)(2,1)S(1)}, u32[]{:S(2)}, u32[]{:S(2)}) collective-permute-start(bf16[24,128,128]{2,1,0:T(8,128)(2,1)S(1)} %pad_maximum_fusion.9), channel_id=1, source_target_pairs={{0,192},{1,49},{2,194},{3,51},{4,196},{5,53},{6,198},{7,55},{8,200... | collective-permute-start | bytes 2359304 | tf_op jit(solution)/shard_map/gh/ppermute | solution.py:191
  61.8 12.2 %collective-permute-start.10 = (bf16[12,128,128]{2,1,0:T(8,128)(2,1)S(1)}, bf16[12,128,128]{2,1,0:T(8,128)(2,1)S(1)}, u32[]{:S(2)}, u32[]{:S(2)}) collective-permute-start(bf16[12,128,128]{2,1,0:T(8,128)(2,1)S(1)} %get-tuple-element.53), channel_id=1, source_target_pairs={{0,2},{1,15},{2,4},{3,1},{4,6},{5,3},{6,8},{7,5},{8,10},{9,7},{10,... | collective-permute-start | bytes 1179656 | tf_op jit(solution)/shard_map/z4/ppermute | solution.py:191
  65.2 16.3 %collective-permute-start.16 = (bf16[24,128,128]{2,1,0:T(8,128)(2,1)S(1)}, bf16[24,128,128]{2,1,0:T(8,128)(2,1)S(1)}, u32[]{:S(2)}, u32[]{:S(2)}) collective-permute-start(bf16[24,128,128]{2,1,0:T(8,128)(2,1)S(1)} %pad_maximum_fusion.6), channel_id=1, source_target_pairs={{0,64},{1,17},{2,66},{3,19},{4,68},{5,21},{6,70},{7,23},{8,72},{9,... | collective-permute-start | bytes 2359304 | tf_op jit(solution)/shard_map/a2/ppermute | solution.py:191
  66.3 7.9 %copy-start = (bf16[1,32,128,128]{3,2,1,0:T(8,128)(2,1)S(1)}, bf16[1,32,128,128]{3,2,1,0:T(8,128)(2,1)}, u32[]{:S(2)}) copy-start(bf16[1,32,128,128]{3,2,1,0:T(8,128)(2,1)} %param.8) | copy-start | bytes 3145732
  66.3 7.9 %copy-start.1 = (s32[3,272]{1,0:T(4,128)S(1)}, s32[3,272]{1,0:T(4,128)}, u32[]{:S(2)}) copy-start(s32[3,272]{1,0:T(4,128)} %get-tuple-element.29.entries) | copy-start | bytes 9796
  66.3 7.9 %copy-start.2 = (s32[3]{0:T(128)S(1)}, s32[3]{0:T(128)}, u32[]{:S(2)}) copy-start(s32[3]{0:T(128)} %get-tuple-element.28.groups) | copy-start | bytes 40
  73.0 12.0 %collective-permute-start.17 = (bf16[24,128,128]{2,1,0:T(8,128)(2,1)S(1)}, bf16[24,128,128]{2,1,0:T(8,128)(2,1)S(1)}, u32[]{:S(2)}, u32[]{:S(2)}) collective-permute-start(bf16[24,128,128]{2,1,0:T(8,128)(2,1)S(1)} %pad_maximum_fusion.7), channel_id=1, source_target_pairs={{0,192},{1,49},{2,194},{3,51},{4,196},{5,53},{6,198},{7,55},{8,200... | collective-permute-start | bytes 2359304 | tf_op jit(solution)/shard_map/a2/ppermute | solution.py:191
  79.7 5.4 %collective-permute-start.24 = (f32[11,128,128]{2,1,0:T(8,128)S(1)}, f32[11,128,128]{2,1,0:T(8,128)S(1)}, u32[]{:S(2)}, u32[]{:S(2)}) collective-permute-start(f32[11,128,128]{2,1,0:T(8,128)S(1)} %get-tuple-element.42), channel_id=1, source_target_pairs={{0,1},{1,0},{2,3},{3,2},{4,5},{5,4},{6,7},{7,6},{8,9},{9,8},{10,11... | collective-permute-start | bytes 2162696 | tf_op jit(solution)/shard_map/w3/ppermute | solution.py:191
  79.8 5.3 %collective-permute-start.25 = (f32[11,128,128]{2,1,0:T(8,128)S(1)}, f32[11,128,128]{2,1,0:T(8,128)S(1)}, u32[]{:S(2)}, u32[]{:S(2)}) collective-permute-start(f32[11,128,128]{2,1,0:T(8,128)S(1)} %get-tuple-element.43), channel_id=1, source_target_pairs={{0,1},{1,0},{2,3},{3,2},{4,5},{5,4},{6,7},{7,6},{8,9},{9,8},{10,11... | collective-permute-start | bytes 2162696 | tf_op jit(solution)/shard_map/w3/ppermute | solution.py:191
  80.3 4.8 %collective-permute-start.26 = (f32[10,128,128]{2,1,0:T(8,128)S(1)}, f32[10,128,128]{2,1,0:T(8,128)S(1)}, u32[]{:S(2)}, u32[]{:S(2)}) collective-permute-start(f32[10,128,128]{2,1,0:T(8,128)S(1)} %get-tuple-element.44), channel_id=1, source_target_pairs={{0,1},{1,0},{2,3},{3,2},{4,5},{5,4},{6,7},{7,6},{8,9},{9,8},{10,11... | collective-permute-start | bytes 1966088 | tf_op jit(solution)/shard_map/w3/ppermute | solution.py:191

commit v4 on v3

--- a/solution.py
+++ b/solution.py
@@ -9,7 +9,7 @@
 from jax.sharding import PartitionSpec as P
 
 SIDE = 4
-GROUP = 16
+GROUP = 32
 STAGES = 3
 PARTS = (11, 11, 10)
 

time: 88.2 us -> 88.3 us (level)
  the two profiles are of different devices: /device:TPU:96 before, /device:TPU:1 now
where the time goes in v4:
time: 88.3 us; the launch traced here: 87.7 us
  starting transfers between devices  43.8 us (50%)
  waiting for transfers between devices  20.4 us (23%)
  Pallas kernels  11.4 us (13%)
  local copies, waits for them, and re-layouts  6.83 us (8%)
  other arithmetic  4.71 us (5%)
    ppermute x27, starting transfers between devices, move(): return lax.ppermute(blocks, ('row', 'col'), pairs)  43.8 us
    ppermute x27, waiting for transfers between devices, move(): return lax.ppermute(blocks, ('row', 'col'), pairs)  20.4 us
    pallas_call x3, Pallas kernels, add_products(): pl.pallas_call(functools.partial(products_kernel, stage), out_shape=outs,...  6.92 us
    pallas_call x1, Pallas kernels, sort_lists(): pl.pallas_call(functools.partial(sort_kernel, left_shard, shard, depth, p...  4.51 us
    unnamed x32, local copies, waits for them, and re-layouts  3.68 us
    select_n x4, other arithmetic, panel(): return jnp.where((core == 1) != other, blocks[1], blocks[0])  2.29 us
  transfers between devices with their start and end apart: 27, of which 7 were waited for; matrix products, arithmetic and copies ran while one was open for 13% of the time, Pallas kernels for 10%

profile of v4, /device:TPU:1, one launch (start us, length us, event | category | flops | bytes accessed | tf_op | source)
XLA Modules:
  0.0 87.7 jit_solution(16293413004932058587)
XLA Ops:
  0.0 3.2 %collective-permute-start.1 = (bf16[2,6,128,128]{3,2,1,0:T(8,128)(2,1)}, bf16[2,6,128,128]{3,2,1,0:T(8,128)(2,1)S(1)}, u32[]{:S(2)}, u32[]{:S(2)}) collective-permute-start(bf16[2,6,128,128]{3,2,1,0:T(8,128)(2,1)} %bitcast.23), channel_id=1, source_target_pairs={{0,1},{1,0},{2,3},{3,2},{4,5},{5,4},{6,7},{7,6},{8,9},{9,8},{10,11... | collective-permute-start | bytes 1179656 | tf_op jit(solution)/shard_map/w1/ppermute | solution.py:191
  3.2 1.1 %select_bitcast_fusion.4 = (bf16[6,128,128]{2,1,0:T(8,128)(2,1)S(1)}, bf16[6,128,128]{2,1,0:T(8,128)(2,1)S(1)}) fusion(pred[]{:T(512)S(6)} %eq.5, bf16[2,1,6,128,128]{4,3,2,1,0:T(8,128)(2,1)} %param.6, pred[]{:T(512)S(6)} %ne.25), kind=kLoop, calls=%fused_computation.19 | loop fusion | flops 196608 | bytes 786434 | tf_op jit(solution)/shard_map/jit(_where)/select_n | solution.py:241
  4.3 1.2 %select_bitcast_fusion = bf16[12,128,128]{2,1,0:T(8,128)(2,1)S(1)} fusion(bf16[2,1,12,128,128]{4,3,2,1,0:T(8,128)(2,1)} %param.7, pred[]{:T(512)S(6)} %eq.5), kind=kLoop, calls=%fused_computation.15 | loop fusion | flops 196608 | bytes 1179649 | tf_op jit(solution)/shard_map/jit(_where)/select_n | solution.py:241
  5.5 1.0 %pad_maximum_fusion.3 = bf16[24,128,128]{2,1,0:T(8,128)(2,1)} fusion(bf16[6,128,128]{2,1,0:T(8,128)(2,1)S(1)} %get-tuple-element.61, bf16[6,128,128]{2,1,0:T(8,128)(2,1)S(1)} %get-tuple-element.59, bf16[6,128,128]{2,1,0:T(8,128)(2,1)S(1)} %get-tuple-element.60, bf16[6,128,128]{2,1,0:T(8,128)(2,1)S(1)} %get-tuple-element.58), kind=kLoop, calls=%fused_computation.3 | loop fusion | flops 1179648 | bytes 1572864 | tf_op jit(solution)/shard_map/concatenate | solution.py:217
  6.6 0.1 collective-permute-start.4
  6.8 0.6 collective-permute-start.6
  7.4 2.4 %collective-permute-start.5 = (bf16[24,128,128]{2,1,0:T(8,128)(2,1)S(1)}, bf16[24,128,128]{2,1,0:T(8,128)(2,1)S(1)}, u32[]{:S(2)}, u32[]{:S(2)}) collective-permute-start(bf16[24,128,128]{2,1,0:T(8,128)(2,1)S(1)} %pad_maximum_fusion.2), channel_id=1, source_target_pairs={{0,48},{1,193},{2,50},{3,195},{4,52},{5,197},{6,54},{7,199},{8,56}... | collective-permute-start | bytes 2359304 | tf_op jit(solution)/shard_map/s1/ppermute | solution.py:191
  9.8 1.2 %collective-permute-start.2 = (bf16[24,128,128]{2,1,0:T(8,128)(2,1)S(1)}, bf16[24,128,128]{2,1,0:T(8,128)(2,1)S(1)}, u32[]{:S(2)}, u32[]{:S(2)}) collective-permute-start(bf16[24,128,128]{2,1,0:T(8,128)(2,1)S(1)} %pad_maximum_fusion.2), channel_id=1, source_target_pairs={{0,64},{1,17},{2,66},{3,19},{4,68},{5,21},{6,70},{7,23},{8,72},{9,... | collective-permute-start | bytes 2359304 | tf_op jit(solution)/shard_map/t/ppermute | solution.py:191
  11.0 1.5 %collective-permute-start.3 = (bf16[24,128,128]{2,1,0:T(8,128)(2,1)S(1)}, bf16[24,128,128]{2,1,0:T(8,128)(2,1)}, u32[]{:S(2)}, u32[]{:S(2)}) collective-permute-start(bf16[24,128,128]{2,1,0:T(8,128)(2,1)S(1)} %pad_maximum_fusion.2), channel_id=1, source_target_pairs={{0,192},{1,49},{2,194},{3,51},{4,196},{5,53},{6,198},{7,55},{8,200... | collective-permute-start | bytes 2359304 | tf_op jit(solution)/shard_map/t/ppermute | solution.py:191
  12.5 5.6 %collective-permute-start.7 = (bf16[24,128,128]{2,1,0:T(8,128)(2,1)}, bf16[24,128,128]{2,1,0:T(8,128)(2,1)}, u32[]{:S(2)}, u32[]{:S(2)}) collective-permute-start(bf16[24,128,128]{2,1,0:T(8,128)(2,1)} %pad_maximum_fusion.3), channel_id=1, source_target_pairs={{0,2},{1,15},{2,4},{3,1},{4,6},{5,3},{6,8},{7,5},{8,10},{9,7},{10,... | collective-permute-start | bytes 2359304 | tf_op jit(solution)/shard_map/z1/ppermute | solution.py:191
  18.1 0.7 pad_add_fusion.1.here
  18.8 4.5 %sort_lists.1 = (s32[3,288]{1,0:T(4,128)}, s32[3]{0:T(128)}) custom-call(s32[4]{0:T(128)} %pad_add_fusion.1.here, s32[64]{0:T(128)} %constant.54.clone.right_at, s32[770]{0:T(1024)} %copy-done.4, s32[770]{0:T(1024)} %copy-done.5), custom_call_target="tpu_custom_call" | custom-call | bytes 8388608 | tf_op jit(solution)/shard_map/sort_lists/pallas_call | solution.py:93
  23.3 1.0 %slice_dynamic-update-slice_fusion.2 = bf16[96,128,128]{2,1,0:T(8,128)(2,1)S(1)} fusion(bf16[24,128,128]{2,1,0:T(8,128)(2,1)} %pad_maximum_fusion.3), kind=kLoop, calls=%fused_computation.14 | loop fusion | bytes 786432
  24.5 0.1 collective-permute-start.18
  24.6 2.7 %collective-permute-start.19 = (bf16[12,128,128]{2,1,0:T(8,128)(2,1)S(1)}, bf16[12,128,128]{2,1,0:T(8,128)(2,1)S(1)}, u32[]{:S(2)}, u32[]{:S(2)}) collective-permute-start(bf16[12,128,128]{2,1,0:T(8,128)(2,1)S(1)} %slice.133), channel_id=1, source_target_pairs={{0,48},{1,193},{2,50},{3,195},{4,52},{5,197},{6,54},{7,199},{8,56}... | collective-permute-start | bytes 1179656 | tf_op jit(solution)/shard_map/s2/ppermute | solution.py:191
  27.3 1.2 %collective-permute-done.2 = bf16[24,128,128]{2,1,0:T(8,128)(2,1)S(1)} collective-permute-done((bf16[24,128,128]{2,1,0:T(8,128)(2,1)S(1)}, bf16[24,128,128]{2,1,0:T(8,128)(2,1)S(1)}, u32[]{:S(2)}, u32[]{:S(2)}) %collective-permute-start.2) | collective-permute-done | bytes 786464 | tf_op jit(solution)/shard_map/t/ppermute | solution.py:191
  28.6 1.9 %collective-permute-start.12 = (bf16[24,128,128]{2,1,0:T(8,128)(2,1)S(1)}, bf16[24,128,128]{2,1,0:T(8,128)(2,1)S(1)}, u32[]{:S(2)}, u32[]{:S(2)}) collective-permute-start(bf16[24,128,128]{2,1,0:T(8,128)(2,1)S(1)} %collective-permute-done.4), channel_id=1, source_target_pairs={{0,64},{1,17},{2,66},{3,19},{4,68},{5,21},{6,70},{7,23},{8,72},{9,... | collective-permute-start | bytes 2359304 | tf_op jit(solution)/shard_map/a1/ppermute | solution.py:191
  30.5 1.0 %collective-permute-start.14 = (bf16[24,128,128]{2,1,0:T(8,128)(2,1)S(1)}, bf16[24,128,128]{2,1,0:T(8,128)(2,1)S(1)}, u32[]{:S(2)}, u32[]{:S(2)}) collective-permute-start(bf16[24,128,128]{2,1,0:T(8,128)(2,1)S(1)} %collective-permute-done.5), channel_id=1, source_target_pairs={{0,192},{1,49},{2,194},{3,51},{4,196},{5,53},{6,198},{7,55},{8,200... | collective-permute-start | bytes 2359304 | tf_op jit(solution)/shard_map/a1/ppermute | solution.py:191
  31.4 1.0 %slice.120 = bf16[12,128,128]{2,1,0:T(8,128)(2,1)S(1)} slice(bf16[24,128,128]{2,1,0:T(8,128)(2,1)} %collective-permute-done.3), slice={[12:24], [0:128], [0:128]} | slice | bytes 786432 | tf_op jit(solution)/shard_map/gh/slice | solution.py:276
  32.5 5.0 %collective-permute-start.8 = (bf16[24,128,128]{2,1,0:T(8,128)(2,1)}, bf16[24,128,128]{2,1,0:T(8,128)(2,1)S(1)}, u32[]{:S(2)}, u32[]{:S(2)}) collective-permute-start(bf16[24,128,128]{2,1,0:T(8,128)(2,1)} %collective-permute-done.7), channel_id=1, source_target_pairs={{0,2},{1,15},{2,4},{3,1},{4,6},{5,3},{6,8},{7,5},{8,10},{9,7},{10,... | collective-permute-start | bytes 2359304 | tf_op jit(solution)/shard_map/z2/ppermute | solution.py:191
  37.5 1.2 %fusion.2 = (bf16[12,128,128]{2,1,0:T(8,128)(2,1)S(1)}, bf16[96,128,128]{2,1,0:T(8,128)(2,1)S(1)}) fusion(bf16[24,128,128]{2,1,0:T(8,128)(2,1)} %collective-permute-done.7, bf16[96,128,128]{2,1,0:T(8,128)(2,1)S(1)} %slice_dynamic-update-slice_fusion.2), kind=kLoop, calls=%fused_computation.43 | loop fusion | bytes 1572864 | tf_op jit(solution)/shard_map/w4/slice | solution.py:262
  38.7 0.1 constant_dynamic-update-slice_fusion.18
  38.8 0.1 constant_dynamic-update-slice_fusion.17
  38.9 0.1 constant_dynamic-update-slice_fusion.16
  39.0 0.2 constant_dynamic-update-slice_fusion.15
  39.3 1.5 %collective-permute-start.20 = (bf16[24,128,128]{2,1,0:T(8,128)(2,1)S(1)}, bf16[24,128,128]{2,1,0:T(8,128)(2,1)S(1)}, u32[]{:S(2)}, u32[]{:S(2)}) collective-permute-start(bf16[24,128,128]{2,1,0:T(8,128)(2,1)S(1)} %get-tuple-element.55), channel_id=1, source_target_pairs={{0,64},{1,17},{2,66},{3,19},{4,68},{5,21},{6,70},{7,23},{8,72},{9,... | collective-permute-start | bytes 2359304 | tf_op jit(solution)/shard_map/b/ppermute | solution.py:191
  40.8 1.2 %collective-permute-start.21 = (bf16[24,128,128]{2,1,0:T(8,128)(2,1)S(1)}, bf16[24,128,128]{2,1,0:T(8,128)(2,1)S(1)}, u32[]{:S(2)}, u32[]{:S(2)}) collective-permute-start(bf16[24,128,128]{2,1,0:T(8,128)(2,1)S(1)} %get-tuple-element.55), channel_id=1, source_target_pairs={{0,192},{1,49},{2,194},{3,51},{4,196},{5,53},{6,198},{7,55},{8,200... | collective-permute-start | bytes 2359304 | tf_op jit(solution)/shard_map/b/ppermute | solution.py:191
  42.0 0.1 constant_dynamic-update-slice_fusion.14
  42.1 1.3 %constant_dynamic-update-slice_fusion.13 = bf16[192,128,128]{2,1,0:T(8,128)(2,1)S(1)} fusion(bf16[192,128,128]{2,1,0:T(8,128)(2,1)S(1)} %constant_dynamic-update-slice_fusion.14, bf16[24,128,128]{2,1,0:T(8,128)(2,1)} %collective-permute-done.3), kind=kLoop, calls=%fused_computation.33 | loop fusion | bytes 1572864
  43.4 3.3 %collective-permute-done.8 = bf16[24,128,128]{2,1,0:T(8,128)(2,1)S(1)} collective-permute-done((bf16[24,128,128]{2,1,0:T(8,128)(2,1)}, bf16[24,128,128]{2,1,0:T(8,128)(2,1)S(1)}, u32[]{:S(2)}, u32[]{:S(2)}) %collective-permute-start.8) | collective-permute-done | bytes 786464 | tf_op jit(solution)/shard_map/z2/ppermute | solution.py:191
  46.7 3.3 %collective-permute-start.9 = (bf16[24,128,128]{2,1,0:T(8,128)(2,1)S(1)}, bf16[24,128,128]{2,1,0:T(8,128)(2,1)S(1)}, u32[]{:S(2)}, u32[]{:S(2)}) collective-permute-start(bf16[24,128,128]{2,1,0:T(8,128)(2,1)S(1)} %collective-permute-done.8), channel_id=1, source_target_pairs={{0,2},{1,15},{2,4},{3,1},{4,6},{5,3},{6,8},{7,5},{8,10},{9,7},{10,... | collective-permute-start | bytes 2359304 | tf_op jit(solution)/shard_map/z3/ppermute | solution.py:191
  50.1 0.1 pad_maximum_fusion.5
  50.1 1.1 %collective-permute-start.15 = (bf16[24,128,128]{2,1,0:T(8,128)(2,1)S(1)}, bf16[24,128,128]{2,1,0:T(8,128)(2,1)S(1)}, u32[]{:S(2)}, u32[]{:S(2)}) collective-permute-start(bf16[24,128,128]{2,1,0:T(8,128)(2,1)S(1)} %pad_maximum_fusion.5), channel_id=1, source_target_pairs={{0,192},{1,49},{2,194},{3,51},{4,196},{5,53},{6,198},{7,55},{8,200... | collective-permute-start | bytes 2359304 | tf_op jit(solution)/shard_map/ga/ppermute | solution.py:191
  51.2 0.1 pad_maximum_fusion.4
  51.3 0.6 collective-permute-start.13
  51.9 0.1 constant_dynamic-update-slice_fusion.12
  52.0 0.1 constant_dynamic-update-slice_fusion.11.right
  52.1 0.1 fusion.3
  52.3 1.5 %collective-permute-start.22 = (bf16[24,128,128]{2,1,0:T(8,128)(2,1)S(1)}, bf16[24,128,128]{2,1,0:T(8,128)(2,1)S(1)}, u32[]{:S(2)}, u32[]{:S(2)}) collective-permute-start(bf16[24,128,128]{2,1,0:T(8,128)(2,1)S(1)} %pad_maximum_fusion.8), channel_id=1, source_target_pairs={{0,64},{1,17},{2,66},{3,19},{4,68},{5,21},{6,70},{7,23},{8,72},{9,... | collective-permute-start | bytes 2359304 | tf_op jit(solution)/shard_map/gh/ppermute | solution.py:191
  53.9 5.0 %collective-permute-done.9 = bf16[24,128,128]{2,1,0:T(8,128)(2,1)S(1)} collective-permute-done((bf16[24,128,128]{2,1,0:T(8,128)(2,1)S(1)}, bf16[24,128,128]{2,1,0:T(8,128)(2,1)S(1)}, u32[]{:S(2)}, u32[]{:S(2)}) %collective-permute-start.9) | collective-permute-done | bytes 786464 | tf_op jit(solution)/shard_map/z3/ppermute | solution.py:191
  58.9 0.2 fusion.4
  59.1 0.1 pad_maximum_fusion.1
  59.3 4.6 %collective-permute-start.11 = (bf16[36,128,128]{2,1,0:T(8,128)(2,1)S(1)}, bf16[36,128,128]{2,1,0:T(8,128)(2,1)S(1)}, u32[]{:S(2)}, u32[]{:S(2)}) collective-permute-start(bf16[36,128,128]{2,1,0:T(8,128)(2,1)S(1)} %pad_maximum_fusion.1), channel_id=1, source_target_pairs={{0,1},{1,0},{2,3},{3,2},{4,5},{5,4},{6,7},{7,6},{8,9},{9,8},{10,11... | collective-permute-start | bytes 3538952 | tf_op jit(solution)/shard_map/w4/ppermute | solution.py:191
  64.0 0.5 collective-permute-start.23
  64.6 0.1 constant_dynamic-update-slice_fusion.9
  64.7 1.4 %collective-permute-start.10 = (bf16[12,128,128]{2,1,0:T(8,128)(2,1)S(1)}, bf16[12,128,128]{2,1,0:T(8,128)(2,1)S(1)}, u32[]{:S(2)}, u32[]{:S(2)}) collective-permute-start(bf16[12,128,128]{2,1,0:T(8,128)(2,1)S(1)} %get-tuple-element.53), channel_id=1, source_target_pairs={{0,2},{1,15},{2,4},{3,1},{4,6},{5,3},{6,8},{7,5},{8,10},{9,7},{10,... | collective-permute-start | bytes 1179656 | tf_op jit(solution)/shard_map/z4/ppermute | solution.py:191
  66.3 0.3 collective-permute-start.16
  66.6 0.1 constant_dynamic-update-slice_fusion.8
  66.7 0.1 constant_dynamic-update-slice_fusion.7
  66.9 5.2 %collective-permute-done.22 = bf16[24,128,128]{2,1,0:T(8,128)(2,1)S(1)} collective-permute-done((bf16[24,128,128]{2,1,0:T(8,128)(2,1)S(1)}, bf16[24,128,128]{2,1,0:T(8,128)(2,1)S(1)}, u32[]{:S(2)}, u32[]{:S(2)}) %collective-permute-start.22) | collective-permute-done | bytes 786464 | tf_op jit(solution)/shard_map/gh/ppermute | solution.py:191
  72.2 0.5 collective-permute-start.17
  72.6 0.1 constant_dynamic-update-slice_fusion.6
  72.7 2.4 %collective-permute-done.23 = bf16[24,128,128]{2,1,0:T(8,128)(2,1)S(1)} collective-permute-done((bf16[24,128,128]{2,1,0:T(8,128)(2,1)S(1)}, bf16[24,128,128]{2,1,0:T(8,128)(2,1)S(1)}, u32[]{:S(2)}, u32[]{:S(2)}) %collective-permute-start.23) | collective-permute-done | bytes 786464 | tf_op jit(solution)/shard_map/gh/ppermute | solution.py:191
  75.2 0.1 constant_dynamic-update-slice_fusion.5.right
  75.4 0.2 constant_dynamic-update-slice_fusion.left
  75.6 2.3 %products.3.refs_0_ = f32[65,128,128]{2,1,0:T(8,128)S(1)} custom-call(s32[3]{0:T(128)S(1)} %copy-done.2, s32[3,288]{1,0:T(4,128)S(1)} %copy-done.1, bf16[96,128,128]{2,1,0:T(8,128)(2,1)S(1)} %constant_dynamic-update-slice_fusion.left, bf16[192,128,128]{2,1,0:T(8,128)(2,1)S(1)} %constant_dynamic-update-slice_fusion.11.right, bf16[32,128,128]{2,1,0:T(8,128)(2,1)S(1)} %bitcast.21), custom_call_target="tpu_custom_call" | custom-call | flops 1048576 | bytes 1048576 | tf_op jit(solution)/shard_map/products/pallas_call | solution.py:169
  77.9 2.2 %products.4 = (f32[32,128,128]{2,1,0:T(8,128)S(1)}, f32[11,128,128]{2,1,0:T(8,128)S(1)}, f32[11,128,128]{2,1,0:T(8,128)S(1)}, f32[10,128,128]{2,1,0:T(8,128)S(1)}) custom-call(s32[3]{0:T(128)S(1)} %copy-done.2, s32[3,288]{1,0:T(4,128)S(1)} %copy-done.1, bf16[96,128,128]{2,1,0:T(8,128)(2,1)S(1)} %constant_dynamic-update-slice_fusion.left, ...), custom_call_target="tpu_custom_call" | custom-call | flops 1048576 | bytes 1048576 | tf_op jit(solution)/shard_map/products/pallas_call | solution.py:169
  80.1 1.5 %collective-permute-start.24 = (f32[11,128,128]{2,1,0:T(8,128)S(1)}, f32[11,128,128]{2,1,0:T(8,128)S(1)}, u32[]{:S(2)}, u32[]{:S(2)}) collective-permute-start(f32[11,128,128]{2,1,0:T(8,128)S(1)} %get-tuple-element.42), channel_id=1, source_target_pairs={{0,1},{1,0},{2,3},{3,2},{4,5},{5,4},{6,7},{7,6},{8,9},{9,8},{10,11... | collective-permute-start | bytes 2162696 | tf_op jit(solution)/shard_map/w3/ppermute | solution.py:191
  81.5 0.1 collective-permute-start.25
  81.6 0.4 collective-permute-start.26
  82.0 1.6 %collective-permute-done.17 = bf16[24,128,128]{2,1,0:T(8,128)(2,1)S(1)} collective-permute-done((bf16[24,128,128]{2,1,0:T(8,128)(2,1)S(1)}, bf16[24,128,128]{2,1,0:T(8,128)(2,1)S(1)}, u32[]{:S(2)}, u32[]{:S(2)}) %collective-permute-start.17) | collective-permute-done | bytes 786464 | tf_op jit(solution)/shard_map/a2/ppermute | solution.py:191
  83.6 0.1 pad_maximum_fusion.right
  83.7 1.6 %collective-permute-done.26.refs_3_ = f32[10,128,128]{2,1,0:T(8,128)S(1)} collective-permute-done((f32[10,128,128]{2,1,0:T(8,128)S(1)}, f32[10,128,128]{2,1,0:T(8,128)S(1)}, u32[]{:S(2)}, u32[]{:S(2)}) %collective-permute-start.26) | collective-permute-done | bytes 655392 | tf_op jit(solution)/shard_map/w3/ppermute | solution.py:191
  85.3 2.4 %products.5 = bf16[32,128,128]{2,1,0:T(8,128)(2,1)} custom-call(s32[3]{0:T(128)S(1)} %copy-done.2, s32[3,288]{1,0:T(4,128)S(1)} %copy-done.1, bf16[96,128,128]{2,1,0:T(8,128)(2,1)S(1)} %constant_dynamic-update-slice_fusion.left, bf16[48,128,128]{2,1,0:T(8,128)(2,1)S(1)} %pad_maximum_fusion.right, f32[32,128,128]{2,1,0:T(8,128)S(1)} %get-tuple-element.41.refs_0_, ...), custom_call_target="tpu_custom_call" | custom-call | flops 1048576 | bytes 1048576 | tf_op jit(solution)/shard_map/products/pallas_call | solution.py:169
  (62 shorter events, 1.0 us)
Async XLA Ops:
  0.0 6.7 %copy-start.6 = (s32[1,1,2,3,128]{4,2,3,1,0:T(2,128)S(1)}, s32[1,1,2,3,128]{4,2,3,1,0:T(2,128)}, u32[]{:S(2)}) copy-start(s32[1,1,2,3,128]{4,2,3,1,0:T(2,128)} %param.9) | copy-start | bytes 9220
  0.0 6.8 %copy-start.7 = (s32[1,1,2]{2,1,0:T(1,128)S(1)}, s32[1,1,2]{2,1,0:T(1,128)}, u32[]{:S(2)}) copy-start(s32[1,1,2]{2,1,0:T(1,128)} %param.10) | copy-start | bytes 28
  0.0 5.5 %collective-permute-start.1 = (bf16[2,6,128,128]{3,2,1,0:T(8,128)(2,1)}, bf16[2,6,128,128]{3,2,1,0:T(8,128)(2,1)S(1)}, u32[]{:S(2)}, u32[]{:S(2)}) collective-permute-start(bf16[2,6,128,128]{3,2,1,0:T(8,128)(2,1)} %bitcast.23), channel_id=1, source_target_pairs={{0,1},{1,0},{2,3},{3,2},{4,5},{5,4},{6,7},{7,6},{8,9},{9,8},{10,11... | collective-permute-start | bytes 1179656 | tf_op jit(solution)/shard_map/w1/ppermute | solution.py:191
  3.2 3.3 %collective-permute-start = (bf16[2,12,128,128]{3,2,1,0:T(8,128)(2,1)}, bf16[2,12,128,128]{3,2,1,0:T(8,128)(2,1)S(1)}, u32[]{:S(2)}, u32[]{:S(2)}) collective-permute-start(bf16[2,12,128,128]{3,2,1,0:T(8,128)(2,1)} %bitcast.22), channel_id=1, source_target_pairs={{0,1},{1,0},{2,3},{3,2},{4,5},{5,4},{6,7},{7,6},{8,9},{9,8},{10,11... | collective-permute-start | bytes 2359304 | tf_op jit(solution)/shard_map/w0/ppermute | solution.py:191
  6.6 17.8 %collective-permute-start.4 = (bf16[24,128,128]{2,1,0:T(8,128)(2,1)S(1)}, bf16[24,128,128]{2,1,0:T(8,128)(2,1)S(1)}, u32[]{:S(2)}, u32[]{:S(2)}) collective-permute-start(bf16[24,128,128]{2,1,0:T(8,128)(2,1)S(1)} %pad_maximum_fusion.2), channel_id=1, source_target_pairs={{0,16},{1,65},{2,18},{3,67},{4,20},{5,69},{6,22},{7,71},{8,24},{9,... | collective-permute-start | bytes 2359304 | tf_op jit(solution)/shard_map/s1/ppermute | solution.py:191
  6.8 12.0 %copy-start.4 = (s32[770]{0:T(1024)}, s32[770]{0:T(1024)S(1)}, u32[]{:S(2)}) copy-start(s32[770]{0:T(1024)S(1)} %pad_add_fusion.own) | copy-start | bytes 9244
  6.8 5.7 %collective-permute-start.6 = (s32[770]{0:T(1024)S(1)}, s32[770]{0:T(1024)S(1)}, u32[]{:S(2)}, u32[]{:S(2)}) collective-permute-start(s32[770]{0:T(1024)S(1)} %pad_add_fusion.own), channel_id=1, source_target_pairs={{0,1},{1,0},{2,3},{3,2},{4,5},{5,4},{6,7},{7,6},{8,9},{9,8},{10,11... | collective-permute-start | bytes 9248 | tf_op jit(solution)/shard_map/w2/ppermute | solution.py:191
  7.4 17.2 %collective-permute-start.5 = (bf16[24,128,128]{2,1,0:T(8,128)(2,1)S(1)}, bf16[24,128,128]{2,1,0:T(8,128)(2,1)S(1)}, u32[]{:S(2)}, u32[]{:S(2)}) collective-permute-start(bf16[24,128,128]{2,1,0:T(8,128)(2,1)S(1)} %pad_maximum_fusion.2), channel_id=1, source_target_pairs={{0,48},{1,193},{2,50},{3,195},{4,52},{5,197},{6,54},{7,199},{8,56}... | collective-permute-start | bytes 2359304 | tf_op jit(solution)/shard_map/s1/ppermute | solution.py:191
  9.8 18.7 %collective-permute-start.2 = (bf16[24,128,128]{2,1,0:T(8,128)(2,1)S(1)}, bf16[24,128,128]{2,1,0:T(8,128)(2,1)S(1)}, u32[]{:S(2)}, u32[]{:S(2)}) collective-permute-start(bf16[24,128,128]{2,1,0:T(8,128)(2,1)S(1)} %pad_maximum_fusion.2), channel_id=1, source_target_pairs={{0,64},{1,17},{2,66},{3,19},{4,68},{5,21},{6,70},{7,23},{8,72},{9,... | collective-permute-start | bytes 2359304 | tf_op jit(solution)/shard_map/t/ppermute | solution.py:191
  11.0 17.5 %collective-permute-start.3 = (bf16[24,128,128]{2,1,0:T(8,128)(2,1)S(1)}, bf16[24,128,128]{2,1,0:T(8,128)(2,1)}, u32[]{:S(2)}, u32[]{:S(2)}) collective-permute-start(bf16[24,128,128]{2,1,0:T(8,128)(2,1)S(1)} %pad_maximum_fusion.2), channel_id=1, source_target_pairs={{0,192},{1,49},{2,194},{3,51},{4,196},{5,53},{6,198},{7,55},{8,200... | collective-permute-start | bytes 2359304 | tf_op jit(solution)/shard_map/t/ppermute | solution.py:191
  12.5 6.2 %copy-start.5 = (s32[770]{0:T(1024)}, s32[770]{0:T(1024)S(1)}, u32[]{:S(2)}) copy-start(s32[770]{0:T(1024)S(1)} %collective-permute-done.6.got) | copy-start | bytes 9244
  12.5 19.9 %collective-permute-start.7 = (bf16[24,128,128]{2,1,0:T(8,128)(2,1)}, bf16[24,128,128]{2,1,0:T(8,128)(2,1)}, u32[]{:S(2)}, u32[]{:S(2)}) collective-permute-start(bf16[24,128,128]{2,1,0:T(8,128)(2,1)} %pad_maximum_fusion.3), channel_id=1, source_target_pairs={{0,2},{1,15},{2,4},{3,1},{4,6},{5,3},{6,8},{7,5},{8,10},{9,7},{10,... | collective-permute-start | bytes 2359304 | tf_op jit(solution)/shard_map/z1/ppermute | solution.py:191
  24.5 14.4 %collective-permute-start.18 = (bf16[12,128,128]{2,1,0:T(8,128)(2,1)S(1)}, bf16[12,128,128]{2,1,0:T(8,128)(2,1)S(1)}, u32[]{:S(2)}, u32[]{:S(2)}) collective-permute-start(bf16[12,128,128]{2,1,0:T(8,128)(2,1)S(1)} %get-tuple-element.45), channel_id=1, source_target_pairs={{0,16},{1,65},{2,18},{3,67},{4,20},{5,69},{6,22},{7,71},{8,24},{9,... | collective-permute-start | bytes 1179656 | tf_op jit(solution)/shard_map/s2/ppermute | solution.py:191
  24.6 14.4 %collective-permute-start.19 = (bf16[12,128,128]{2,1,0:T(8,128)(2,1)S(1)}, bf16[12,128,128]{2,1,0:T(8,128)(2,1)S(1)}, u32[]{:S(2)}, u32[]{:S(2)}) collective-permute-start(bf16[12,128,128]{2,1,0:T(8,128)(2,1)S(1)} %slice.133), channel_id=1, source_target_pairs={{0,48},{1,193},{2,50},{3,195},{4,52},{5,197},{6,54},{7,199},{8,56}... | collective-permute-start | bytes 1179656 | tf_op jit(solution)/shard_map/s2/ppermute | solution.py:191
  28.6 13.6 %copy-start.3 = (bf16[24,128,128]{2,1,0:T(8,128)(2,1)}, bf16[24,128,128]{2,1,0:T(8,128)(2,1)S(1)}, u32[]{:S(2)}) copy-start(bf16[24,128,128]{2,1,0:T(8,128)(2,1)S(1)} %collective-permute-done.2) | copy-start | bytes 2359300
  28.6 22.7 %collective-permute-start.12 = (bf16[24,128,128]{2,1,0:T(8,128)(2,1)S(1)}, bf16[24,128,128]{2,1,0:T(8,128)(2,1)S(1)}, u32[]{:S(2)}, u32[]{:S(2)}) collective-permute-start(bf16[24,128,128]{2,1,0:T(8,128)(2,1)S(1)} %collective-permute-done.4), channel_id=1, source_target_pairs={{0,64},{1,17},{2,66},{3,19},{4,68},{5,21},{6,70},{7,23},{8,72},{9,... | collective-permute-start | bytes 2359304 | tf_op jit(solution)/shard_map/a1/ppermute | solution.py:191
  30.5 19.6 %collective-permute-start.14 = (bf16[24,128,128]{2,1,0:T(8,128)(2,1)S(1)}, bf16[24,128,128]{2,1,0:T(8,128)(2,1)S(1)}, u32[]{:S(2)}, u32[]{:S(2)}) collective-permute-start(bf16[24,128,128]{2,1,0:T(8,128)(2,1)S(1)} %collective-permute-done.5), channel_id=1, source_target_pairs={{0,192},{1,49},{2,194},{3,51},{4,196},{5,53},{6,198},{7,55},{8,200... | collective-permute-start | bytes 2359304 | tf_op jit(solution)/shard_map/a1/ppermute | solution.py:191
  32.5 14.2 %collective-permute-start.8 = (bf16[24,128,128]{2,1,0:T(8,128)(2,1)}, bf16[24,128,128]{2,1,0:T(8,128)(2,1)S(1)}, u32[]{:S(2)}, u32[]{:S(2)}) collective-permute-start(bf16[24,128,128]{2,1,0:T(8,128)(2,1)} %collective-permute-done.7), channel_id=1, source_target_pairs={{0,2},{1,15},{2,4},{3,1},{4,6},{5,3},{6,8},{7,5},{8,10},{9,7},{10,... | collective-permute-start | bytes 2359304 | tf_op jit(solution)/shard_map/z2/ppermute | solution.py:191
  39.3 12.9 %collective-permute-start.20 = (bf16[24,128,128]{2,1,0:T(8,128)(2,1)S(1)}, bf16[24,128,128]{2,1,0:T(8,128)(2,1)S(1)}, u32[]{:S(2)}, u32[]{:S(2)}) collective-permute-start(bf16[24,128,128]{2,1,0:T(8,128)(2,1)S(1)} %get-tuple-element.55), channel_id=1, source_target_pairs={{0,64},{1,17},{2,66},{3,19},{4,68},{5,21},{6,70},{7,23},{8,72},{9,... | collective-permute-start | bytes 2359304 | tf_op jit(solution)/shard_map/b/ppermute | solution.py:191
  40.8 13.1 %collective-permute-start.21 = (bf16[24,128,128]{2,1,0:T(8,128)(2,1)S(1)}, bf16[24,128,128]{2,1,0:T(8,128)(2,1)S(1)}, u32[]{:S(2)}, u32[]{:S(2)}) collective-permute-start(bf16[24,128,128]{2,1,0:T(8,128)(2,1)S(1)} %get-tuple-element.55), channel_id=1, source_target_pairs={{0,192},{1,49},{2,194},{3,51},{4,196},{5,53},{6,198},{7,55},{8,200... | collective-permute-start | bytes 2359304 | tf_op jit(solution)/shard_map/b/ppermute | solution.py:191
  46.7 12.2 %collective-permute-start.9 = (bf16[24,128,128]{2,1,0:T(8,128)(2,1)S(1)}, bf16[24,128,128]{2,1,0:T(8,128)(2,1)S(1)}, u32[]{:S(2)}, u32[]{:S(2)}) collective-permute-start(bf16[24,128,128]{2,1,0:T(8,128)(2,1)S(1)} %collective-permute-done.8), channel_id=1, source_target_pairs={{0,2},{1,15},{2,4},{3,1},{4,6},{5,3},{6,8},{7,5},{8,10},{9,7},{10,... | collective-permute-start | bytes 2359304 | tf_op jit(solution)/shard_map/z3/ppermute | solution.py:191
  50.0 2.2 %slice-start = ((bf16[24,128,128]{2,1,0:T(8,128)(2,1)}), bf16[12,128,128]{2,1,0:T(8,128)(2,1)S(1)}, s32[]{:S(2)}) async-start(bf16[24,128,128]{2,1,0:T(8,128)(2,1)} %copy-done.3), calls=%async_computation | async-start | bytes 786432 | tf_op jit(solution)/shard_map/gh/slice | solution.py:276
  50.1 14.5 %collective-permute-start.15 = (bf16[24,128,128]{2,1,0:T(8,128)(2,1)S(1)}, bf16[24,128,128]{2,1,0:T(8,128)(2,1)S(1)}, u32[]{:S(2)}, u32[]{:S(2)}) collective-permute-start(bf16[24,128,128]{2,1,0:T(8,128)(2,1)S(1)} %pad_maximum_fusion.5), channel_id=1, source_target_pairs={{0,192},{1,49},{2,194},{3,51},{4,196},{5,53},{6,198},{7,55},{8,200... | collective-permute-start | bytes 2359304 | tf_op jit(solution)/shard_map/ga/ppermute | solution.py:191
  51.3 14.8 %collective-permute-start.13 = (bf16[24,128,128]{2,1,0:T(8,128)(2,1)S(1)}, bf16[24,128,128]{2,1,0:T(8,128)(2,1)S(1)}, u32[]{:S(2)}, u32[]{:S(2)}) collective-permute-start(bf16[24,128,128]{2,1,0:T(8,128)(2,1)S(1)} %pad_maximum_fusion.4), channel_id=1, source_target_pairs={{0,64},{1,17},{2,66},{3,19},{4,68},{5,21},{6,70},{7,23},{8,72},{9,... | collective-permute-start | bytes 2359304 | tf_op jit(solution)/shard_map/ga/ppermute | solution.py:191
  52.3 19.8 %collective-permute-start.22 = (bf16[24,128,128]{2,1,0:T(8,128)(2,1)S(1)}, bf16[24,128,128]{2,1,0:T(8,128)(2,1)S(1)}, u32[]{:S(2)}, u32[]{:S(2)}) collective-permute-start(bf16[24,128,128]{2,1,0:T(8,128)(2,1)S(1)} %pad_maximum_fusion.8), channel_id=1, source_target_pairs={{0,64},{1,17},{2,66},{3,19},{4,68},{5,21},{6,70},{7,23},{8,72},{9,... | collective-permute-start | bytes 2359304 | tf_op jit(solution)/shard_map/gh/ppermute | solution.py:191
  59.3 16.1 %collective-permute-start.11 = (bf16[36,128,128]{2,1,0:T(8,128)(2,1)S(1)}, bf16[36,128,128]{2,1,0:T(8,128)(2,1)S(1)}, u32[]{:S(2)}, u32[]{:S(2)}) collective-permute-start(bf16[36,128,128]{2,1,0:T(8,128)(2,1)S(1)} %pad_maximum_fusion.1), channel_id=1, source_target_pairs={{0,1},{1,0},{2,3},{3,2},{4,5},{5,4},{6,7},{7,6},{8,9},{9,8},{10,11... | collective-permute-start | bytes 3538952 | tf_op jit(solution)/shard_map/w4/ppermute | solution.py:191
  64.0 11.2 %collective-permute-start.23 = (bf16[24,128,128]{2,1,0:T(8,128)(2,1)S(1)}, bf16[24,128,128]{2,1,0:T(8,128)(2,1)S(1)}, u32[]{:S(2)}, u32[]{:S(2)}) collective-permute-start(bf16[24,128,128]{2,1,0:T(8,128)(2,1)S(1)} %pad_maximum_fusion.9), channel_id=1, source_target_pairs={{0,192},{1,49},{2,194},{3,51},{4,196},{5,53},{6,198},{7,55},{8,200... | collective-permute-start | bytes 2359304 | tf_op jit(solution)/shard_map/gh/ppermute | solution.py:191
  64.7 10.6 %collective-permute-start.10 = (bf16[12,128,128]{2,1,0:T(8,128)(2,1)S(1)}, bf16[12,128,128]{2,1,0:T(8,128)(2,1)S(1)}, u32[]{:S(2)}, u32[]{:S(2)}) collective-permute-start(bf16[12,128,128]{2,1,0:T(8,128)(2,1)S(1)} %get-tuple-element.53), channel_id=1, source_target_pairs={{0,2},{1,15},{2,4},{3,1},{4,6},{5,3},{6,8},{7,5},{8,10},{9,7},{10,... | collective-permute-start | bytes 1179656 | tf_op jit(solution)/shard_map/z4/ppermute | solution.py:191
  66.3 15.8 %collective-permute-start.16 = (bf16[24,128,128]{2,1,0:T(8,128)(2,1)S(1)}, bf16[24,128,128]{2,1,0:T(8,128)(2,1)S(1)}, u32[]{:S(2)}, u32[]{:S(2)}) collective-permute-start(bf16[24,128,128]{2,1,0:T(8,128)(2,1)S(1)} %pad_maximum_fusion.6), channel_id=1, source_target_pairs={{0,64},{1,17},{2,66},{3,19},{4,68},{5,21},{6,70},{7,23},{8,72},{9,... | collective-permute-start | bytes 2359304 | tf_op jit(solution)/shard_map/a2/ppermute | solution.py:191
  66.7 8.8 %copy-start = (bf16[1,32,128,128]{3,2,1,0:T(8,128)(2,1)S(1)}, bf16[1,32,128,128]{3,2,1,0:T(8,128)(2,1)}, u32[]{:S(2)}) copy-start(bf16[1,32,128,128]{3,2,1,0:T(8,128)(2,1)} %param.8) | copy-start | bytes 3145732
  66.7 8.8 %copy-start.1 = (s32[3,288]{1,0:T(4,128)S(1)}, s32[3,288]{1,0:T(4,128)}, u32[]{:S(2)}) copy-start(s32[3,288]{1,0:T(4,128)} %get-tuple-element.29.entries) | copy-start | bytes 10372
  66.7 8.8 %copy-start.2 = (s32[3]{0:T(128)S(1)}, s32[3]{0:T(128)}, u32[]{:S(2)}) copy-start(s32[3]{0:T(128)} %get-tuple-element.28.groups) | copy-start | bytes 40
  72.2 11.4 %collective-permute-start.17 = (bf16[24,128,128]{2,1,0:T(8,128)(2,1)S(1)}, bf16[24,128,128]{2,1,0:T(8,128)(2,1)S(1)}, u32[]{:S(2)}, u32[]{:S(2)}) collective-permute-start(bf16[24,128,128]{2,1,0:T(8,128)(2,1)S(1)} %pad_maximum_fusion.7), channel_id=1, source_target_pairs={{0,192},{1,49},{2,194},{3,51},{4,196},{5,53},{6,198},{7,55},{8,200... | collective-permute-start | bytes 2359304 | tf_op jit(solution)/shard_map/a2/ppermute | solution.py:191
  80.1 5.2 %collective-permute-start.24 = (f32[11,128,128]{2,1,0:T(8,128)S(1)}, f32[11,128,128]{2,1,0:T(8,128)S(1)}, u32[]{:S(2)}, u32[]{:S(2)}) collective-permute-start(f32[11,128,128]{2,1,0:T(8,128)S(1)} %get-tuple-element.42), channel_id=1, source_target_pairs={{0,1},{1,0},{2,3},{3,2},{4,5},{5,4},{6,7},{7,6},{8,9},{9,8},{10,11... | collective-permute-start | bytes 2162696 | tf_op jit(solution)/shard_map/w3/ppermute | solution.py:191
  81.5 3.8 %collective-permute-start.25 = (f32[11,128,128]{2,1,0:T(8,128)S(1)}, f32[11,128,128]{2,1,0:T(8,128)S(1)}, u32[]{:S(2)}, u32[]{:S(2)}) collective-permute-start(f32[11,128,128]{2,1,0:T(8,128)S(1)} %get-tuple-element.43), channel_id=1, source_target_pairs={{0,1},{1,0},{2,3},{3,2},{4,5},{5,4},{6,7},{7,6},{8,9},{9,8},{10,11... | collective-permute-start | bytes 2162696 | tf_op jit(solution)/shard_map/w3/ppermute | solution.py:191
  81.6 3.7 %collective-permute-start.26 = (f32[10,128,128]{2,1,0:T(8,128)S(1)}, f32[10,128,128]{2,1,0:T(8,128)S(1)}, u32[]{:S(2)}, u32[]{:S(2)}) collective-permute-start(f32[10,128,128]{2,1,0:T(8,128)S(1)} %get-tuple-element.44), channel_id=1, source_target_pairs={{0,1},{1,0},{2,3},{3,2},{4,5},{5,4},{6,7},{7,6},{8,9},{9,8},{10,11... | collective-permute-start | bytes 1966088 | tf_op jit(solution)/shard_map/w3/ppermute | solution.py:191
